TPU v7x, 512 devices: a whole 4x4x16 slice. The times are simulated.
512 devices in a mesh: dp: 32 (over z, core), expert: 16 (over x, y).
Axes of the slice: x: 4, y: 4, z: 16, core: 2. Of those that a mesh axis runs over, the one named last changes fastest.
Arguments:
- acts: bfloat16 [16384, 16, 2048], P('dp', 'expert'), may hold values from -6 to 6
- grads: bfloat16 [16384, 16, 384], P('dp', 'expert'), may hold values from -0.046875 to 0.046875
- tile_expert: int32 [64, 16, 1], P('dp', 'expert'), may hold values from 0 to 1
- momentum: float32 [2048, 32, 384], P('dp', 'expert'), may hold values from -48 to 48
- packing: int32 [32, 1], replicated, may hold values from 0 to 15; in each aligned block of 32 rows (0 to 31, 32 to 63, ...) at most 4 rows name the same one
Outputs:
- new_momentum: float32 [2048, 32, 384], P('dp', 'expert')
- stacked_update: bfloat16 [2048, 64, 384], P('dp', 'expert')
Inputs may be any that keep to these rules, and one draw needn't show every extreme that they name: `tile_expert`: local expert index within the tile's group. `packing`: at most 4 experts share an owner, and some owner holds exactly 4.
All inputs are finite; a program needn't handle non-finite values.
Results may differ from a plain program's by a relative error of at most 0.04.
Values may be sent and summed in bfloat16 or wider, within the bound.
No kernel may reach another device: no remote copies, remote signals or barrier semaphores. Data moves between devices by JAX's collectives and lax.ppermute only.
A program may use at most 64 MiB of HBM per device.

v0:
```python
import math

import jax
import jax.numpy as jnp
from jax import lax
from jax.sharding import PartitionSpec as P

D = 2048
TILE = 256
ITERS = 3
MOST = 4


COEF_A = 3.4445
COEF_B = -4.775
COEF_C = 2.0315
BETA = 0.95
EPSILON = 1e-07


def gram_matrix(current):
    partial_value = jnp.einsum("dsf,dsg->sfg", current, current, preferred_element_type=jnp.float32)
    return lax.psum(partial_value.astype(jnp.bfloat16), "dp").astype(jnp.float32)


def orthogonalize(blocks):
    gram0 = gram_matrix(blocks)
    inv_norm = 1.0 / (jnp.sqrt(jnp.trace(gram0, axis1=1, axis2=2)) + EPSILON)
    current = (blocks.astype(jnp.float32) * inv_norm[None, :, None]).astype(jnp.bfloat16)
    weights_a = (gram0 * (inv_norm * inv_norm)[:, None, None]).astype(jnp.bfloat16)
    result = current
    for sweep in range(ITERS):
        if sweep > 0:
            weights_a = gram_matrix(current).astype(jnp.bfloat16)
        times_a = jnp.einsum("dsf,sfg->dsg", current, weights_a, preferred_element_type=jnp.float32)
        times_aa = jnp.einsum(
            "dsf,sfg->dsg",
            times_a.astype(jnp.bfloat16),
            weights_a,
            preferred_element_type=jnp.float32,
        )
        combined = COEF_A * current.astype(jnp.float32) + COEF_B * times_a + COEF_C * times_aa
        if sweep < ITERS - 1:
            current = combined.astype(jnp.bfloat16)
        else:
            result = (combined * math.sqrt(D)).astype(jnp.bfloat16)
    return result


def body(acts, grads, tile_expert, momentum, packing):
    exp_count = momentum.shape[1]
    hidden_width = momentum.shape[2]
    local_rows = momentum.shape[0]
    tile_count = acts.shape[0] // TILE
    flat_acts = acts[:, 0, :]
    flat_grads = grads[:, 0, :]
    expert_ids = tile_expert[:, 0, 0]
    onehot = (expert_ids[:, None] == jnp.arange(exp_count, dtype=jnp.int32)[None, :]).astype(
        jnp.float32
    )
    summed = jnp.zeros((lax.axis_size("dp") * local_rows, exp_count, hidden_width), jnp.float32)
    for tile_pos in range(tile_count):
        lower = tile_pos * TILE
        contrib = lax.dot_general(
            flat_acts[lower : lower + TILE],
            flat_grads[lower : lower + TILE],
            (((0,), (0,)), ((), ())),
            preferred_element_type=jnp.float32,
        )
        summed = summed + contrib[:, None, :] * onehot[tile_pos][None, :, None]
    grad_local = lax.psum_scatter(
        summed.astype(jnp.bfloat16), "dp", scatter_dimension=0, tiled=True
    ).astype(jnp.float32)
    new_momentum = BETA * momentum + grad_local
    ns_input = (grad_local + BETA * new_momentum).astype(jnp.bfloat16)
    owner_ids = packing[:, 0]
    all_experts = owner_ids.shape[0]
    positions = jnp.arange(all_experts, dtype=jnp.int32)
    shared = (owner_ids[:, None] == owner_ids[None, :]) & (positions[None, :] < positions[:, None])
    slot_rank = jnp.sum(shared.astype(jnp.int32), axis=1)
    target = owner_ids * MOST + slot_rank
    my_owner = lax.axis_index("expert")
    wanted = my_owner * MOST + jnp.arange(MOST, dtype=jnp.int32)
    selector = (target[None, :] == wanted[:, None]).astype(jnp.bfloat16)
    picked = jnp.einsum(
        "sn,dnf->dsf",
        selector,
        lax.all_gather(ns_input, "expert", axis=1, tiled=True),
        preferred_element_type=jnp.float32,
    )
    stacked = orthogonalize(picked.astype(jnp.bfloat16))
    return (new_momentum, stacked)


def solution(mesh):
    in_specs = (
        P("dp", "expert", None),
        P("dp", "expert", None),
        P("dp", "expert", None),
        P("dp", "expert", None),
        P(),
    )
    out_specs = (P("dp", "expert", None), P("dp", "expert", None))
    return jax.shard_map(body, mesh=mesh, in_specs=in_specs, out_specs=out_specs, check_vma=False)
```

profile of v0, /device:TPU:1, one launch (start us, length us, event | category | flops | bytes accessed | tf_op | source)
XLA Modules:
  0.0 948.4 jit_solution(13506718911482853390)
XLA Ops:
  7.2 0.0 all-reduce.12.cloned.1.call-start
  7.2 2.1 fusion.14
  9.4 0.7 fusion.16
  10.2 0.1 compare_convert_fusion
  10.2 5.0 add_convert_fusion
  15.2 0.0 all-reduce.12.cloned.1.call-update
  15.2 0.0 all-gather.2.cloned.1.call-start
  15.3 1.3 dynamic-slice
  17.2 220.8 %all-reduce.12.cloned.1.call-done = bf16[2048,2,384]{2,1,0:T(2,128)(2,1)} async-done(((bf16[2048,2,384]{2,1,0:T(2,128)(2,1)}), bf16[2048,2,384]{2,1,0:T(2,128)(2,1)}) %all-reduce.12.cloned.1.call-update) | async-done | bytes 3145744
  238.0 1.8 fusion.23
  239.8 0.7 copy.56
  240.5 0.0 all-gather.2.cloned.1.call-update
  240.5 0.0 all-reduce.6.cloned.1.call-start
  240.6 0.2 convert_reduce_fusion
  240.7 59.5 %all-gather.2.cloned.1.call-done = bf16[64,32,384]{2,0,1:T(8,128)(2,1)} async-done(((bf16[64,2,384]{2,0,1:T(8,128)(2,1)}), bf16[64,32,384]{2,0,1:T(8,128)(2,1)}) %all-gather.2.cloned.1.call-update) | async-done | bytes 1572880 | tf_op jit(solution)/shard_map/all_gather | solution.py:88
  300.2 2.4 fusion.2
  302.6 1.6 convolution_convert_fusion.2
  304.2 0.0 all-reduce.8.cloned.1.call-start
  304.3 208.9 %all-reduce.6.cloned.1.call-done = bf16[4,384,384]{2,1,0:T(8,128)(2,1)} async-done(((bf16[4,384,384]{2,1,0:T(8,128)(2,1)}), bf16[4,384,384]{2,1,0:T(8,128)(2,1)}) %all-reduce.6.cloned.1.call-update) | async-done | bytes 1179664 | tf_op jit(solution)/shard_map/psum | solution.py:23
  513.2 1.9 fusion
  515.1 1.7 fusion.20
  516.8 0.4 fusion.12
  517.2 1.6 convolution_convert_fusion.1
  518.8 0.0 all-reduce.10.cloned.1.call-start
  518.8 208.3 %all-reduce.8.cloned.1.call-done = bf16[4,384,384]{2,1,0:T(8,128)(2,1)} async-done(((bf16[4,384,384]{2,1,0:T(8,128)(2,1)}), bf16[4,384,384]{2,1,0:T(8,128)(2,1)}) %all-reduce.8.cloned.1.call-update) | async-done | bytes 1179664 | tf_op jit(solution)/shard_map/psum | solution.py:23
  727.1 1.7 fusion.43
  728.8 0.3 fusion.11
  729.1 1.6 convolution_convert_fusion
  730.7 208.3 %all-reduce.10.cloned.1.call-done = bf16[4,384,384]{2,1,0:T(8,128)(2,1)} async-done(((bf16[4,384,384]{2,1,0:T(8,128)(2,1)}), bf16[4,384,384]{2,1,0:T(8,128)(2,1)}) %all-reduce.10.cloned.1.call-update) | async-done | bytes 1179664 | tf_op jit(solution)/shard_map/psum | solution.py:23
  939.1 1.7 fusion.44
  940.8 0.3 fusion.13
  941.1 0.8 copy.59
  (24 shorter events, 0.2 us)
Async XLA Ops:
  7.2 2.2 copy-start.3
  7.2 2.2 copy-start.4
  7.2 230.8 %all-reduce.12.cloned.1.call-start = ((), (), s32[]{:S(2)}) async-start(), calls=%async_computation.4 | async-start | bytes 6291456
  9.4 0.8 copy-start.6
  15.2 222.8 %copy-start.5 = (f32[64,2,384]{2,1,0:T(2,128)S(1)}, f32[64,2,384]{2,1,0:T(2,128)}, u32[]{:S(2)}) copy-start(f32[64,2,384]{2,1,0:T(2,128)} %param.8) | copy-start | bytes 589828
  15.2 225.3 %copy-start.7 = (s32[32,1]{0,1:T(1,128)S(1)}, s32[32,1]{0,1:T(1,128)}, u32[]{:S(2)}) copy-start(s32[32,1]{0,1:T(1,128)} %param.9) | copy-start | bytes 388
  15.2 285.0 %all-gather.2.cloned.1.call-start = ((), (), s32[]{:S(2)}) async-start(), calls=%async_computation | async-start | bytes 1671168 | tf_op jit(solution)/shard_map/all_gather | solution.py:88
  240.5 272.7 %all-reduce.6.cloned.1.call-start = ((), (), s32[]{:S(2)}) async-start(), calls=%async_computation.1 | async-start | bytes 2359296 | tf_op jit(solution)/shard_map/psum | solution.py:23
  304.2 423.0 %all-reduce.8.cloned.1.call-start = ((), (), s32[]{:S(2)}) async-start(), calls=%async_computation.2 | async-start | bytes 2359296 | tf_op jit(solution)/shard_map/psum | solution.py:23
  513.2 3.6 copy-start
  518.8 420.3 %all-reduce.10.cloned.1.call-start = ((), (), s32[]{:S(2)}) async-start(), calls=%async_computation.3 | async-start | bytes 2359296 | tf_op jit(solution)/shard_map/psum | solution.py:23
  727.1 1.7 copy-start.1
  939.1 1.7 copy-start.2
Sparse Core Ops, SparseCore 0:
  15.3 222.6 all-reduce.11
  242.1 58.0 all-gather.1
  304.3 208.8 all-reduce.5
  518.9 208.1 all-reduce.7
  730.8 208.1 all-reduce.9
where the time goes:
time: 949 us; the launch traced here: 948 us
  waiting for transfers between devices  906 us (95%)
  matrix products  16 us (2%)
  between operations  14.6 us (2%)
    psum x3, waiting for transfers between devices, gram_matrix(): lax.psum(partial_value.astype(jnp.bfloat16), 'dp').astype(jnp.float32)  626 us
    unnamed x6, waiting for transfers between devices  221 us
    all_gather x1, waiting for transfers between devices, body(): lax.all_gather(ns_input, 'expert', axis=1, tiled=True)  59.5 us
  transfers between devices with their start and end apart: 5, of which 5 were waited for; matrix products, arithmetic and copies ran while one was open for 0% of the time, Pallas kernels for 0%

commit v1 on v0

v1 whole, which is shorter than its diff:
```python
import math

import jax
import jax.numpy as jnp
from jax import lax
from jax.experimental import pallas as pl
from jax.experimental.pallas import tpu as pltpu
from jax.sharding import PartitionSpec as P

D = 2048
FF = 384
TILE = 256
ITERS = 3
MOST = 4
CORES = 2
NEAR = 4
LANE = 128

COEF_A = 3.4445
COEF_B = -4.775
COEF_C = 2.0315
BETA = 0.95
EPSILON = 1e-07
BLOCKS = ((0, 0), (0, 1), (0, 2), (1, 1), (1, 2), (2, 2))


def split(x):
    high = x.astype(jnp.bfloat16)
    return high, (x - high.astype(jnp.float32)).astype(jnp.bfloat16)


def dot(x, y):
    return jnp.dot(x, y, preferred_element_type=jnp.float32)


def dot3(x, y):
    (xh, xl), (yh, yl) = x, y
    return dot(xh, yh) + (dot(xh, yl) + dot(xl, yh))


def newton_schulz_kernel(gram_ref, x_ref, out_ref):
    blocks = {}
    for at, (i, j) in enumerate(BLOCKS):
        block = gram_ref[at * LANE : (at + 1) * LANE, :]
        blocks[i, j] = block
        if i != j:
            blocks[j, i] = block.T
    gram = jnp.concatenate(
        [jnp.concatenate([blocks[i, j] for j in range(3)], axis=1) for i in range(3)], axis=0
    )
    rows = lax.broadcasted_iota(jnp.int32, (FF, FF), 0)
    cols = lax.broadcasted_iota(jnp.int32, (FF, FF), 1)
    eye = (rows == cols).astype(jnp.float32)
    trace = jnp.sum(jnp.sum(gram * eye, axis=1, keepdims=True), axis=0, keepdims=True)
    inv_norm = 1.0 / (jnp.sqrt(trace) + EPSILON)
    weights = gram * (inv_norm * inv_norm)
    total = None
    for sweep in range(ITERS):
        parts = split(weights)
        poly = COEF_A * eye + COEF_B * weights + COEF_C * dot3(parts, parts)
        poly_parts = split(poly)
        total = poly if total is None else dot3(split(total), poly_parts)
        if sweep < ITERS - 1:
            weights = dot3(split(dot3(parts, poly_parts)), poly_parts)
    high, low = split(total * (inv_norm * math.sqrt(D)))
    x = x_ref[...]
    out_ref[...] = (dot(x, high) + dot(x, low)).astype(jnp.bfloat16)


def body(acts, grads, tile_expert, momentum, packing):
    n_dp = lax.axis_size("dp")
    n_z = n_dp // CORES
    far = n_z // NEAR
    local_rows = momentum.shape[0]
    pair_rows = CORES * local_rows
    core = lax.rem(lax.axis_index("dp"), CORES)
    swap = [(i, i ^ 1) for i in range(n_dp)]
    near_groups = [
        [(b * NEAR + j) * CORES + c for j in range(NEAR)] for b in range(far) for c in range(CORES)
    ]
    far_groups = [
        [(j * NEAR + b) * CORES + c for j in range(far)] for b in range(NEAR) for c in range(CORES)
    ]
    z_groups = [[j * CORES + c for j in range(n_z)] for c in range(CORES)]

    flat_acts = acts[:, 0, :]
    flat_grads = grads[:, 0, :]
    row_expert = jnp.repeat(tile_expert[:, 0, 0], TILE)[:, None]

    def partial_of(expert):
        masked = jnp.where(row_expert == expert, flat_grads, jnp.zeros_like(flat_grads))
        return lax.dot_general(
            flat_acts, masked, (((0,), (0,)), ((), ())), preferred_element_type=jnp.float32
        ).astype(jnp.bfloat16)

    other = lax.ppermute(partial_of(1 - core), "dp", swap)
    chip = (partial_of(core).astype(jnp.float32) + other.astype(jnp.float32)).astype(jnp.bfloat16)
    chip = chip.reshape(far, NEAR, pair_rows, FF).transpose(1, 0, 2, 3)
    near = lax.all_to_all(chip, "dp", 0, 0, axis_index_groups=near_groups)
    near = jnp.sum(near.astype(jnp.float32), axis=0).astype(jnp.bfloat16)
    grad = lax.all_to_all(near, "dp", 0, 0, axis_index_groups=far_groups)
    grad = jnp.sum(grad.astype(jnp.float32), axis=0)

    def by_row(mine, theirs):
        low = jnp.where(core == 0, mine, theirs)
        high = jnp.where(core == 0, theirs, mine)
        return jnp.concatenate([low, high], axis=0)

    def swap_rows(value):
        halves = value.reshape(CORES, local_rows, FF)
        mine = lax.dynamic_index_in_dim(halves, core, 0, keepdims=False)
        given = lax.dynamic_index_in_dim(halves, 1 - core, 0, keepdims=False)
        theirs = lax.ppermute(given, "dp", swap)
        return jnp.where(core == 0, mine, theirs), jnp.where(core == 0, theirs, mine)

    kept = lax.dynamic_index_in_dim(momentum, core, 1, keepdims=False)
    lent = lax.dynamic_index_in_dim(momentum, 1 - core, 1, keepdims=False)
    pair_momentum = by_row(kept, lax.ppermute(lent, "dp", swap))
    pair_new = BETA * pair_momentum + grad
    ns_input = (grad + BETA * pair_new).astype(jnp.bfloat16)
    new_momentum = jnp.stack(swap_rows(pair_new), axis=1)

    gram = lax.dot_general(
        ns_input, ns_input, (((0,), (0,)), ((), ())), preferred_element_type=jnp.float32
    ).astype(jnp.bfloat16)
    packed = jnp.concatenate(
        [gram[i * LANE : (i + 1) * LANE, j * LANE : (j + 1) * LANE] for i, j in BLOCKS], axis=0
    )
    packed = packed.reshape(n_z, -1, LANE)
    piece = lax.all_to_all(packed, "dp", 0, 0, axis_index_groups=z_groups)
    piece = jnp.sum(piece.astype(jnp.float32), axis=0)
    whole = lax.all_to_all(
        jnp.broadcast_to(piece[None], packed.shape), "dp", 0, 0, axis_index_groups=z_groups
    ).reshape(-1, LANE)

    update = pl.pallas_call(
        newton_schulz_kernel,
        out_shape=jax.ShapeDtypeStruct((pair_rows, FF), jnp.bfloat16),
        in_specs=[pl.BlockSpec(memory_space=pltpu.VMEM)] * 2,
        out_specs=pl.BlockSpec(memory_space=pltpu.VMEM),
        compiler_params=pltpu.CompilerParams(vmem_limit_bytes=32 * 1024 * 1024),
    )(whole, ns_input)
    update = jnp.stack(swap_rows(update), axis=0)

    owner_ids = packing[:, 0]
    n_owner = lax.axis_size("expert")
    all_experts = owner_ids.shape[0]
    exp_count = momentum.shape[1]
    positions = jnp.arange(all_experts, dtype=jnp.int32)
    shared = (owner_ids[:, None] == owner_ids[None, :]) & (positions[None, :] < positions[:, None])
    target = owner_ids * MOST + jnp.sum(shared.astype(jnp.int32), axis=1)
    group = lax.axis_index("expert")
    my_owners = lax.dynamic_slice_in_dim(owner_ids, group * exp_count, exp_count, 0)
    goes = jnp.arange(n_owner, dtype=jnp.int32)[:, None] == my_owners[None, :]
    sent = jnp.where(goes[:, :, None, None], update[None], jnp.zeros_like(update)[None])
    got = lax.all_to_all(sent, "expert", 0, 0).reshape(all_experts, local_rows, FF)
    wanted = group * MOST + jnp.arange(MOST, dtype=jnp.int32)
    hits = target[None, :] == wanted[:, None]
    source = jnp.argmax(hits, axis=1)
    filled = jnp.any(hits, axis=1)
    slots = [
        jnp.where(
            filled[s], lax.dynamic_index_in_dim(got, source[s], 0, keepdims=False), jnp.bfloat16(0)
        )
        for s in range(MOST)
    ]
    return new_momentum, jnp.stack(slots, axis=1)


def solution(mesh):
    in_specs = (
        P("dp", "expert", None),
        P("dp", "expert", None),
        P("dp", "expert", None),
        P("dp", "expert", None),
        P(),
    )
    out_specs = (P("dp", "expert", None), P("dp", "expert", None))
    return jax.shard_map(body, mesh=mesh, in_specs=in_specs, out_specs=out_specs, check_vma=False)
```

time: 949 us -> 200 us (0.21)
  waiting for transfers between devices: 906 us -> 48.8 us
  blocking collectives: 0 us -> 59.2 us
  starting transfers between devices: 0.21 us -> 47.4 us
    psum x3 -> x0, waiting for transfers between devices: 626 us -> none  [gram_matrix(): lax.psum(partial_value.astype(jnp.bfloat16), 'dp').astype(jnp.float32)]
    unnamed x6 -> x0, waiting for transfers between devices: 221 us -> none
    all_gather x1 -> x0, waiting for transfers between devices: 59.5 us -> none  [body(): lax.all_gather(ns_input, 'expert', axis=1, tiled=True)]
    all_to_all x0 -> x2, blocking collectives: none -> 59.2 us  [the longest x1 39.9 us: body(): near = lax.all_to_all(chip, 'dp', 0, 0, axis_index_groups=near_groups)]
    all_to_all x0 -> x3, waiting for transfers between devices: none -> 43.5 us  [the longest x1 17.7 us: body(): lax.all_to_all(jnp.broadcast_to(piece[None], packed.shape), 'dp', 0, 0, a...]
    all_to_all x0 -> x3, starting transfers between devices: none -> 24 us  [the longest x1 9.43 us: body(): grad = lax.all_to_all(near, 'dp', 0, 0, axis_index_groups=far_groups)]
    ppermute x0 -> x4, starting transfers between devices: none -> 23.4 us  [the longest x2 11.2 us: swap_rows(): theirs = lax.ppermute(given, 'dp', swap)]
  transfers between devices with their start and end apart: 5 -> 7, of which waited for: 5 -> 7; matrix products, arithmetic and copies ran while one was open for 0% -> 2% of each run, Pallas kernels for 0% -> 0%
where the time goes in v1:
time: 200 us; the launch traced here: 199 us
  blocking collectives  59.2 us (30%)
  waiting for transfers between devices  48.8 us (24%)
  starting transfers between devices  47.4 us (24%)
  local copies, waits for them, and re-layouts  11.7 us (6%)
  other arithmetic  9.24 us (5%)
  between operations  8.25 us (4%)
  matrix products  7.23 us (4%)
  Pallas kernels  6.9 us (3%)
    all_to_all x1, blocking collectives, body(): near = lax.all_to_all(chip, 'dp', 0, 0, axis_index_groups=near_groups)  39.9 us
    all_to_all x1, blocking collectives, body(): piece = lax.all_to_all(packed, 'dp', 0, 0, axis_index_groups=z_groups)  19.3 us
    all_to_all x1, waiting for transfers between devices, body(): lax.all_to_all(jnp.broadcast_to(piece[None], packed.shape), 'dp', 0, 0, a...  17.7 us
    all_to_all x1, waiting for transfers between devices, body(): grad = lax.all_to_all(near, 'dp', 0, 0, axis_index_groups=far_groups)  16.8 us
    ppermute x2, starting transfers between devices, swap_rows(): theirs = lax.ppermute(given, 'dp', swap)  11.2 us
    all_to_all x1, starting transfers between devices, body(): grad = lax.all_to_all(near, 'dp', 0, 0, axis_index_groups=far_groups)  9.43 us
    all_to_all x1, waiting for transfers between devices, body(): lax.all_to_all(sent, 'expert', 0, 0).reshape(all_experts, local_rows, FF)  9.02 us
    ppermute x1, starting transfers between devices, body(): other = lax.ppermute(partial_of(1 - core), 'dp', swap)  8.78 us
  transfers between devices with their start and end apart: 7, of which 7 were waited for; matrix products, arithmetic and copies ran while one was open for 2% of the time, Pallas kernels for 0%

profile of v1, /device:TPU:1, one launch (start us, length us, event | category | flops | bytes accessed | tf_op | source)
XLA Modules:
  0.0 198.7 jit_solution(10127543828954423609)
XLA Ops:
  0.7 0.8 compare_bitcast_fusion.1
  1.6 0.7 copy-done
  2.2 3.3 %fusion.1 = bf16[2048,384]{0,1:T(8,128)(2,1)} fusion(bf16[512,1,2048]{2,0,1:T(8,128)(2,1)S(1)} %copy-done, bf16[512,1,384]{2,0,1:T(8,128)(2,1)} %param.6, pred[512]{0:T(512)(128)(4,1)S(1)} %eq.99), kind=kOutput, calls=%fused_computation.4 | convolution fusion | flops 806289408 | bytes 4063744 | tf_op jit(solution)/shard_map/dot_general | solution.py:92
  5.6 8.8 %collective-permute-start.1 = (bf16[2048,384]{0,1:T(8,128)(2,1)}, bf16[2048,384]{0,1:T(8,128)(2,1)}, u32[]{:S(2)}, u32[]{:S(2)}) collective-permute-start(bf16[2048,384]{0,1:T(8,128)(2,1)} %fusion.1), channel_id=1, source_target_pairs={{0,16},{16,0},{32,48},{48,32},{64,80},{80,64},{96,112},{112,96},{1... | collective-permute-start | bytes 4718600 | tf_op jit(solution)/shard_map/ppermute | solution.py:96
  14.4 3.3 %collective-permute-done.1 = bf16[2048,384]{0,1:T(8,128)(2,1)} collective-permute-done((bf16[2048,384]{0,1:T(8,128)(2,1)}, bf16[2048,384]{0,1:T(8,128)(2,1)}, u32[]{:S(2)}, u32[]{:S(2)}) %collective-permute-start.1) | collective-permute-done | bytes 1572896 | tf_op jit(solution)/shard_map/ppermute | solution.py:96
  17.7 3.7 %fusion = bf16[2048,384]{0,1:T(8,128)(2,1)} fusion(bf16[2048,384]{0,1:T(8,128)(2,1)} %collective-permute-done.1, bf16[512,1,2048]{2,0,1:T(8,128)(2,1)S(1)} %copy-done, bf16[512,1,384]{2,0,1:T(8,128)(2,1)S(1)} %copy-done.2, pred[512]{0:T(512)(128)(4,1)S(1)} %eq.95), kind=kOutput, calls=%fused_computation.1 | convolution fusion | flops 809435136 | bytes 5636608 | tf_op jit(solution)/shard_map/dot_general | solution.py:92
  21.4 3.8 %reshape.150 = bf16[4,4,128,384]{2,1,0,3:T(4,128)(2,1)} reshape(bf16[2048,384]{0,1:T(8,128)(2,1)} %fusion) | data formatting | bytes 3145728 | tf_op jit(solution)/shard_map/reshape | solution.py:98
  25.2 2.0 %copy.52 = bf16[4,4,128,384]{2,0,3,1:T(4,128)(2,1)S(1)} copy(bf16[4,4,128,384]{2,1,0,3:T(4,128)(2,1)} %reshape.150) | data formatting | bytes 3145728 | tf_op jit(solution)/shard_map/reshape | solution.py:98
  27.2 39.9 %all_to_all.25 = bf16[4,4,128,384]{2,1,3,0:T(4,128)(2,1)} all-to-all(bf16[4,4,128,384]{2,1,3,0:T(4,128)(2,1)S(1)} %bitcast.91), channel_id=1, replica_groups={{0,32,64,96},{16,48,80,112},{128,160,192,224},{144,176,208,240},{256,28..., dimensions={0} | all-to-all | bytes 3145728 | tf_op jit(solution)/shard_map/all_to_all | solution.py:99
  67.1 2.3 %reduce_sum.39 = bf16[4,128,384]{1,0,2:T(4,128)(2,1)S(1)} reduce(bf16[4,4,128,384]{2,1,3,0:T(4,128)(2,1)} %all_to_all.25, bf16[]{:T(256)} %constant.62.clone.1), dimensions={0}, to_apply=%region_0.1 | reduce | flops 589824 | bytes 1966082 | tf_op jit(solution)/shard_map/reduce_sum | solution.py:100
  69.4 0.8 copy.35
  70.2 9.4 %all-to-all-start.1 = ((bf16[4,128,384]{1,2,0:T(8,128)(2,1)}), bf16[4,128,384]{1,2,0:T(8,128)(2,1)S(1)}, u32[]{:S(2)}, u32[]{:S(2)}) async-start(bf16[4,128,384]{1,2,0:T(8,128)(2,1)} %copy.35), calls=%async_computation.1 | async-start | bytes 786432 | tf_op jit(solution)/shard_map/all_to_all | solution.py:101
  79.8 3.4 %collective-permute-start = (f32[64,384]{1,0:T(8,128)S(1)}, f32[64,384]{1,0:T(8,128)S(1)}, u32[]{:S(2)}, u32[]{:S(2)}) collective-permute-start(f32[64,384]{1,0:T(8,128)S(1)} %bitcast.95), channel_id=1, source_target_pairs={{0,16},{16,0},{32,48},{48,32},{64,80},{80,64},{96,112},{112,96},{1... | collective-permute-start | bytes 294920 | tf_op jit(solution)/shard_map/ppermute | solution.py:118
  83.3 0.9 collective-permute-done
  84.2 16.8 %all-to-all-done.1 = bf16[4,128,384]{1,2,0:T(8,128)(2,1)S(1)} async-done(((bf16[4,128,384]{1,2,0:T(8,128)(2,1)}), bf16[4,128,384]{1,2,0:T(8,128)(2,1)S(1)}, u32[]{:S(2)}, u32[]{:S(2)}) %all-to-all-start.1) | async-done | bytes 393248 | tf_op jit(solution)/shard_map/all_to_all | solution.py:101
  101.6 19.3 %all_to_all.26 = bf16[16,48,128]{2,1,0:T(8,128)(2,1)S(1)} all-to-all(bf16[16,48,128]{2,1,0:T(8,128)(2,1)S(1)} %bitcast.94), channel_id=1, replica_groups={{0,32,64,96,128,160,192,224,256,288,320,352,384,416,448,480},{16,48,80,..., dimensions={0} | all-to-all | bytes 393216 | tf_op jit(solution)/shard_map/all_to_all | solution.py:130
  120.9 0.8 broadcast_in_dim.68
  121.7 7.8 %all-to-all-start.3 = ((f32[16,48,128]{2,1,0:T(8,128)}), f32[16,48,128]{2,1,0:T(8,128)S(1)}, u32[]{:S(2)}, u32[]{:S(2)}) async-start(f32[16,48,128]{2,1,0:T(8,128)} %broadcast_in_dim.68), calls=%async_computation.3 | async-start | bytes 786432 | tf_op jit(solution)/shard_map/all_to_all | solution.py:132
  129.6 17.7 %all-to-all-done.3 = f32[16,48,128]{2,1,0:T(8,128)S(1)} async-done(((f32[16,48,128]{2,1,0:T(8,128)}), f32[16,48,128]{2,1,0:T(8,128)S(1)}, u32[]{:S(2)}, u32[]{:S(2)}) %all-to-all-start.3) | async-done | bytes 393248 | tf_op jit(solution)/shard_map/all_to_all | solution.py:132
  147.3 6.9 %shard_map.68 = bf16[128,384]{1,0:T(8,128)(2,1)S(1)} custom-call(f32[768,128]{1,0:T(8,128)S(1)} %bitcast.88, bf16[128,384]{1,0:T(8,128)(2,1)S(1)} %get-tuple-element.18.x_ref), custom_call_target="tpu_custom_call" | custom-call | tf_op jit(solution)/shard_map/pallas_call | solution.py:136
  154.2 8.7 %collective-permute-start.3 = (bf16[64,384]{1,0:T(8,128)(2,1)S(1)}, bf16[64,384]{1,0:T(8,128)(2,1)S(1)}, u32[]{:S(2)}, u32[]{:S(2)}) collective-permute-start(bf16[64,384]{1,0:T(8,128)(2,1)S(1)} %dynamic-slice_bitcast_fusion.1), channel_id=1, source_target_pairs={{0,16},{16,0},{32,48},{48,32},{64,80},{80,64},{96,112},{112,96},{1... | collective-permute-start | bytes 147464 | tf_op jit(solution)/shard_map/ppermute | solution.py:113
  162.9 0.8 collective-permute-done.3
  163.8 1.4 broadcast_select_fusion
  165.2 6.8 %all-to-all-start.4 = ((bf16[16,2,64,384]{3,2,1,0:T(8,128)(2,1)}), bf16[16,2,64,384]{3,2,1,0:T(8,128)(2,1)}, u32[]{:S(2)}, u32[]{:S(2)}) async-start(bf16[16,2,64,384]{3,2,1,0:T(8,128)(2,1)} %broadcast_select_fusion), calls=%async_computation.4 | async-start | bytes 3145728 | tf_op jit(solution)/shard_map/all_to_all | solution.py:156
  172.2 0.7 compare_reduce_fusion
  172.9 0.6 fusion.24
  181.1 2.5 %collective-permute-start.2 = (f32[64,384]{1,0:T(8,128)S(1)}, f32[64,384]{1,0:T(8,128)S(1)}, u32[]{:S(2)}, u32[]{:S(2)}) collective-permute-start(f32[64,384]{1,0:T(8,128)S(1)} %dynamic-slice_bitcast_fusion), channel_id=1, source_target_pairs={{0,16},{16,0},{32,48},{48,32},{64,80},{80,64},{96,112},{112,96},{1... | collective-permute-start | bytes 294920 | tf_op jit(solution)/shard_map/ppermute | solution.py:113
  183.6 0.7 fusion.23
  184.6 0.8 copy.39
  185.4 9.0 %all-to-all-done.4 = bf16[16,2,64,384]{3,2,1,0:T(8,128)(2,1)} async-done(((bf16[16,2,64,384]{3,2,1,0:T(8,128)(2,1)}), bf16[16,2,64,384]{3,2,1,0:T(8,128)(2,1)}, u32[]{:S(2)}, u32[]{:S(2)}) %all-to-all-start.4) | async-done | bytes 1572896 | tf_op jit(solution)/shard_map/all_to_all | solution.py:156
  194.4 3.4 %select_bitcast_fusion.3 = (bf16[64,1,384]{2,0,1:T(8,128)(2,1)S(1)}, bf16[64,1,384]{2,0,1:T(8,128)(2,1)S(1)}, bf16[64,1,384]{2,0,1:T(8,128)(2,1)S(1)}, bf16[64,1,384]{2,0,1:T(8,128)(2,1)S(1)}) fusion(bf16[32,64,384]{2,1,0:T(8,128)(2,1)} %bitcast.25, s32[]{:T(128)S(6)} %select_n.162, pred[]{:T(512)} %bitcast.16, s32[]{:T(128)S(6)} %select_n.174, ...), kind=kLoop, calls=%fused_computation.43 | loop fusion | flops 98304 | bytes 393236 | tf_op jit(solution)/shard_map/jit(_where)/select_n | solution.py:162
  197.9 0.8 copy.40
  (38 shorter events, 1.8 us)
Async XLA Ops:
  0.6 1.6 copy-start
  2.2 15.5 %copy-start.2 = (bf16[512,1,384]{2,0,1:T(8,128)(2,1)S(1)}, bf16[512,1,384]{2,0,1:T(8,128)(2,1)}, u32[]{:S(2)}) copy-start(bf16[512,1,384]{2,0,1:T(8,128)(2,1)} %param.6) | copy-start | bytes 1179652
  5.6 12.1 %collective-permute-start.1 = (bf16[2048,384]{0,1:T(8,128)(2,1)}, bf16[2048,384]{0,1:T(8,128)(2,1)}, u32[]{:S(2)}, u32[]{:S(2)}) collective-permute-start(bf16[2048,384]{0,1:T(8,128)(2,1)} %fusion.1), channel_id=1, source_target_pairs={{0,16},{16,0},{32,48},{48,32},{64,80},{80,64},{96,112},{112,96},{1... | collective-permute-start | bytes 4718600 | tf_op jit(solution)/shard_map/ppermute | solution.py:96
  67.1 12.6 %copy-start.1 = (f32[64,2,384]{2,1,0:T(2,128)S(1)}, f32[64,2,384]{2,1,0:T(2,128)}, u32[]{:S(2)}) copy-start(f32[64,2,384]{2,1,0:T(2,128)} %param.8) | copy-start | bytes 589828
  70.2 30.8 %all-to-all-start.1 = ((bf16[4,128,384]{1,2,0:T(8,128)(2,1)}), bf16[4,128,384]{1,2,0:T(8,128)(2,1)S(1)}, u32[]{:S(2)}, u32[]{:S(2)}) async-start(bf16[4,128,384]{1,2,0:T(8,128)(2,1)} %copy.35), calls=%async_computation.1 | async-start | bytes 786432 | tf_op jit(solution)/shard_map/all_to_all | solution.py:101
  79.8 4.3 %collective-permute-start = (f32[64,384]{1,0:T(8,128)S(1)}, f32[64,384]{1,0:T(8,128)S(1)}, u32[]{:S(2)}, u32[]{:S(2)}) collective-permute-start(f32[64,384]{1,0:T(8,128)S(1)} %bitcast.95), channel_id=1, source_target_pairs={{0,16},{16,0},{32,48},{48,32},{64,80},{80,64},{96,112},{112,96},{1... | collective-permute-start | bytes 294920 | tf_op jit(solution)/shard_map/ppermute | solution.py:118
  101.2 28.3 %copy-start.3 = (s32[32,1]{0,1:T(1,128)S(1)}, s32[32,1]{0,1:T(1,128)}, u32[]{:S(2)}) copy-start(s32[32,1]{0,1:T(1,128)} %param.9) | copy-start | bytes 388
  121.7 25.6 %all-to-all-start.3 = ((f32[16,48,128]{2,1,0:T(8,128)}), f32[16,48,128]{2,1,0:T(8,128)S(1)}, u32[]{:S(2)}, u32[]{:S(2)}) async-start(f32[16,48,128]{2,1,0:T(8,128)} %broadcast_in_dim.68), calls=%async_computation.3 | async-start | bytes 786432 | tf_op jit(solution)/shard_map/all_to_all | solution.py:132
  154.2 9.6 %collective-permute-start.3 = (bf16[64,384]{1,0:T(8,128)(2,1)S(1)}, bf16[64,384]{1,0:T(8,128)(2,1)S(1)}, u32[]{:S(2)}, u32[]{:S(2)}) collective-permute-start(bf16[64,384]{1,0:T(8,128)(2,1)S(1)} %dynamic-slice_bitcast_fusion.1), channel_id=1, source_target_pairs={{0,16},{16,0},{32,48},{48,32},{64,80},{80,64},{96,112},{112,96},{1... | collective-permute-start | bytes 147464 | tf_op jit(solution)/shard_map/ppermute | solution.py:113
  165.2 29.2 %all-to-all-start.4 = ((bf16[16,2,64,384]{3,2,1,0:T(8,128)(2,1)}), bf16[16,2,64,384]{3,2,1,0:T(8,128)(2,1)}, u32[]{:S(2)}, u32[]{:S(2)}) async-start(bf16[16,2,64,384]{3,2,1,0:T(8,128)(2,1)} %broadcast_select_fusion), calls=%async_computation.4 | async-start | bytes 3145728 | tf_op jit(solution)/shard_map/all_to_all | solution.py:156
  181.1 3.5 %collective-permute-start.2 = (f32[64,384]{1,0:T(8,128)S(1)}, f32[64,384]{1,0:T(8,128)S(1)}, u32[]{:S(2)}, u32[]{:S(2)}) collective-permute-start(f32[64,384]{1,0:T(8,128)S(1)} %dynamic-slice_bitcast_fusion), channel_id=1, source_target_pairs={{0,16},{16,0},{32,48},{48,32},{64,80},{80,64},{96,112},{112,96},{1... | collective-permute-start | bytes 294920 | tf_op jit(solution)/shard_map/ppermute | solution.py:113

commit v2 on v1

v2 whole, which is shorter than its diff:
```python
import functools
import math

import jax
import jax.numpy as jnp
import numpy as np
from jax import lax
from jax.experimental import pallas as pl
from jax.experimental.pallas import tpu as pltpu
from jax.sharding import Mesh
from jax.sharding import PartitionSpec as P

D = 2048
FF = 384
TILE = 256
ITERS = 3
MOST = 4
CORES = 2
NEAR = 4
FAR = 4
ROWS = 64
PAIR = CORES * ROWS
LANE = 128

COEF_A = 3.4445
COEF_B = -4.775
COEF_C = 2.0315
BETA = 0.95
EPSILON = 1e-07
BLOCKS = ((0, 0), (0, 1), (0, 2), (1, 1), (1, 2), (2, 2))
MIB = 1024 * 1024
VMEM = pl.BlockSpec(memory_space=pltpu.VMEM)
SMEM = pl.BlockSpec(memory_space=pltpu.SMEM)
BF16 = jnp.bfloat16
F32 = jnp.float32


def call(kernel, outs, *args, scalars=1, scratch=(), flops=0):
    many = isinstance(outs, list)
    nbytes = sum(a.size * a.dtype.itemsize for a in args)
    return pl.pallas_call(
        kernel,
        out_shape=outs,
        in_specs=[SMEM] * scalars + [VMEM] * (len(args) - scalars),
        out_specs=[VMEM] * len(outs) if many else VMEM,
        scratch_shapes=list(scratch),
        compiler_params=pltpu.CompilerParams(vmem_limit_bytes=16 * MIB),
        cost_estimate=pl.CostEstimate(flops=flops, bytes_accessed=nbytes, transcendentals=0),
    )(*args)


def shape(dims, dtype=BF16):
    return jax.ShapeDtypeStruct(dims, dtype)


def transposed_dot(x, y):
    return lax.dot_general(x, y, (((0,), (0,)), ((), ())), preferred_element_type=F32)


def partial_kernel(theirs, where_ref, acts_ref, grads_ref, out_ref, masked_ref):
    z, core = where_ref[0], where_ref[1]
    expert = 1 - core if theirs else core
    for tile in range(acts_ref.shape[0] // TILE):
        rows = slice(tile * TILE, (tile + 1) * TILE)
        factor = jnp.where(where_ref[2 + tile] == expert, 1.0, 0.0).astype(F32)
        masked_ref[rows, :] = (grads_ref[rows, :].astype(F32) * factor).astype(BF16)
    masked = masked_ref[...]
    for rel in range(NEAR):
        cls = lax.rem(z + rel, NEAR)
        for q in range(FAR):
            start = pl.multiple_of((q * NEAR + cls) * PAIR, PAIR)
            block = transposed_dot(acts_ref[:, pl.ds(start, PAIR)], masked)
            out_ref[rel, q] = block.astype(BF16)


def add_kernel(mine_ref, other_ref, own_ref, up1_ref, up2_ref, down2_ref, down1_ref):
    def total(rel, qs):
        return (mine_ref[rel, qs].astype(F32) + other_ref[rel, qs].astype(F32)).astype(BF16)

    half = FAR // 2
    own_ref[...] = total(0, slice(None))
    up1_ref[...] = total(1, slice(None))
    up2_ref[...] = total(2, slice(0, half))
    down2_ref[...] = total(2, slice(half, FAR))
    down1_ref[...] = total(3, slice(None))


def near_kernel(
    where_ref, own_ref, a_ref, b_ref, c_ref, d_ref, keep_ref, up1_ref, up2_ref, down1_ref
):
    at = where_ref[0] // NEAR
    half = FAR // 2

    def total(q):
        return own_ref[q].astype(F32) + a_ref[q].astype(F32) + b_ref[q].astype(F32)

    for rel, out_ref in enumerate((keep_ref, up1_ref, up2_ref, down1_ref)):
        q = lax.rem(at + rel, FAR)

        @pl.when(q < half)
        def _():
            out_ref[...] = (total(q) + c_ref[q].astype(F32)).astype(out_ref.dtype)

        @pl.when(q >= half)
        def _():
            out_ref[...] = (total(q) + d_ref[q - half].astype(F32)).astype(out_ref.dtype)


def momentum_kernel(
    where_ref, keep_ref, a_ref, b_ref, c_ref, kept_ref, lent_ref, ns_ref, mine_ref, give_ref, gram_ref
):
    core = where_ref[1]
    for who, old_ref, new_ref in ((core, kept_ref, mine_ref), (1 - core, lent_ref, give_ref)):
        rows = pl.ds(pl.multiple_of(who * ROWS, ROWS), ROWS)
        grad = keep_ref[rows, :] + a_ref[rows, :].astype(F32)
        grad = grad + b_ref[rows, :].astype(F32) + c_ref[rows, :].astype(F32)
        new = BETA * old_ref[...] + grad
        new_ref[...] = new
        ns_ref[rows, :] = (grad + BETA * new).astype(BF16)
    x = ns_ref[...]
    gram = transposed_dot(x, x).astype(BF16)
    for at, (i, j) in enumerate(BLOCKS):
        gram_ref[at * LANE : (at + 1) * LANE, :] = gram[
            i * LANE : (i + 1) * LANE, j * LANE : (j + 1) * LANE
        ]


def piece_kernel(parts_ref, out_ref):
    total = parts_ref[0].astype(F32)
    for at in range(1, parts_ref.shape[0]):
        total = total + parts_ref[at].astype(F32)
    for at in range(out_ref.shape[0]):
        out_ref[at] = total


def split(x):
    high = x.astype(BF16)
    return high, (x - high.astype(F32)).astype(BF16)


def dot(x, y):
    return jnp.dot(x, y, preferred_element_type=F32)


def dot3(x, y):
    (xh, xl), (yh, yl) = x, y
    return dot(xh, yh) + (dot(xh, yl) + dot(xl, yh))


def newton_schulz_kernel(owner_ref, gram_ref, x_ref, out_ref):
    blocks = {}
    for at, (i, j) in enumerate(BLOCKS):
        block = gram_ref[at * LANE : (at + 1) * LANE, :]
        blocks[i, j] = block
        if i != j:
            blocks[j, i] = block.T
    gram = jnp.concatenate(
        [jnp.concatenate([blocks[i, j] for j in range(3)], axis=1) for i in range(3)], axis=0
    )
    rows = lax.broadcasted_iota(jnp.int32, (FF, FF), 0)
    cols = lax.broadcasted_iota(jnp.int32, (FF, FF), 1)
    eye = (rows == cols).astype(F32)
    trace = jnp.sum(jnp.sum(gram * eye, axis=1, keepdims=True), axis=0, keepdims=True)
    inv_norm = 1.0 / (jnp.sqrt(trace) + EPSILON)
    weights = gram * (inv_norm * inv_norm)
    total = None
    for sweep in range(ITERS):
        parts = split(weights)
        poly = COEF_A * eye + COEF_B * weights + COEF_C * dot3(parts, parts)
        poly_parts = split(poly)
        total = poly if total is None else dot3(split(total), poly_parts)
        if sweep < ITERS - 1:
            weights = dot3(split(dot3(parts, poly_parts)), poly_parts)
    high, low = split(total * (inv_norm * math.sqrt(D)))
    x = x_ref[...]
    update = (dot(x, high) + dot(x, low)).astype(BF16)
    out_ref[...] = jnp.zeros_like(out_ref)
    for core in range(CORES):
        out_ref[core, owner_ref[0]] = update[core * ROWS : (core + 1) * ROWS, :]


def stack_kernel(source_ref, got_ref, out_ref, wide_ref):
    for slot in range(MOST):
        source = source_ref[slot]
        filled = jnp.where(source >= 0, 1.0, 0.0).astype(F32)
        wide_ref[:, slot, :] = got_ref[jnp.maximum(source, 0)].astype(F32) * filled
    out_ref[...] = wide_ref[...].astype(BF16)


def ring(size, step):
    return [(i, (i + step) % size) for i in range(size)]


def body(acts, grads, tile_expert, momentum, packing):
    z, core, group = lax.axis_index("z"), lax.axis_index("core"), lax.axis_index("expert")
    n_z, n_owner = lax.axis_size("z"), lax.axis_size("expert")
    where = jnp.concatenate([jnp.stack([z, core]), tile_expert[:, 0, 0]]).astype(jnp.int32)
    flat_acts, flat_grads = acts[:, 0, :], grads[:, 0, :]

    def go(value, step):
        return lax.ppermute(value, "z", ring(n_z, step))

    def swap(value):
        return lax.ppermute(value, "core", ring(CORES, 1))

    def partial_of(theirs):
        return call(
            functools.partial(partial_kernel, theirs),
            shape((NEAR, FAR, PAIR, FF)),
            where,
            flat_acts,
            flat_grads,
            scratch=[pltpu.VMEM(flat_grads.shape, BF16)],
            flops=2 * flat_acts.size * FF,
        )

    other = swap(partial_of(True))
    mine = partial_of(False)
    whole, half = shape((FAR, PAIR, FF)), shape((FAR // 2, PAIR, FF))
    own, up1, up2, down2, down1 = call(
        add_kernel, [whole, whole, half, half, whole], mine, other, scalars=0
    )
    chunk = shape((PAIR, FF))
    keep, up1, up2, down1 = call(
        near_kernel,
        [shape((PAIR, FF), F32), chunk, chunk, chunk],
        where,
        own,
        go(up1, 1),
        go(down1, -1),
        go(up2, 2),
        go(down2, -2),
    )
    kept = lax.dynamic_index_in_dim(momentum, core, 1, keepdims=False)
    lent = swap(lax.dynamic_index_in_dim(momentum, 1 - core, 1, keepdims=False))
    rows = shape((ROWS, FF), F32)
    packed_rows = len(BLOCKS) * LANE
    ns_input, new_mine, new_give, packed = call(
        momentum_kernel,
        [chunk, rows, rows, shape((packed_rows, LANE))],
        where,
        keep,
        go(up1, NEAR),
        go(up2, 2 * NEAR),
        go(down1, -NEAR),
        kept,
        lent,
        flops=2 * PAIR * FF * FF,
    )
    packed = packed.reshape(n_z, packed_rows // n_z, LANE)
    pieces = call(
        piece_kernel, shape(packed.shape, F32), lax.all_to_all(packed, "z", 0, 0), scalars=0
    )
    gram = lax.all_to_all(pieces, "z", 0, 0).reshape(packed_rows, LANE)

    new_other = swap(new_give)
    new_momentum = jnp.stack(
        [jnp.where(core == 0, new_mine, new_other), jnp.where(core == 0, new_other, new_mine)], axis=1
    )

    owner_ids = packing[:, 0]
    experts = owner_ids.shape[0]
    positions = jnp.arange(experts, dtype=jnp.int32)
    shared = (owner_ids[:, None] == owner_ids[None, :]) & (positions[None, :] < positions[:, None])
    target = owner_ids * MOST + jnp.sum(shared.astype(jnp.int32), axis=1)
    hits = target[None, :] == group * MOST + jnp.arange(MOST, dtype=jnp.int32)[:, None]
    lies = positions % CORES * n_owner + positions // CORES
    source = jnp.max(jnp.where(hits, lies[None, :], -1), axis=1)
    my_owner = lax.dynamic_slice_in_dim(owner_ids, group * CORES + core, 1, 0)

    sent = call(
        newton_schulz_kernel,
        shape((CORES, n_owner, ROWS, FF)),
        my_owner,
        gram,
        ns_input,
        flops=2 * 27 * FF * FF * FF,
    )
    got = lax.all_to_all(
        sent.reshape(CORES * n_owner, ROWS, FF), ("core", "expert"), 0, 0
    )
    stacked = call(
        stack_kernel,
        shape((ROWS, MOST, FF)),
        source,
        got,
        scratch=[pltpu.VMEM((ROWS, MOST, FF), F32)],
    )
    return new_momentum, stacked


def solution(mesh):
    n_dp, n_owner = mesh.devices.shape
    devices = np.asarray(mesh.devices).reshape(n_dp // CORES, CORES, n_owner)
    finer = Mesh(devices, ("z", "core", "expert"))
    spec = P(("z", "core"), "expert", None)
    return jax.shard_map(
        body, mesh=finer, in_specs=(spec,) * 4 + (P(),), out_specs=(spec, spec), check_vma=False
    )
```

time: 200 us -> 171 us (0.85)
  blocking collectives: 59.2 us -> 20.8 us
  starting transfers between devices: 47.4 us -> 70.2 us
  Pallas kernels: 6.9 us -> 16.9 us
  other arithmetic: 9.24 us -> 1.14 us
  local copies, waits for them, and re-layouts: 11.7 us -> 4.2 us
  between operations: 8.25 us -> 0.88 us
  waiting for transfers between devices: 48.8 us -> 56.1 us
  matrix products: 7.23 us -> 0 us
    all_to_all x2 -> x1, blocking collectives: 59.2 us -> 20.8 us  [body(): lax.all_to_all(packed, 'z', 0, 0)]
    ppermute x4 -> x10, starting transfers between devices: 23.4 us -> 47.6 us  [the longest x7 33.5 us: go(): return lax.ppermute(value, 'z', ring(n_z, step))]
    ppermute x4 -> x10, waiting for transfers between devices: 5.27 us -> 20.8 us  [the longest x7 18.9 us: go(): return lax.ppermute(value, 'z', ring(n_z, step))]
    pallas_call x1 -> x8, Pallas kernels: 6.9 us -> 16.9 us  [call(): pl.pallas_call(kernel, out_shape=outs, in_specs=[SMEM] * scalars + [VMEM]...]
    all_to_all x3 -> x2, waiting for transfers between devices: 43.5 us -> 35.3 us  [the longest x1 17.9 us: body(): lax.all_to_all(sent.reshape(CORES * n_owner, ROWS, FF), ('core', 'expert'...]
    dot_general x3 -> x0, matrix products: 7.23 us -> none  [the longest x2 6.97 us: partial_of(): lax.dot_general(flat_acts, masked, (((0,), (0,)), ((), ())), preferred_el...]
    reshape x2 -> x0, local copies, waits for them, and re-layouts: 5.83 us -> none  [body(): chip = chip.reshape(far, NEAR, pair_rows, FF).transpose(1, 0, 2, 3)]
    select_n x3 -> x0, other arithmetic: 4.78 us -> none  [the longest x1 3.39 us: body(): jnp.where(filled[s], lax.dynamic_index_in_dim(got, source[s], 0, keepdims...]
  transfers between devices with their start and end apart: 7 -> 12, of which waited for: 7 -> 8; matrix products, arithmetic and copies ran while one was open for 2% -> 1% of each run, Pallas kernels for 0% -> 2%
where the time goes in v2:
time: 171 us; the launch traced here: 170 us
  starting transfers between devices  70.2 us (41%)
  waiting for transfers between devices  56.1 us (33%)
  blocking collectives  20.8 us (12%)
  Pallas kernels  16.9 us (10%)
  local copies, waits for them, and re-layouts  4.2 us (2%)
    ppermute x7, starting transfers between devices, go(): return lax.ppermute(value, 'z', ring(n_z, step))  33.5 us
    all_to_all x1, blocking collectives, body(): lax.all_to_all(packed, 'z', 0, 0)  20.8 us
    ppermute x7, waiting for transfers between devices, go(): return lax.ppermute(value, 'z', ring(n_z, step))  18.9 us
    all_to_all x1, waiting for transfers between devices, body(): lax.all_to_all(sent.reshape(CORES * n_owner, ROWS, FF), ('core', 'expert'...  17.9 us
    all_to_all x1, waiting for transfers between devices, body(): gram = lax.all_to_all(pieces, 'z', 0, 0).reshape(packed_rows, LANE)  17.4 us
    pallas_call x8, Pallas kernels, call(): pl.pallas_call(kernel, out_shape=outs, in_specs=[SMEM] * scalars + [VMEM]...  16.9 us
    ppermute x3, starting transfers between devices, swap(): return lax.ppermute(value, 'core', ring(CORES, 1))  14 us
    all_to_all x1, starting transfers between devices, body(): lax.all_to_all(sent.reshape(CORES * n_owner, ROWS, FF), ('core', 'expert'...  13.9 us
  transfers between devices with their start and end apart: 12, of which 8 were waited for; matrix products, arithmetic and copies ran while one was open for 1% of the time, Pallas kernels for 2%

profile of v2, /device:TPU:1, one launch (start us, length us, event | category | flops | bytes accessed | tf_op | source)
XLA Modules:
  0.0 170.2 jit_solution(14826478182366801970)
XLA Ops:
  0.6 0.7 pad_add_fusion.where_ref
  1.4 1.6 copy-done
  3.0 1.0 copy-done.1
  4.0 1.9 %shard_map.69 = bf16[4,4,128,384]{3,2,1,0:T(8,128)(2,1)S(1)} custom-call(s32[4]{0:T(128)S(1)} %pad_add_fusion.where_ref, bf16[512,2048]{1,0:T(8,128)(2,1)S(1)} %bitcast.21, bf16[512,384]{1,0:T(8,128)(2,1)S(1)} %bitcast.23), custom_call_target="tpu_custom_call" | custom-call | flops 805306368 | bytes 2490384 | tf_op jit(solution)/shard_map/pallas_call | solution.py:41
  5.9 8.8 %collective-permute-start = (bf16[4,4,128,384]{3,2,1,0:T(8,128)(2,1)S(1)}, bf16[4,4,128,384]{3,2,1,0:T(8,128)(2,1)S(1)}, u32[]{:S(2)}, u32[]{:S(2)}) collective-permute-start(bf16[4,4,128,384]{3,2,1,0:T(8,128)(2,1)S(1)} %shard_map.69), channel_id=1, source_target_pairs={{0,16},{16,0},{1,17},{17,1},{2,18},{18,2},{3,19},{19,3},{4,20},{20... | collective-permute-start | bytes 4718600 | tf_op jit(solution)/shard_map/ppermute | solution.py:204
  14.7 1.9 %shard_map.68.mine_ref = bf16[4,4,128,384]{3,2,1,0:T(8,128)(2,1)S(1)} custom-call(s32[4]{0:T(128)S(1)} %pad_add_fusion.where_ref, bf16[512,2048]{1,0:T(8,128)(2,1)S(1)} %bitcast.22, bf16[512,384]{1,0:T(8,128)(2,1)S(1)} %bitcast.24), custom_call_target="tpu_custom_call" | custom-call | flops 805306368 | bytes 2490384 | tf_op jit(solution)/shard_map/pallas_call | solution.py:41
  16.6 1.1 collective-permute-done.other_ref
  18.1 1.9 %collective-permute-start.1 = (bf16[4,128,384]{2,1,0:T(8,128)(2,1)S(1)}, bf16[4,128,384]{2,1,0:T(8,128)(2,1)S(1)}, u32[]{:S(2)}, u32[]{:S(2)}) collective-permute-start(bf16[4,128,384]{2,1,0:T(8,128)(2,1)S(1)} %get-tuple-element.16), channel_id=1, source_target_pairs={{0,32},{32,64},{64,96},{96,128},{128,160},{160,192},{192,224},{224... | collective-permute-start | bytes 1179656 | tf_op jit(solution)/shard_map/ppermute | solution.py:201
  20.0 5.7 %collective-permute-start.2 = (bf16[4,128,384]{2,1,0:T(8,128)(2,1)S(1)}, bf16[4,128,384]{2,1,0:T(8,128)(2,1)S(1)}, u32[]{:S(2)}, u32[]{:S(2)}) collective-permute-start(bf16[4,128,384]{2,1,0:T(8,128)(2,1)S(1)} %get-tuple-element.17), channel_id=1, source_target_pairs={{0,480},{32,0},{64,32},{96,64},{128,96},{160,128},{192,160},{224,1... | collective-permute-start | bytes 1179656 | tf_op jit(solution)/shard_map/ppermute | solution.py:201
  25.7 1.9 %collective-permute-start.3 = (bf16[2,128,384]{2,1,0:T(8,128)(2,1)S(1)}, bf16[2,128,384]{2,1,0:T(8,128)(2,1)S(1)}, u32[]{:S(2)}, u32[]{:S(2)}) collective-permute-start(bf16[2,128,384]{2,1,0:T(8,128)(2,1)S(1)} %get-tuple-element.18), channel_id=1, source_target_pairs={{0,64},{32,96},{64,128},{96,160},{128,192},{160,224},{192,256},{22... | collective-permute-start | bytes 589832 | tf_op jit(solution)/shard_map/ppermute | solution.py:201
  27.7 5.5 %collective-permute-start.4 = (bf16[2,128,384]{2,1,0:T(8,128)(2,1)S(1)}, bf16[2,128,384]{2,1,0:T(8,128)(2,1)S(1)}, u32[]{:S(2)}, u32[]{:S(2)}) collective-permute-start(bf16[2,128,384]{2,1,0:T(8,128)(2,1)S(1)} %get-tuple-element.19), channel_id=1, source_target_pairs={{0,448},{32,480},{64,0},{96,32},{128,64},{160,96},{192,128},{224,1... | collective-permute-start | bytes 589832 | tf_op jit(solution)/shard_map/ppermute | solution.py:201
  33.4 3.1 %collective-permute-start.8 = (f32[64,384]{1,0:T(8,128)S(1)}, f32[64,384]{1,0:T(8,128)S(1)}, u32[]{:S(2)}, u32[]{:S(2)}) collective-permute-start(f32[64,384]{1,0:T(8,128)S(1)} %bitcast.28), channel_id=1, source_target_pairs={{0,16},{16,0},{1,17},{17,1},{2,18},{18,2},{3,19},{19,3},{4,20},{20... | collective-permute-start | bytes 294920 | tf_op jit(solution)/shard_map/ppermute | solution.py:204
  36.5 3.1 %collective-permute-done.3.c_ref = bf16[2,128,384]{2,1,0:T(8,128)(2,1)S(1)} collective-permute-done((bf16[2,128,384]{2,1,0:T(8,128)(2,1)S(1)}, bf16[2,128,384]{2,1,0:T(8,128)(2,1)S(1)}, u32[]{:S(2)}, u32[]{:S(2)}) %collective-permute-start.3) | collective-permute-done | bytes 196640 | tf_op jit(solution)/shard_map/ppermute | solution.py:201
  39.6 2.7 %collective-permute-done.4.d_ref = bf16[2,128,384]{2,1,0:T(8,128)(2,1)S(1)} collective-permute-done((bf16[2,128,384]{2,1,0:T(8,128)(2,1)S(1)}, bf16[2,128,384]{2,1,0:T(8,128)(2,1)S(1)}, u32[]{:S(2)}, u32[]{:S(2)}) %collective-permute-start.4) | collective-permute-done | bytes 196640 | tf_op jit(solution)/shard_map/ppermute | solution.py:201
  42.3 0.8 shard_map.71
  43.1 5.2 %collective-permute-start.5 = (bf16[128,384]{1,0:T(8,128)(2,1)S(1)}, bf16[128,384]{1,0:T(8,128)(2,1)S(1)}, u32[]{:S(2)}, u32[]{:S(2)}) collective-permute-start(bf16[128,384]{1,0:T(8,128)(2,1)S(1)} %get-tuple-element.21), channel_id=1, source_target_pairs={{0,128},{32,160},{64,192},{96,224},{128,256},{160,288},{192,320},{... | collective-permute-start | bytes 294920 | tf_op jit(solution)/shard_map/ppermute | solution.py:201
  48.3 8.1 %collective-permute-start.6 = (bf16[128,384]{1,0:T(8,128)(2,1)S(1)}, bf16[128,384]{1,0:T(8,128)(2,1)S(1)}, u32[]{:S(2)}, u32[]{:S(2)}) collective-permute-start(bf16[128,384]{1,0:T(8,128)(2,1)S(1)} %get-tuple-element.22), channel_id=1, source_target_pairs={{0,256},{32,288},{64,320},{96,352},{128,384},{160,416},{192,448},{... | collective-permute-start | bytes 294920 | tf_op jit(solution)/shard_map/ppermute | solution.py:201
  56.4 5.2 %collective-permute-start.7 = (bf16[128,384]{1,0:T(8,128)(2,1)S(1)}, bf16[128,384]{1,0:T(8,128)(2,1)S(1)}, u32[]{:S(2)}, u32[]{:S(2)}) collective-permute-start(bf16[128,384]{1,0:T(8,128)(2,1)S(1)} %get-tuple-element.23), channel_id=1, source_target_pairs={{0,384},{32,416},{64,448},{96,480},{128,0},{160,32},{192,64},{224,... | collective-permute-start | bytes 294920 | tf_op jit(solution)/shard_map/ppermute | solution.py:201
  61.6 1.0 collective-permute-done.6.b_ref
  62.6 12.1 %collective-permute-done.7.c_ref = bf16[128,384]{1,0:T(8,128)(2,1)S(1)} collective-permute-done((bf16[128,384]{1,0:T(8,128)(2,1)S(1)}, bf16[128,384]{1,0:T(8,128)(2,1)S(1)}, u32[]{:S(2)}, u32[]{:S(2)}) %collective-permute-start.7) | collective-permute-done | bytes 98336 | tf_op jit(solution)/shard_map/ppermute | solution.py:201
  74.7 0.9 shard_map.72
  75.6 20.8 %all_to_all.15.parts_ref = bf16[16,48,128]{2,1,0:T(8,128)(2,1)S(1)} all-to-all(bf16[16,48,128]{2,1,0:T(8,128)(2,1)S(1)} %bitcast.27), channel_id=1, replica_groups=mesh['z'=16,'core'=2,'expert'=16] {'z'}, dimensions={0} | all-to-all | bytes 393216 | tf_op jit(solution)/shard_map/all_to_all | solution.py:252
  96.4 0.8 shard_map.73
  97.2 8.8 %all-to-all-start.1 = ((f32[16,48,128]{2,1,0:T(8,128)}), f32[16,48,128]{2,1,0:T(8,128)S(1)}, u32[]{:S(2)}, u32[]{:S(2)}) async-start(f32[16,48,128]{2,1,0:T(8,128)} %shard_map.73), calls=%async_computation.1 | async-start | bytes 786432 | tf_op jit(solution)/shard_map/all_to_all | solution.py:254
  106.6 17.4 %all-to-all-done.1 = f32[16,48,128]{2,1,0:T(8,128)S(1)} async-done(((f32[16,48,128]{2,1,0:T(8,128)}), f32[16,48,128]{2,1,0:T(8,128)S(1)}, u32[]{:S(2)}, u32[]{:S(2)}) %all-to-all-start.1) | async-done | bytes 393248 | tf_op jit(solution)/shard_map/all_to_all | solution.py:254
  124.0 8.8 %shard_map.74 = bf16[2,16,64,384]{3,2,1,0:T(8,128)(2,1)} custom-call(s32[1]{0:T(128)} %bitcast.10.owner_ref, f32[768,128]{1,0:T(8,128)S(1)} %bitcast.25, bf16[128,384]{1,0:T(8,128)(2,1)S(1)} %get-tuple-element.27.x_ref), custom_call_target="tpu_custom_call" | custom-call | flops 3057647616 | bytes 491524 | tf_op jit(solution)/shard_map/pallas_call | solution.py:41
  132.8 13.9 %all-to-all-start.2 = ((bf16[32,64,384]{2,1,0:T(8,128)(2,1)}), bf16[32,64,384]{2,1,0:T(8,128)(2,1)S(1)}, u32[]{:S(2)}, u32[]{:S(2)}) async-start(bf16[32,64,384]{2,1,0:T(8,128)(2,1)} %bitcast.13), calls=%async_computation.2 | async-start | bytes 3145728 | tf_op jit(solution)/shard_map/all_to_all | solution.py:279
  146.9 2.1 %collective-permute-start.9 = (f32[64,384]{1,0:T(8,128)S(1)}, f32[64,384]{1,0:T(8,128)S(1)}, u32[]{:S(2)}, u32[]{:S(2)}) collective-permute-start(f32[64,384]{1,0:T(8,128)S(1)} %get-tuple-element.25), channel_id=1, source_target_pairs={{0,16},{16,0},{1,17},{17,1},{2,18},{18,2},{3,19},{19,3},{4,20},{20... | collective-permute-start | bytes 294920 | tf_op jit(solution)/shard_map/ppermute | solution.py:204
  149.2 0.9 collective-permute-done.9
  150.1 0.8 copy.13
  150.9 17.9 %all-to-all-done.2.got_ref = bf16[32,64,384]{2,1,0:T(8,128)(2,1)S(1)} async-done(((bf16[32,64,384]{2,1,0:T(8,128)(2,1)}), bf16[32,64,384]{2,1,0:T(8,128)(2,1)S(1)}, u32[]{:S(2)}, u32[]{:S(2)}) %all-to-all-start.2) | async-done | bytes 1572896 | tf_op jit(solution)/shard_map/all_to_all | solution.py:279
  168.8 1.4 shard_map.75
  (21 shorter events, 1.6 us)
Async XLA Ops:
  1.4 1.6 copy-start
  3.0 1.0 copy-start.1
  5.9 11.8 %collective-permute-start = (bf16[4,4,128,384]{3,2,1,0:T(8,128)(2,1)S(1)}, bf16[4,4,128,384]{3,2,1,0:T(8,128)(2,1)S(1)}, u32[]{:S(2)}, u32[]{:S(2)}) collective-permute-start(bf16[4,4,128,384]{3,2,1,0:T(8,128)(2,1)S(1)} %shard_map.69), channel_id=1, source_target_pairs={{0,16},{16,0},{1,17},{17,1},{2,18},{18,2},{3,19},{19,3},{4,20},{20... | collective-permute-start | bytes 4718600 | tf_op jit(solution)/shard_map/ppermute | solution.py:204
  16.6 16.6 %copy-start.2 = (f32[64,2,384]{2,1,0:T(2,128)S(1)}, f32[64,2,384]{2,1,0:T(2,128)}, u32[]{:S(2)}) copy-start(f32[64,2,384]{2,1,0:T(2,128)} %param.8) | copy-start | bytes 589828
  18.1 24.2 %collective-permute-start.1 = (bf16[4,128,384]{2,1,0:T(8,128)(2,1)S(1)}, bf16[4,128,384]{2,1,0:T(8,128)(2,1)S(1)}, u32[]{:S(2)}, u32[]{:S(2)}) collective-permute-start(bf16[4,128,384]{2,1,0:T(8,128)(2,1)S(1)} %get-tuple-element.16), channel_id=1, source_target_pairs={{0,32},{32,64},{64,96},{96,128},{128,160},{160,192},{192,224},{224... | collective-permute-start | bytes 1179656 | tf_op jit(solution)/shard_map/ppermute | solution.py:201
  20.0 22.3 %collective-permute-start.2 = (bf16[4,128,384]{2,1,0:T(8,128)(2,1)S(1)}, bf16[4,128,384]{2,1,0:T(8,128)(2,1)S(1)}, u32[]{:S(2)}, u32[]{:S(2)}) collective-permute-start(bf16[4,128,384]{2,1,0:T(8,128)(2,1)S(1)} %get-tuple-element.17), channel_id=1, source_target_pairs={{0,480},{32,0},{64,32},{96,64},{128,96},{160,128},{192,160},{224,1... | collective-permute-start | bytes 1179656 | tf_op jit(solution)/shard_map/ppermute | solution.py:201
  25.7 13.9 %collective-permute-start.3 = (bf16[2,128,384]{2,1,0:T(8,128)(2,1)S(1)}, bf16[2,128,384]{2,1,0:T(8,128)(2,1)S(1)}, u32[]{:S(2)}, u32[]{:S(2)}) collective-permute-start(bf16[2,128,384]{2,1,0:T(8,128)(2,1)S(1)} %get-tuple-element.18), channel_id=1, source_target_pairs={{0,64},{32,96},{64,128},{96,160},{128,192},{160,224},{192,256},{22... | collective-permute-start | bytes 589832 | tf_op jit(solution)/shard_map/ppermute | solution.py:201
  27.7 14.6 %collective-permute-start.4 = (bf16[2,128,384]{2,1,0:T(8,128)(2,1)S(1)}, bf16[2,128,384]{2,1,0:T(8,128)(2,1)S(1)}, u32[]{:S(2)}, u32[]{:S(2)}) collective-permute-start(bf16[2,128,384]{2,1,0:T(8,128)(2,1)S(1)} %get-tuple-element.19), channel_id=1, source_target_pairs={{0,448},{32,480},{64,0},{96,32},{128,64},{160,96},{192,128},{224,1... | collective-permute-start | bytes 589832 | tf_op jit(solution)/shard_map/ppermute | solution.py:201
  33.4 28.3 %collective-permute-start.8 = (f32[64,384]{1,0:T(8,128)S(1)}, f32[64,384]{1,0:T(8,128)S(1)}, u32[]{:S(2)}, u32[]{:S(2)}) collective-permute-start(f32[64,384]{1,0:T(8,128)S(1)} %bitcast.28), channel_id=1, source_target_pairs={{0,16},{16,0},{1,17},{17,1},{2,18},{18,2},{3,19},{19,3},{4,20},{20... | collective-permute-start | bytes 294920 | tf_op jit(solution)/shard_map/ppermute | solution.py:204
  43.1 62.9 %copy-start.3 = (s32[32,1]{0,1:T(1,128)S(1)}, s32[32,1]{0,1:T(1,128)}, u32[]{:S(2)}) copy-start(s32[32,1]{0,1:T(1,128)} %param.9) | copy-start | bytes 388
  43.1 18.5 %collective-permute-start.5 = (bf16[128,384]{1,0:T(8,128)(2,1)S(1)}, bf16[128,384]{1,0:T(8,128)(2,1)S(1)}, u32[]{:S(2)}, u32[]{:S(2)}) collective-permute-start(bf16[128,384]{1,0:T(8,128)(2,1)S(1)} %get-tuple-element.21), channel_id=1, source_target_pairs={{0,128},{32,160},{64,192},{96,224},{128,256},{160,288},{192,320},{... | collective-permute-start | bytes 294920 | tf_op jit(solution)/shard_map/ppermute | solution.py:201
  48.3 14.3 %collective-permute-start.6 = (bf16[128,384]{1,0:T(8,128)(2,1)S(1)}, bf16[128,384]{1,0:T(8,128)(2,1)S(1)}, u32[]{:S(2)}, u32[]{:S(2)}) collective-permute-start(bf16[128,384]{1,0:T(8,128)(2,1)S(1)} %get-tuple-element.22), channel_id=1, source_target_pairs={{0,256},{32,288},{64,320},{96,352},{128,384},{160,416},{192,448},{... | collective-permute-start | bytes 294920 | tf_op jit(solution)/shard_map/ppermute | solution.py:201
  56.4 18.3 %collective-permute-start.7 = (bf16[128,384]{1,0:T(8,128)(2,1)S(1)}, bf16[128,384]{1,0:T(8,128)(2,1)S(1)}, u32[]{:S(2)}, u32[]{:S(2)}) collective-permute-start(bf16[128,384]{1,0:T(8,128)(2,1)S(1)} %get-tuple-element.23), channel_id=1, source_target_pairs={{0,384},{32,416},{64,448},{96,480},{128,0},{160,32},{192,64},{224,... | collective-permute-start | bytes 294920 | tf_op jit(solution)/shard_map/ppermute | solution.py:201
  97.2 26.8 %all-to-all-start.1 = ((f32[16,48,128]{2,1,0:T(8,128)}), f32[16,48,128]{2,1,0:T(8,128)S(1)}, u32[]{:S(2)}, u32[]{:S(2)}) async-start(f32[16,48,128]{2,1,0:T(8,128)} %shard_map.73), calls=%async_computation.1 | async-start | bytes 786432 | tf_op jit(solution)/shard_map/all_to_all | solution.py:254
  132.8 36.0 %all-to-all-start.2 = ((bf16[32,64,384]{2,1,0:T(8,128)(2,1)}), bf16[32,64,384]{2,1,0:T(8,128)(2,1)S(1)}, u32[]{:S(2)}, u32[]{:S(2)}) async-start(bf16[32,64,384]{2,1,0:T(8,128)(2,1)} %bitcast.13), calls=%async_computation.2 | async-start | bytes 3145728 | tf_op jit(solution)/shard_map/all_to_all | solution.py:279
  146.9 3.2 %collective-permute-start.9 = (f32[64,384]{1,0:T(8,128)S(1)}, f32[64,384]{1,0:T(8,128)S(1)}, u32[]{:S(2)}, u32[]{:S(2)}) collective-permute-start(f32[64,384]{1,0:T(8,128)S(1)} %get-tuple-element.25), channel_id=1, source_target_pairs={{0,16},{16,0},{1,17},{17,1},{2,18},{18,2},{3,19},{19,3},{4,20},{20... | collective-permute-start | bytes 294920 | tf_op jit(solution)/shard_map/ppermute | solution.py:204

commit v3 on v2

--- a/solution.py
+++ b/solution.py
@@ -58,7 +58,7 @@
 
 
 def partial_kernel(theirs, where_ref, acts_ref, grads_ref, out_ref, masked_ref):
-    z, core = where_ref[0], where_ref[1]
+    near_at, core = where_ref[0], where_ref[1]
     expert = 1 - core if theirs else core
     for tile in range(acts_ref.shape[0] // TILE):
         rows = slice(tile * TILE, (tile + 1) * TILE)
@@ -66,7 +66,7 @@
         masked_ref[rows, :] = (grads_ref[rows, :].astype(F32) * factor).astype(BF16)
     masked = masked_ref[...]
     for rel in range(NEAR):
-        cls = lax.rem(z + rel, NEAR)
+        cls = lax.rem(near_at + rel, NEAR)
         for q in range(FAR):
             start = pl.multiple_of((q * NEAR + cls) * PAIR, PAIR)
             block = transposed_dot(acts_ref[:, pl.ds(start, PAIR)], masked)
@@ -85,35 +85,23 @@
     down1_ref[...] = total(3, slice(None))
 
 
-def near_kernel(
-    where_ref, own_ref, a_ref, b_ref, c_ref, d_ref, keep_ref, up1_ref, up2_ref, down1_ref
-):
-    at = where_ref[0] // NEAR
+def near_kernel(own_ref, a_ref, b_ref, c_ref, d_ref, out_ref):
     half = FAR // 2
-
-    def total(q):
-        return own_ref[q].astype(F32) + a_ref[q].astype(F32) + b_ref[q].astype(F32)
-
-    for rel, out_ref in enumerate((keep_ref, up1_ref, up2_ref, down1_ref)):
-        q = lax.rem(at + rel, FAR)
-
-        @pl.when(q < half)
-        def _():
-            out_ref[...] = (total(q) + c_ref[q].astype(F32)).astype(out_ref.dtype)
-
-        @pl.when(q >= half)
-        def _():
-            out_ref[...] = (total(q) + d_ref[q - half].astype(F32)).astype(out_ref.dtype)
+    for q in range(FAR):
+        last = c_ref[q] if q < half else d_ref[q - half]
+        total = own_ref[q].astype(F32) + a_ref[q].astype(F32)
+        out_ref[q] = (total + (b_ref[q].astype(F32) + last.astype(F32))).astype(BF16)
 
 
 def momentum_kernel(
-    where_ref, keep_ref, a_ref, b_ref, c_ref, kept_ref, lent_ref, ns_ref, mine_ref, give_ref, gram_ref
+    where_ref, parts_ref, kept_ref, lent_ref, ns_ref, mine_ref, give_ref, gram_ref
 ):
     core = where_ref[1]
     for who, old_ref, new_ref in ((core, kept_ref, mine_ref), (1 - core, lent_ref, give_ref)):
         rows = pl.ds(pl.multiple_of(who * ROWS, ROWS), ROWS)
-        grad = keep_ref[rows, :] + a_ref[rows, :].astype(F32)
-        grad = grad + b_ref[rows, :].astype(F32) + c_ref[rows, :].astype(F32)
+        grad = parts_ref[0, rows, :].astype(F32)
+        for at in range(1, FAR):
+            grad = grad + parts_ref[at, rows, :].astype(F32)
         new = BETA * old_ref[...] + grad
         new_ref[...] = new
         ns_ref[rows, :] = (grad + BETA * new).astype(BF16)
@@ -125,12 +113,12 @@
         ]
 
 
-def piece_kernel(parts_ref, out_ref):
+def spread_sum_kernel(parts_ref, out_ref):
     total = parts_ref[0].astype(F32)
     for at in range(1, parts_ref.shape[0]):
         total = total + parts_ref[at].astype(F32)
     for at in range(out_ref.shape[0]):
-        out_ref[at] = total
+        out_ref[at] = total.astype(out_ref.dtype)
 
 
 def split(x):
@@ -163,17 +151,15 @@
     trace = jnp.sum(jnp.sum(gram * eye, axis=1, keepdims=True), axis=0, keepdims=True)
     inv_norm = 1.0 / (jnp.sqrt(trace) + EPSILON)
     weights = gram * (inv_norm * inv_norm)
-    total = None
+    current = x_ref[...].astype(F32) * inv_norm
     for sweep in range(ITERS):
         parts = split(weights)
         poly = COEF_A * eye + COEF_B * weights + COEF_C * dot3(parts, parts)
         poly_parts = split(poly)
-        total = poly if total is None else dot3(split(total), poly_parts)
+        current = dot3(split(current), poly_parts)
         if sweep < ITERS - 1:
             weights = dot3(split(dot3(parts, poly_parts)), poly_parts)
-    high, low = split(total * (inv_norm * math.sqrt(D)))
-    x = x_ref[...]
-    update = (dot(x, high) + dot(x, low)).astype(BF16)
+    update = (current * math.sqrt(D)).astype(BF16)
     out_ref[...] = jnp.zeros_like(out_ref)
     for core in range(CORES):
         out_ref[core, owner_ref[0]] = update[core * ROWS : (core + 1) * ROWS, :]
@@ -192,13 +178,13 @@
 
 
 def body(acts, grads, tile_expert, momentum, packing):
-    z, core, group = lax.axis_index("z"), lax.axis_index("core"), lax.axis_index("expert")
-    n_z, n_owner = lax.axis_size("z"), lax.axis_size("expert")
-    where = jnp.concatenate([jnp.stack([z, core]), tile_expert[:, 0, 0]]).astype(jnp.int32)
+    near_at, core, group = (lax.axis_index(name) for name in ("near", "core", "expert"))
+    n_owner = lax.axis_size("expert")
+    where = jnp.concatenate([jnp.stack([near_at, core]), tile_expert[:, 0, 0]]).astype(jnp.int32)
     flat_acts, flat_grads = acts[:, 0, :], grads[:, 0, :]
 
     def go(value, step):
-        return lax.ppermute(value, "z", ring(n_z, step))
+        return lax.ppermute(value, ("far", "near"), ring(FAR * NEAR, step))
 
     def swap(value):
         return lax.ppermute(value, "core", ring(CORES, 1))
@@ -221,15 +207,15 @@
         add_kernel, [whole, whole, half, half, whole], mine, other, scalars=0
     )
     chunk = shape((PAIR, FF))
-    keep, up1, up2, down1 = call(
+    near = call(
         near_kernel,
-        [shape((PAIR, FF), F32), chunk, chunk, chunk],
-        where,
+        shape((FAR, PAIR, FF)),
         own,
         go(up1, 1),
         go(down1, -1),
         go(up2, 2),
         go(down2, -2),
+        scalars=0,
     )
     kept = lax.dynamic_index_in_dim(momentum, core, 1, keepdims=False)
     lent = swap(lax.dynamic_index_in_dim(momentum, 1 - core, 1, keepdims=False))
@@ -239,19 +225,20 @@
         momentum_kernel,
         [chunk, rows, rows, shape((packed_rows, LANE))],
         where,
-        keep,
-        go(up1, NEAR),
-        go(up2, 2 * NEAR),
-        go(down1, -NEAR),
+        lax.all_to_all(near, "far", 0, 0),
         kept,
         lent,
         flops=2 * PAIR * FF * FF,
     )
-    packed = packed.reshape(n_z, packed_rows // n_z, LANE)
-    pieces = call(
-        piece_kernel, shape(packed.shape, F32), lax.all_to_all(packed, "z", 0, 0), scalars=0
-    )
-    gram = lax.all_to_all(pieces, "z", 0, 0).reshape(packed_rows, LANE)
+    packed = packed.reshape(NEAR, packed_rows // NEAR, LANE)
+    near_sum = call(spread_sum_kernel, shape(packed.shape), lax.all_to_all(packed, "near", 0, 0), scalars=0)
+    far_sum = call(
+        spread_sum_kernel,
+        shape(packed.shape, F32),
+        lax.all_to_all(near_sum, "far", 0, 0),
+        scalars=0,
+    )
+    gram = lax.all_to_all(far_sum, "near", 0, 0).reshape(packed_rows, LANE)
 
     new_other = swap(new_give)
     new_momentum = jnp.stack(
@@ -290,10 +277,10 @@
 
 
 def solution(mesh):
-    n_dp, n_owner = mesh.devices.shape
-    devices = np.asarray(mesh.devices).reshape(n_dp // CORES, CORES, n_owner)
-    finer = Mesh(devices, ("z", "core", "expert"))
-    spec = P(("z", "core"), "expert", None)
+    n_owner = mesh.devices.shape[1]
+    devices = np.asarray(mesh.devices).reshape(FAR, NEAR, CORES, n_owner)
+    finer = Mesh(devices, ("far", "near", "core", "expert"))
+    spec = P(("far", "near", "core"), "expert", None)
     return jax.shard_map(
         body, mesh=finer, in_specs=(spec,) * 4 + (P(),), out_specs=(spec, spec), check_vma=False
     )

time: 171 us -> 161 us (0.942)
  starting transfers between devices: 70.2 us -> 55 us
  blocking collectives: 20.8 us -> 30.5 us
  waiting for transfers between devices: 56.1 us -> 52.7 us
    ppermute x7 -> x4, starting transfers between devices: 33.5 us -> 15.2 us  [go(): return lax.ppermute(value, ('far', 'near'), ring(FAR * NEAR, step))]
    ppermute x7 -> x4, waiting for transfers between devices: 18.9 us -> 9.13 us  [go(): return lax.ppermute(value, ('far', 'near'), ring(FAR * NEAR, step))]
    all_to_all x1 -> x2, blocking collectives: 20.8 us -> 30.5 us  [the longest x1 17.4 us: body(): lax.all_to_all(near_sum, 'far', 0, 0)]
    all_to_all x1 -> x2, waiting for transfers between devices: 17.4 us -> 22.8 us  [the longest x1 15.7 us: body(): lax.all_to_all(near, 'far', 0, 0)]
    all_to_all x1 -> x2, starting transfers between devices: 8.8 us -> 13.1 us  [the longest x1 8.64 us: body(): lax.all_to_all(near, 'far', 0, 0)]
    pallas_call x8 -> x9, Pallas kernels: 16.9 us -> 16.3 us  [call(): pl.pallas_call(kernel, out_shape=outs, in_specs=[SMEM] * scalars + [VMEM]...]
  transfers between devices with their start and end apart: 12 -> 10, of which waited for: 8 -> 8; matrix products, arithmetic and copies ran while one was open for 1% -> 1% of each run, Pallas kernels for 2% -> 1%
where the time goes in v3:
time: 161 us
  starting transfers between devices  55 us (34%)
  waiting for transfers between devices  52.7 us (33%)
  blocking collectives  30.5 us (19%)
  Pallas kernels  16.3 us (10%)
  local copies, waits for them, and re-layouts  4.2 us (3%)
    all_to_all x1, waiting for transfers between devices, body(): lax.all_to_all(sent.reshape(CORES * n_owner, ROWS, FF), ('core', 'expert'...  17.9 us
    all_to_all x1, blocking collectives, body(): lax.all_to_all(near_sum, 'far', 0, 0)  17.4 us
    pallas_call x9, Pallas kernels, call(): pl.pallas_call(kernel, out_shape=outs, in_specs=[SMEM] * scalars + [VMEM]...  16.3 us
    all_to_all x1, waiting for transfers between devices, body(): lax.all_to_all(near, 'far', 0, 0)  15.7 us
    ppermute x4, starting transfers between devices, go(): return lax.ppermute(value, ('far', 'near'), ring(FAR * NEAR, step))  15.2 us
    ppermute x3, starting transfers between devices, swap(): return lax.ppermute(value, 'core', ring(CORES, 1))  14.6 us
    all_to_all x1, blocking collectives, body(): lax.all_to_all(packed, 'near', 0, 0)  13.1 us
    all_to_all x1, starting transfers between devices, body(): lax.all_to_all(sent.reshape(CORES * n_owner, ROWS, FF), ('core', 'expert'...  12.2 us
  transfers between devices with their start and end apart: 10, of which 8 were waited for; matrix products, arithmetic and copies ran while one was open for 1% of the time, Pallas kernels for 1%

profile of v3, /device:TPU:1, one launch (start us, length us, event | category | flops | bytes accessed | tf_op | source)
XLA Modules:
  0.0 160.6 jit_solution(705112686563853922)
XLA Ops:
  0.6 0.7 pad_add_fusion.where_ref
  1.4 1.6 copy-done
  3.0 1.0 copy-done.1
  4.0 1.9 %shard_map.69 = bf16[4,4,128,384]{3,2,1,0:T(8,128)(2,1)S(1)} custom-call(s32[4]{0:T(128)S(1)} %pad_add_fusion.where_ref, bf16[512,2048]{1,0:T(8,128)(2,1)S(1)} %bitcast.21, bf16[512,384]{1,0:T(8,128)(2,1)S(1)} %bitcast.23), custom_call_target="tpu_custom_call" | custom-call | flops 805306368 | bytes 2490384 | tf_op jit(solution)/shard_map/pallas_call | solution.py:41
  5.9 8.8 %collective-permute-start = (bf16[4,4,128,384]{3,2,1,0:T(8,128)(2,1)S(1)}, bf16[4,4,128,384]{3,2,1,0:T(8,128)(2,1)S(1)}, u32[]{:S(2)}, u32[]{:S(2)}) collective-permute-start(bf16[4,4,128,384]{3,2,1,0:T(8,128)(2,1)S(1)} %shard_map.69), channel_id=1, source_target_pairs={{0,16},{16,0},{1,17},{17,1},{2,18},{18,2},{3,19},{19,3},{4,20},{20... | collective-permute-start | bytes 4718600 | tf_op jit(solution)/shard_map/ppermute | solution.py:190
  14.7 1.9 %shard_map.68.mine_ref = bf16[4,4,128,384]{3,2,1,0:T(8,128)(2,1)S(1)} custom-call(s32[4]{0:T(128)S(1)} %pad_add_fusion.where_ref, bf16[512,2048]{1,0:T(8,128)(2,1)S(1)} %bitcast.22, bf16[512,384]{1,0:T(8,128)(2,1)S(1)} %bitcast.24), custom_call_target="tpu_custom_call" | custom-call | flops 805306368 | bytes 2490384 | tf_op jit(solution)/shard_map/pallas_call | solution.py:41
  16.6 1.1 collective-permute-done.other_ref
  18.1 2.1 %collective-permute-start.1 = (bf16[4,128,384]{2,1,0:T(8,128)(2,1)S(1)}, bf16[4,128,384]{2,1,0:T(8,128)(2,1)S(1)}, u32[]{:S(2)}, u32[]{:S(2)}) collective-permute-start(bf16[4,128,384]{2,1,0:T(8,128)(2,1)S(1)} %get-tuple-element.12), channel_id=1, source_target_pairs={{0,32},{32,64},{64,96},{96,128},{128,160},{160,192},{192,224},{224... | collective-permute-start | bytes 1179656 | tf_op jit(solution)/shard_map/ppermute | solution.py:187
  20.1 5.7 %collective-permute-start.2 = (bf16[4,128,384]{2,1,0:T(8,128)(2,1)S(1)}, bf16[4,128,384]{2,1,0:T(8,128)(2,1)S(1)}, u32[]{:S(2)}, u32[]{:S(2)}) collective-permute-start(bf16[4,128,384]{2,1,0:T(8,128)(2,1)S(1)} %get-tuple-element.13), channel_id=1, source_target_pairs={{0,480},{32,0},{64,32},{96,64},{128,96},{160,128},{192,160},{224,1... | collective-permute-start | bytes 1179656 | tf_op jit(solution)/shard_map/ppermute | solution.py:187
  25.9 1.9 %collective-permute-start.3 = (bf16[2,128,384]{2,1,0:T(8,128)(2,1)S(1)}, bf16[2,128,384]{2,1,0:T(8,128)(2,1)S(1)}, u32[]{:S(2)}, u32[]{:S(2)}) collective-permute-start(bf16[2,128,384]{2,1,0:T(8,128)(2,1)S(1)} %get-tuple-element.14), channel_id=1, source_target_pairs={{0,64},{32,96},{64,128},{96,160},{128,192},{160,224},{192,256},{22... | collective-permute-start | bytes 589832 | tf_op jit(solution)/shard_map/ppermute | solution.py:187
  27.8 5.5 %collective-permute-start.4 = (bf16[2,128,384]{2,1,0:T(8,128)(2,1)S(1)}, bf16[2,128,384]{2,1,0:T(8,128)(2,1)S(1)}, u32[]{:S(2)}, u32[]{:S(2)}) collective-permute-start(bf16[2,128,384]{2,1,0:T(8,128)(2,1)S(1)} %get-tuple-element.15), channel_id=1, source_target_pairs={{0,448},{32,480},{64,0},{96,32},{128,64},{160,96},{192,128},{224,1... | collective-permute-start | bytes 589832 | tf_op jit(solution)/shard_map/ppermute | solution.py:187
  33.3 6.5 %collective-permute-done.3.c_ref = bf16[2,128,384]{2,1,0:T(8,128)(2,1)S(1)} collective-permute-done((bf16[2,128,384]{2,1,0:T(8,128)(2,1)S(1)}, bf16[2,128,384]{2,1,0:T(8,128)(2,1)S(1)}, u32[]{:S(2)}, u32[]{:S(2)}) %collective-permute-start.3) | collective-permute-done | bytes 196640 | tf_op jit(solution)/shard_map/ppermute | solution.py:187
  39.7 2.7 %collective-permute-done.4.d_ref = bf16[2,128,384]{2,1,0:T(8,128)(2,1)S(1)} collective-permute-done((bf16[2,128,384]{2,1,0:T(8,128)(2,1)S(1)}, bf16[2,128,384]{2,1,0:T(8,128)(2,1)S(1)}, u32[]{:S(2)}, u32[]{:S(2)}) %collective-permute-start.4) | collective-permute-done | bytes 196640 | tf_op jit(solution)/shard_map/ppermute | solution.py:187
  42.4 1.0 shard_map.71
  43.4 8.6 %all-to-all-start = ((bf16[4,128,384]{2,1,0:T(8,128)(2,1)}), bf16[4,128,384]{2,1,0:T(8,128)(2,1)S(1)}, u32[]{:S(2)}, u32[]{:S(2)}) async-start(bf16[4,128,384]{2,1,0:T(8,128)(2,1)} %shard_map.71), calls=%async_computation | async-start | bytes 786432 | tf_op jit(solution)/shard_map/all_to_all | solution.py:228
  52.2 3.7 %collective-permute-start.5 = (f32[64,384]{1,0:T(8,128)S(1)}, f32[64,384]{1,0:T(8,128)S(1)}, u32[]{:S(2)}, u32[]{:S(2)}) collective-permute-start(f32[64,384]{1,0:T(8,128)S(1)} %bitcast.28), channel_id=1, source_target_pairs={{0,16},{16,0},{1,17},{17,1},{2,18},{18,2},{3,19},{19,3},{4,20},{20... | collective-permute-start | bytes 294920 | tf_op jit(solution)/shard_map/ppermute | solution.py:190
  56.0 0.9 collective-permute-done.5.lent_ref
  56.9 15.7 %all-to-all-done.parts_ref = bf16[4,128,384]{2,1,0:T(8,128)(2,1)S(1)} async-done(((bf16[4,128,384]{2,1,0:T(8,128)(2,1)}), bf16[4,128,384]{2,1,0:T(8,128)(2,1)S(1)}, u32[]{:S(2)}, u32[]{:S(2)}) %all-to-all-start) | async-done | bytes 393248 | tf_op jit(solution)/shard_map/all_to_all | solution.py:228
  72.5 0.9 shard_map.72
  73.4 13.1 %all_to_all.25.parts_ref = bf16[4,192,128]{2,1,0:T(8,128)(2,1)S(1)} all-to-all(bf16[4,192,128]{2,1,0:T(8,128)(2,1)S(1)} %bitcast.27), channel_id=1, replica_groups=mesh['far'=4,'near'=4,'core'=2,'expert'=16] {'near'}, dimensions={0} | all-to-all | bytes 393216 | tf_op jit(solution)/shard_map/all_to_all | solution.py:234
  86.6 17.4 %all_to_all.26.parts_ref = bf16[4,192,128]{2,1,0:T(8,128)(2,1)S(1)} all-to-all(bf16[4,192,128]{2,1,0:T(8,128)(2,1)S(1)} %shard_map.73), channel_id=1, replica_groups=mesh['far'=4,'near'=4,'core'=2,'expert'=16] {'far'}, dimensions={0} | all-to-all | bytes 393216 | tf_op jit(solution)/shard_map/all_to_all | solution.py:238
  103.9 0.8 shard_map.74
  104.7 4.4 %all-to-all-start.3 = ((f32[4,192,128]{2,1,0:T(8,128)}), f32[4,192,128]{2,1,0:T(8,128)S(1)}, u32[]{:S(2)}, u32[]{:S(2)}) async-start(f32[4,192,128]{2,1,0:T(8,128)} %shard_map.74), calls=%async_computation.3 | async-start | bytes 786432 | tf_op jit(solution)/shard_map/all_to_all | solution.py:241
  109.1 0.6 constant_dynamic-slice_fusion
  109.7 7.2 %all-to-all-done.3 = f32[4,192,128]{2,1,0:T(8,128)S(1)} async-done(((f32[4,192,128]{2,1,0:T(8,128)}), f32[4,192,128]{2,1,0:T(8,128)S(1)}, u32[]{:S(2)}, u32[]{:S(2)}) %all-to-all-start.3) | async-done | bytes 393248 | tf_op jit(solution)/shard_map/all_to_all | solution.py:241
  116.9 8.0 %shard_map.75 = bf16[2,16,64,384]{3,2,1,0:T(8,128)(2,1)} custom-call(s32[1]{0:T(128)} %bitcast.10.owner_ref, f32[768,128]{1,0:T(8,128)S(1)} %bitcast.25, bf16[128,384]{1,0:T(8,128)(2,1)S(1)} %get-tuple-element.19.x_ref), custom_call_target="tpu_custom_call" | custom-call | flops 3057647616 | bytes 491524 | tf_op jit(solution)/shard_map/pallas_call | solution.py:41
  124.9 12.2 %all-to-all-start.4 = ((bf16[32,64,384]{2,1,0:T(8,128)(2,1)}), bf16[32,64,384]{2,1,0:T(8,128)(2,1)S(1)}, u32[]{:S(2)}, u32[]{:S(2)}) async-start(bf16[32,64,384]{2,1,0:T(8,128)(2,1)} %bitcast.13), calls=%async_computation.4 | async-start | bytes 3145728 | tf_op jit(solution)/shard_map/all_to_all | solution.py:266
  137.3 2.1 %collective-permute-start.6 = (f32[64,384]{1,0:T(8,128)S(1)}, f32[64,384]{1,0:T(8,128)S(1)}, u32[]{:S(2)}, u32[]{:S(2)}) collective-permute-start(f32[64,384]{1,0:T(8,128)S(1)} %get-tuple-element.17), channel_id=1, source_target_pairs={{0,16},{16,0},{1,17},{17,1},{2,18},{18,2},{3,19},{19,3},{4,20},{20... | collective-permute-start | bytes 294920 | tf_op jit(solution)/shard_map/ppermute | solution.py:190
  139.6 0.9 collective-permute-done.6
  140.5 0.8 copy.13
  141.4 17.9 %all-to-all-done.4.got_ref = bf16[32,64,384]{2,1,0:T(8,128)(2,1)S(1)} async-done(((bf16[32,64,384]{2,1,0:T(8,128)(2,1)}), bf16[32,64,384]{2,1,0:T(8,128)(2,1)S(1)}, u32[]{:S(2)}, u32[]{:S(2)}) %all-to-all-start.4) | async-done | bytes 1572896 | tf_op jit(solution)/shard_map/all_to_all | solution.py:266
  159.2 1.4 shard_map.76
  (19 shorter events, 1.0 us)
Async XLA Ops:
  1.4 1.6 copy-start
  3.0 1.0 copy-start.1
  5.9 11.8 %collective-permute-start = (bf16[4,4,128,384]{3,2,1,0:T(8,128)(2,1)S(1)}, bf16[4,4,128,384]{3,2,1,0:T(8,128)(2,1)S(1)}, u32[]{:S(2)}, u32[]{:S(2)}) collective-permute-start(bf16[4,4,128,384]{3,2,1,0:T(8,128)(2,1)S(1)} %shard_map.69), channel_id=1, source_target_pairs={{0,16},{16,0},{1,17},{17,1},{2,18},{18,2},{3,19},{19,3},{4,20},{20... | collective-permute-start | bytes 4718600 | tf_op jit(solution)/shard_map/ppermute | solution.py:190
  18.1 34.0 %copy-start.2 = (f32[64,2,384]{2,1,0:T(2,128)S(1)}, f32[64,2,384]{2,1,0:T(2,128)}, u32[]{:S(2)}) copy-start(f32[64,2,384]{2,1,0:T(2,128)} %param.8) | copy-start | bytes 589828
  18.1 24.3 %collective-permute-start.1 = (bf16[4,128,384]{2,1,0:T(8,128)(2,1)S(1)}, bf16[4,128,384]{2,1,0:T(8,128)(2,1)S(1)}, u32[]{:S(2)}, u32[]{:S(2)}) collective-permute-start(bf16[4,128,384]{2,1,0:T(8,128)(2,1)S(1)} %get-tuple-element.12), channel_id=1, source_target_pairs={{0,32},{32,64},{64,96},{96,128},{128,160},{160,192},{192,224},{224... | collective-permute-start | bytes 1179656 | tf_op jit(solution)/shard_map/ppermute | solution.py:187
  20.1 22.3 %collective-permute-start.2 = (bf16[4,128,384]{2,1,0:T(8,128)(2,1)S(1)}, bf16[4,128,384]{2,1,0:T(8,128)(2,1)S(1)}, u32[]{:S(2)}, u32[]{:S(2)}) collective-permute-start(bf16[4,128,384]{2,1,0:T(8,128)(2,1)S(1)} %get-tuple-element.13), channel_id=1, source_target_pairs={{0,480},{32,0},{64,32},{96,64},{128,96},{160,128},{192,160},{224,1... | collective-permute-start | bytes 1179656 | tf_op jit(solution)/shard_map/ppermute | solution.py:187
  25.9 13.9 %collective-permute-start.3 = (bf16[2,128,384]{2,1,0:T(8,128)(2,1)S(1)}, bf16[2,128,384]{2,1,0:T(8,128)(2,1)S(1)}, u32[]{:S(2)}, u32[]{:S(2)}) collective-permute-start(bf16[2,128,384]{2,1,0:T(8,128)(2,1)S(1)} %get-tuple-element.14), channel_id=1, source_target_pairs={{0,64},{32,96},{64,128},{96,160},{128,192},{160,224},{192,256},{22... | collective-permute-start | bytes 589832 | tf_op jit(solution)/shard_map/ppermute | solution.py:187
  27.8 14.6 %collective-permute-start.4 = (bf16[2,128,384]{2,1,0:T(8,128)(2,1)S(1)}, bf16[2,128,384]{2,1,0:T(8,128)(2,1)S(1)}, u32[]{:S(2)}, u32[]{:S(2)}) collective-permute-start(bf16[2,128,384]{2,1,0:T(8,128)(2,1)S(1)} %get-tuple-element.15), channel_id=1, source_target_pairs={{0,448},{32,480},{64,0},{96,32},{128,64},{160,96},{192,128},{224,1... | collective-permute-start | bytes 589832 | tf_op jit(solution)/shard_map/ppermute | solution.py:187
  43.4 29.1 %all-to-all-start = ((bf16[4,128,384]{2,1,0:T(8,128)(2,1)}), bf16[4,128,384]{2,1,0:T(8,128)(2,1)S(1)}, u32[]{:S(2)}, u32[]{:S(2)}) async-start(bf16[4,128,384]{2,1,0:T(8,128)(2,1)} %shard_map.71), calls=%async_computation | async-start | bytes 786432 | tf_op jit(solution)/shard_map/all_to_all | solution.py:228
  52.2 4.6 %collective-permute-start.5 = (f32[64,384]{1,0:T(8,128)S(1)}, f32[64,384]{1,0:T(8,128)S(1)}, u32[]{:S(2)}, u32[]{:S(2)}) collective-permute-start(f32[64,384]{1,0:T(8,128)S(1)} %bitcast.28), channel_id=1, source_target_pairs={{0,16},{16,0},{1,17},{17,1},{2,18},{18,2},{3,19},{19,3},{4,20},{20... | collective-permute-start | bytes 294920 | tf_op jit(solution)/shard_map/ppermute | solution.py:190
  72.5 36.6 %copy-start.3 = (s32[32,1]{0,1:T(1,128)S(1)}, s32[32,1]{0,1:T(1,128)}, u32[]{:S(2)}) copy-start(s32[32,1]{0,1:T(1,128)} %param.9) | copy-start | bytes 388
  104.7 12.1 %all-to-all-start.3 = ((f32[4,192,128]{2,1,0:T(8,128)}), f32[4,192,128]{2,1,0:T(8,128)S(1)}, u32[]{:S(2)}, u32[]{:S(2)}) async-start(f32[4,192,128]{2,1,0:T(8,128)} %shard_map.74), calls=%async_computation.3 | async-start | bytes 786432 | tf_op jit(solution)/shard_map/all_to_all | solution.py:241
  124.9 34.3 %all-to-all-start.4 = ((bf16[32,64,384]{2,1,0:T(8,128)(2,1)}), bf16[32,64,384]{2,1,0:T(8,128)(2,1)S(1)}, u32[]{:S(2)}, u32[]{:S(2)}) async-start(bf16[32,64,384]{2,1,0:T(8,128)(2,1)} %bitcast.13), calls=%async_computation.4 | async-start | bytes 3145728 | tf_op jit(solution)/shard_map/all_to_all | solution.py:266
  137.3 3.2 %collective-permute-start.6 = (f32[64,384]{1,0:T(8,128)S(1)}, f32[64,384]{1,0:T(8,128)S(1)}, u32[]{:S(2)}, u32[]{:S(2)}) collective-permute-start(f32[64,384]{1,0:T(8,128)S(1)} %get-tuple-element.17), channel_id=1, source_target_pairs={{0,16},{16,0},{1,17},{17,1},{2,18},{18,2},{3,19},{19,3},{4,20},{20... | collective-permute-start | bytes 294920 | tf_op jit(solution)/shard_map/ppermute | solution.py:190

commit v4 on v3

--- a/solution.py
+++ b/solution.py
@@ -35,7 +35,7 @@
 F32 = jnp.float32
 
 
-def call(kernel, outs, *args, scalars=1, scratch=(), flops=0):
+def call(kernel, args, outs, scalars=0, scratch=(), flops=0):
     many = isinstance(outs, list)
     nbytes = sum(a.size * a.dtype.itemsize for a in args)
     return pl.pallas_call(
@@ -57,19 +57,25 @@
     return lax.dot_general(x, y, (((0,), (0,)), ((), ())), preferred_element_type=F32)
 
 
-def partial_kernel(theirs, where_ref, acts_ref, grads_ref, out_ref, masked_ref):
-    near_at, core = where_ref[0], where_ref[1]
-    expert = 1 - core if theirs else core
-    for tile in range(acts_ref.shape[0] // TILE):
+def masked_grads(expert, ids_ref, grads_ref, masked_ref):
+    for tile in range(grads_ref.shape[0] // TILE):
         rows = slice(tile * TILE, (tile + 1) * TILE)
-        factor = jnp.where(where_ref[2 + tile] == expert, 1.0, 0.0).astype(F32)
+        factor = jnp.where(ids_ref[tile] == expert, 1.0, 0.0).astype(F32)
         masked_ref[rows, :] = (grads_ref[rows, :].astype(F32) * factor).astype(BF16)
-    masked = masked_ref[...]
+    return masked_ref[...]
+
+
+def chunk_rows(q, rel):
+    at = lax.rem(lax.axis_index("near") + rel, NEAR)
+    return pl.ds(pl.multiple_of((q * NEAR + at) * PAIR, PAIR), PAIR)
+
+
+def partial_kernel(theirs, ids_ref, acts_ref, grads_ref, out_ref, masked_ref):
+    core = lax.axis_index("core")
+    masked = masked_grads(1 - core if theirs else core, ids_ref, grads_ref, masked_ref)
     for rel in range(NEAR):
-        cls = lax.rem(near_at + rel, NEAR)
         for q in range(FAR):
-            start = pl.multiple_of((q * NEAR + cls) * PAIR, PAIR)
-            block = transposed_dot(acts_ref[:, pl.ds(start, PAIR)], masked)
+            block = transposed_dot(acts_ref[:, chunk_rows(q, rel)], masked)
             out_ref[rel, q] = block.astype(BF16)
 
 
@@ -85,7 +91,7 @@
     down1_ref[...] = total(3, slice(None))
 
 
-def near_kernel(own_ref, a_ref, b_ref, c_ref, d_ref, out_ref):
+def near_kernel(own_ref, c_ref, d_ref, a_ref, b_ref, out_ref):
     half = FAR // 2
     for q in range(FAR):
         last = c_ref[q] if q < half else d_ref[q - half]
@@ -94,9 +100,9 @@
 
 
 def momentum_kernel(
-    where_ref, parts_ref, kept_ref, lent_ref, ns_ref, mine_ref, give_ref, gram_ref
+    parts_ref, kept_ref, lent_ref, ns_ref, mine_ref, give_ref, gram_ref
 ):
-    core = where_ref[1]
+    core = lax.axis_index("core")
     for who, old_ref, new_ref in ((core, kept_ref, mine_ref), (1 - core, lent_ref, give_ref)):
         rows = pl.ds(pl.multiple_of(who * ROWS, ROWS), ROWS)
         grad = parts_ref[0, rows, :].astype(F32)
@@ -132,7 +138,7 @@
 
 def dot3(x, y):
     (xh, xl), (yh, yl) = x, y
-    return dot(xh, yh) + (dot(xh, yl) + dot(xl, yh))
+    return dot(jnp.concatenate([xh, xl, xh], axis=1), jnp.concatenate([yh, yh, yl], axis=0))
 
 
 def newton_schulz_kernel(owner_ref, gram_ref, x_ref, out_ref):
@@ -162,14 +168,25 @@
     update = (current * math.sqrt(D)).astype(BF16)
     out_ref[...] = jnp.zeros_like(out_ref)
     for core in range(CORES):
-        out_ref[core, owner_ref[0]] = update[core * ROWS : (core + 1) * ROWS, :]
+        out_ref[core, lax.rem(owner_ref[0], out_ref.shape[1])] = update[core * ROWS : (core + 1) * ROWS, :]
+
+
+def place_kernel(source_ref, got_ref, out_ref):
+    out_ref[...] = jnp.zeros_like(out_ref)
+    for owner in range(out_ref.shape[0]):
+        for slot in range(MOST):
+            source = source_ref[owner * MOST + slot]
+
+            @pl.when(source >= 0)
+            def _():
+                out_ref[owner, slot] = got_ref[source]
 
 
 def stack_kernel(source_ref, got_ref, out_ref, wide_ref):
     for slot in range(MOST):
         source = source_ref[slot]
         filled = jnp.where(source >= 0, 1.0, 0.0).astype(F32)
-        wide_ref[:, slot, :] = got_ref[jnp.maximum(source, 0)].astype(F32) * filled
+        wide_ref[:, slot, :] = got_ref[jnp.maximum(source, 0), slot].astype(F32) * filled
     out_ref[...] = wide_ref[...].astype(BF16)
 
 
@@ -178,9 +195,8 @@
 
 
 def body(acts, grads, tile_expert, momentum, packing):
-    near_at, core, group = (lax.axis_index(name) for name in ("near", "core", "expert"))
-    n_owner = lax.axis_size("expert")
-    where = jnp.concatenate([jnp.stack([near_at, core]), tile_expert[:, 0, 0]]).astype(jnp.int32)
+    core, x, y = (lax.axis_index(name) for name in ("core", "x", "y"))
+    n_x, n_y = lax.axis_size("x"), lax.axis_size("y")
     flat_acts, flat_grads = acts[:, 0, :], grads[:, 0, :]
 
     def go(value, step):
@@ -192,10 +208,9 @@
     def partial_of(theirs):
         return call(
             functools.partial(partial_kernel, theirs),
+            (tile_expert[:, 0, 0], flat_acts, flat_grads),
             shape((NEAR, FAR, PAIR, FF)),
-            where,
-            flat_acts,
-            flat_grads,
+            scalars=1,
             scratch=[pltpu.VMEM(flat_grads.shape, BF16)],
             flops=2 * flat_acts.size * FF,
         )
@@ -204,40 +219,26 @@
     mine = partial_of(False)
     whole, half = shape((FAR, PAIR, FF)), shape((FAR // 2, PAIR, FF))
     own, up1, up2, down2, down1 = call(
-        add_kernel, [whole, whole, half, half, whole], mine, other, scalars=0
+        add_kernel, (mine, other), [whole, whole, half, half, whole]
     )
     chunk = shape((PAIR, FF))
-    near = call(
-        near_kernel,
-        shape((FAR, PAIR, FF)),
-        own,
-        go(up1, 1),
-        go(down1, -1),
-        go(up2, 2),
-        go(down2, -2),
-        scalars=0,
-    )
+    arrived = (go(up2, 2), go(down2, -2), go(up1, 1), go(down1, -1))
+    near = call(near_kernel, (own, *arrived), shape((FAR, PAIR, FF)))
     kept = lax.dynamic_index_in_dim(momentum, core, 1, keepdims=False)
     lent = swap(lax.dynamic_index_in_dim(momentum, 1 - core, 1, keepdims=False))
     rows = shape((ROWS, FF), F32)
     packed_rows = len(BLOCKS) * LANE
     ns_input, new_mine, new_give, packed = call(
         momentum_kernel,
+        (lax.all_to_all(near, "far", 0, 0), kept, lent),
         [chunk, rows, rows, shape((packed_rows, LANE))],
-        where,
-        lax.all_to_all(near, "far", 0, 0),
-        kept,
-        lent,
         flops=2 * PAIR * FF * FF,
     )
     packed = packed.reshape(NEAR, packed_rows // NEAR, LANE)
-    near_sum = call(spread_sum_kernel, shape(packed.shape), lax.all_to_all(packed, "near", 0, 0), scalars=0)
-    far_sum = call(
-        spread_sum_kernel,
-        shape(packed.shape, F32),
-        lax.all_to_all(near_sum, "far", 0, 0),
-        scalars=0,
-    )
+    near_parts = lax.all_to_all(packed, "near", 0, 0)
+    near_sum = call(spread_sum_kernel, (near_parts,), shape(packed.shape))
+    far_parts = lax.all_to_all(near_sum, "far", 0, 0)
+    far_sum = call(spread_sum_kernel, (far_parts,), shape(packed.shape, F32))
     gram = lax.all_to_all(far_sum, "near", 0, 0).reshape(packed_rows, LANE)
 
     new_other = swap(new_give)
@@ -250,37 +251,42 @@
     positions = jnp.arange(experts, dtype=jnp.int32)
     shared = (owner_ids[:, None] == owner_ids[None, :]) & (positions[None, :] < positions[:, None])
     target = owner_ids * MOST + jnp.sum(shared.astype(jnp.int32), axis=1)
-    hits = target[None, :] == group * MOST + jnp.arange(MOST, dtype=jnp.int32)[:, None]
-    lies = positions % CORES * n_owner + positions // CORES
-    source = jnp.max(jnp.where(hits, lies[None, :], -1), axis=1)
-    my_owner = lax.dynamic_slice_in_dim(owner_ids, group * CORES + core, 1, 0)
+    of_core, of_y = positions % CORES, positions // CORES % n_y
+    of_x = positions // (CORES * n_y)
+    slots = jnp.arange(MOST, dtype=jnp.int32)
+    line = (jnp.arange(n_x, dtype=jnp.int32)[:, None] * n_y + y) * MOST + slots[None, :]
+    passes = (line.reshape(-1)[:, None] == target[None, :]) & (of_x == x)[None, :]
+    placed_from = jnp.max(jnp.where(passes, (of_core * n_y + of_y)[None, :], -1), axis=1)
+    fills = ((x * n_y + y) * MOST + slots)[:, None] == target[None, :]
+    stacked_from = jnp.max(jnp.where(fills, of_x[None, :], -1), axis=1)
+    my_owner = lax.dynamic_slice_in_dim(owner_ids, (x * n_y + y) * CORES + core, 1, 0)
 
     sent = call(
         newton_schulz_kernel,
-        shape((CORES, n_owner, ROWS, FF)),
-        my_owner,
-        gram,
-        ns_input,
+        (my_owner, gram, ns_input),
+        shape((CORES, n_y, ROWS, FF)),
+        scalars=1,
         flops=2 * 27 * FF * FF * FF,
     )
-    got = lax.all_to_all(
-        sent.reshape(CORES * n_owner, ROWS, FF), ("core", "expert"), 0, 0
-    )
+    got = lax.all_to_all(sent.reshape(CORES * n_y, ROWS, FF), ("core", "y"), 0, 0)
+    placed = call(place_kernel, (placed_from, got), shape((n_x, MOST, ROWS, FF)), scalars=1)
+    got = lax.all_to_all(placed, "x", 0, 0)
     stacked = call(
         stack_kernel,
+        (stacked_from, got),
         shape((ROWS, MOST, FF)),
-        source,
-        got,
+        scalars=1,
         scratch=[pltpu.VMEM((ROWS, MOST, FF), F32)],
     )
     return new_momentum, stacked
 
 
 def solution(mesh):
-    n_owner = mesh.devices.shape[1]
-    devices = np.asarray(mesh.devices).reshape(FAR, NEAR, CORES, n_owner)
-    finer = Mesh(devices, ("far", "near", "core", "expert"))
-    spec = P(("far", "near", "core"), "expert", None)
+    devices = np.asarray(mesh.devices)
+    side = math.isqrt(devices.shape[1])
+    devices = devices.reshape(FAR, NEAR, CORES, side, side)
+    finer = Mesh(devices, ("far", "near", "core", "x", "y"))
+    spec = P(("far", "near", "core"), ("x", "y"), None)
     return jax.shard_map(
         body, mesh=finer, in_specs=(spec,) * 4 + (P(),), out_specs=(spec, spec), check_vma=False
     )

time: 161 us -> 160 us (level)
  waiting for transfers between devices: 52.7 us -> 49.5 us
  starting transfers between devices: 55 us -> 56.8 us
    all_to_all x1 -> x2, waiting for transfers between devices: 17.9 us -> 15.1 us  [the longest x1 7.68 us: body(): lax.all_to_all(sent.reshape(CORES * n_y, ROWS, FF), ('core', 'y'), 0, 0)]
    all_to_all x1 -> x2, starting transfers between devices: 12.2 us -> 13.5 us  [the longest x1 9.52 us: body(): lax.all_to_all(sent.reshape(CORES * n_y, ROWS, FF), ('core', 'y'), 0, 0)]
    unnamed x11 -> x13, local copies, waits for them, and re-layouts: 3.44 us -> 4.09 us
    pallas_call x9 -> x10, Pallas kernels: 16.3 us -> 15.9 us  [call(): pl.pallas_call(kernel, out_shape=outs, in_specs=[SMEM] * scalars + [VMEM]...]
  transfers between devices with their start and end apart: 10 -> 11, of which waited for: 8 -> 9; matrix products, arithmetic and copies ran while one was open for 1% -> 1% of each run, Pallas kernels for 1% -> 1%
where the time goes in v4:
time: 160 us; the launch traced here: 159 us
  starting transfers between devices  56.8 us (36%)
  waiting for transfers between devices  49.5 us (31%)
  blocking collectives  30.5 us (19%)
  Pallas kernels  15.9 us (10%)
  local copies, waits for them, and re-layouts  4.93 us (3%)
    all_to_all x1, blocking collectives, body(): far_parts = lax.all_to_all(near_sum, 'far', 0, 0)  17.4 us
    pallas_call x10, Pallas kernels, call(): pl.pallas_call(kernel, out_shape=outs, in_specs=[SMEM] * scalars + [VMEM]...  15.9 us
    all_to_all x1, waiting for transfers between devices, body(): lax.all_to_all(near, 'far', 0, 0)  15.7 us
    ppermute x4, starting transfers between devices, go(): return lax.ppermute(value, ('far', 'near'), ring(FAR * NEAR, step))  15.2 us
    ppermute x3, starting transfers between devices, swap(): return lax.ppermute(value, 'core', ring(CORES, 1))  15 us
    all_to_all x1, blocking collectives, body(): near_parts = lax.all_to_all(packed, 'near', 0, 0)  13.1 us
    all_to_all x1, starting transfers between devices, body(): lax.all_to_all(sent.reshape(CORES * n_y, ROWS, FF), ('core', 'y'), 0, 0)  9.52 us
    ppermute x4, waiting for transfers between devices, go(): return lax.ppermute(value, ('far', 'near'), ring(FAR * NEAR, step))  9.13 us
  transfers between devices with their start and end apart: 11, of which 9 were waited for; matrix products, arithmetic and copies ran while one was open for 1% of the time, Pallas kernels for 1%

profile of v4, /device:TPU:1, one launch (start us, length us, event | category | flops | bytes accessed | tf_op | source)
XLA Modules:
  0.0 159.1 jit_solution(17915967572051388180)
XLA Ops:
  0.6 1.6 copy-done
  2.2 1.0 copy-done.1
  3.9 1.9 %shard_map.69 = bf16[4,4,128,384]{3,2,1,0:T(8,128)(2,1)S(1)} custom-call(s32[2]{0:T(128)S(1)} %bitcast.26, bf16[512,2048]{1,0:T(8,128)(2,1)S(1)} %bitcast.19, bf16[512,384]{1,0:T(8,128)(2,1)S(1)} %bitcast.21), custom_call_target="tpu_custom_call" | custom-call | flops 805306368 | bytes 2490376 | tf_op jit(solution)/shard_map/pallas_call | solution.py:41
  5.8 8.8 %collective-permute-start = (bf16[4,4,128,384]{3,2,1,0:T(8,128)(2,1)S(1)}, bf16[4,4,128,384]{3,2,1,0:T(8,128)(2,1)S(1)}, u32[]{:S(2)}, u32[]{:S(2)}) collective-permute-start(bf16[4,4,128,384]{3,2,1,0:T(8,128)(2,1)S(1)} %shard_map.69), channel_id=1, source_target_pairs={{0,16},{16,0},{1,17},{17,1},{2,18},{18,2},{3,19},{19,3},{4,20},{20... | collective-permute-start | bytes 4718600 | tf_op jit(solution)/shard_map/ppermute | solution.py:206
  14.6 1.9 %shard_map.68.mine_ref = bf16[4,4,128,384]{3,2,1,0:T(8,128)(2,1)S(1)} custom-call(s32[2]{0:T(128)S(1)} %bitcast.27, bf16[512,2048]{1,0:T(8,128)(2,1)S(1)} %bitcast.20, bf16[512,384]{1,0:T(8,128)(2,1)S(1)} %bitcast.22), custom_call_target="tpu_custom_call" | custom-call | flops 805306368 | bytes 2490376 | tf_op jit(solution)/shard_map/pallas_call | solution.py:41
  16.5 1.1 collective-permute-done.other_ref
  18.0 2.1 %collective-permute-start.3 = (bf16[4,128,384]{2,1,0:T(8,128)(2,1)S(1)}, bf16[4,128,384]{2,1,0:T(8,128)(2,1)S(1)}, u32[]{:S(2)}, u32[]{:S(2)}) collective-permute-start(bf16[4,128,384]{2,1,0:T(8,128)(2,1)S(1)} %get-tuple-element.14), channel_id=1, source_target_pairs={{0,32},{32,64},{64,96},{96,128},{128,160},{160,192},{192,224},{224... | collective-permute-start | bytes 1179656 | tf_op jit(solution)/shard_map/ppermute | solution.py:203
  20.1 5.7 %collective-permute-start.4 = (bf16[4,128,384]{2,1,0:T(8,128)(2,1)S(1)}, bf16[4,128,384]{2,1,0:T(8,128)(2,1)S(1)}, u32[]{:S(2)}, u32[]{:S(2)}) collective-permute-start(bf16[4,128,384]{2,1,0:T(8,128)(2,1)S(1)} %get-tuple-element.15), channel_id=1, source_target_pairs={{0,480},{32,0},{64,32},{96,64},{128,96},{160,128},{192,160},{224,1... | collective-permute-start | bytes 1179656 | tf_op jit(solution)/shard_map/ppermute | solution.py:203
  25.8 1.9 %collective-permute-start.1 = (bf16[2,128,384]{2,1,0:T(8,128)(2,1)S(1)}, bf16[2,128,384]{2,1,0:T(8,128)(2,1)S(1)}, u32[]{:S(2)}, u32[]{:S(2)}) collective-permute-start(bf16[2,128,384]{2,1,0:T(8,128)(2,1)S(1)} %get-tuple-element.12), channel_id=1, source_target_pairs={{0,64},{32,96},{64,128},{96,160},{128,192},{160,224},{192,256},{22... | collective-permute-start | bytes 589832 | tf_op jit(solution)/shard_map/ppermute | solution.py:203
  27.7 5.5 %collective-permute-start.2 = (bf16[2,128,384]{2,1,0:T(8,128)(2,1)S(1)}, bf16[2,128,384]{2,1,0:T(8,128)(2,1)S(1)}, u32[]{:S(2)}, u32[]{:S(2)}) collective-permute-start(bf16[2,128,384]{2,1,0:T(8,128)(2,1)S(1)} %get-tuple-element.13), channel_id=1, source_target_pairs={{0,448},{32,480},{64,0},{96,32},{128,64},{160,96},{192,128},{224,1... | collective-permute-start | bytes 589832 | tf_op jit(solution)/shard_map/ppermute | solution.py:203
  33.2 6.5 %collective-permute-done.1.c_ref = bf16[2,128,384]{2,1,0:T(8,128)(2,1)S(1)} collective-permute-done((bf16[2,128,384]{2,1,0:T(8,128)(2,1)S(1)}, bf16[2,128,384]{2,1,0:T(8,128)(2,1)S(1)}, u32[]{:S(2)}, u32[]{:S(2)}) %collective-permute-start.1) | collective-permute-done | bytes 196640 | tf_op jit(solution)/shard_map/ppermute | solution.py:203
  39.7 2.6 %collective-permute-done.2.d_ref = bf16[2,128,384]{2,1,0:T(8,128)(2,1)S(1)} collective-permute-done((bf16[2,128,384]{2,1,0:T(8,128)(2,1)S(1)}, bf16[2,128,384]{2,1,0:T(8,128)(2,1)S(1)}, u32[]{:S(2)}, u32[]{:S(2)}) %collective-permute-start.2) | collective-permute-done | bytes 196640 | tf_op jit(solution)/shard_map/ppermute | solution.py:203
  42.3 1.0 shard_map.71
  43.3 8.7 %all-to-all-start = ((bf16[4,128,384]{2,1,0:T(8,128)(2,1)}), bf16[4,128,384]{2,1,0:T(8,128)(2,1)S(1)}, u32[]{:S(2)}, u32[]{:S(2)}) async-start(bf16[4,128,384]{2,1,0:T(8,128)(2,1)} %shard_map.71), calls=%async_computation | async-start | bytes 786432 | tf_op jit(solution)/shard_map/all_to_all | solution.py:233
  52.1 3.7 %collective-permute-start.5 = (f32[64,384]{1,0:T(8,128)S(1)}, f32[64,384]{1,0:T(8,128)S(1)}, u32[]{:S(2)}, u32[]{:S(2)}) collective-permute-start(f32[64,384]{1,0:T(8,128)S(1)} %bitcast.28), channel_id=1, source_target_pairs={{0,16},{16,0},{1,17},{17,1},{2,18},{18,2},{3,19},{19,3},{4,20},{20... | collective-permute-start | bytes 294920 | tf_op jit(solution)/shard_map/ppermute | solution.py:206
  55.9 0.9 collective-permute-done.5.lent_ref
  56.8 15.7 %all-to-all-done.parts_ref = bf16[4,128,384]{2,1,0:T(8,128)(2,1)S(1)} async-done(((bf16[4,128,384]{2,1,0:T(8,128)(2,1)}), bf16[4,128,384]{2,1,0:T(8,128)(2,1)S(1)}, u32[]{:S(2)}, u32[]{:S(2)}) %all-to-all-start) | async-done | bytes 393248 | tf_op jit(solution)/shard_map/all_to_all | solution.py:233
  72.8 13.1 %all_to_all.30.parts_ref = bf16[4,192,128]{2,1,0:T(8,128)(2,1)S(1)} all-to-all(bf16[4,192,128]{2,1,0:T(8,128)(2,1)S(1)} %bitcast.25), channel_id=1, replica_groups=mesh['far'=4,'near'=4,'core'=2,'x'=4,'y'=4] {'near'}, dimensions={0} | all-to-all | bytes 393216 | tf_op jit(solution)/shard_map/all_to_all | solution.py:238
  86.0 17.4 %all_to_all.31.parts_ref = bf16[4,192,128]{2,1,0:T(8,128)(2,1)S(1)} all-to-all(bf16[4,192,128]{2,1,0:T(8,128)(2,1)S(1)} %shard_map.73), channel_id=1, replica_groups=mesh['far'=4,'near'=4,'core'=2,'x'=4,'y'=4] {'far'}, dimensions={0} | all-to-all | bytes 393216 | tf_op jit(solution)/shard_map/all_to_all | solution.py:240
  103.3 0.8 shard_map.74
  104.1 4.4 %all-to-all-start.3 = ((f32[4,192,128]{2,1,0:T(8,128)}), f32[4,192,128]{2,1,0:T(8,128)S(1)}, u32[]{:S(2)}, u32[]{:S(2)}) async-start(f32[4,192,128]{2,1,0:T(8,128)} %shard_map.74), calls=%async_computation.3 | async-start | bytes 786432 | tf_op jit(solution)/shard_map/all_to_all | solution.py:242
  109.4 6.9 %all-to-all-done.3 = f32[4,192,128]{2,1,0:T(8,128)S(1)} async-done(((f32[4,192,128]{2,1,0:T(8,128)}), f32[4,192,128]{2,1,0:T(8,128)S(1)}, u32[]{:S(2)}, u32[]{:S(2)}) %all-to-all-start.3) | async-done | bytes 393248 | tf_op jit(solution)/shard_map/all_to_all | solution.py:242
  116.3 6.5 %shard_map.75 = bf16[2,4,64,384]{3,2,1,0:T(8,128)(2,1)} custom-call(s32[1]{0:T(128)} %bitcast.8.owner_ref, f32[768,128]{1,0:T(8,128)S(1)} %bitcast.23, bf16[128,384]{1,0:T(8,128)(2,1)S(1)} %get-tuple-element.19.x_ref), custom_call_target="tpu_custom_call" | custom-call | flops 3057647616 | bytes 491524 | tf_op jit(solution)/shard_map/pallas_call | solution.py:41
  122.8 9.5 %all-to-all-start.4 = ((bf16[8,64,384]{2,1,0:T(8,128)(2,1)}), bf16[8,64,384]{2,1,0:T(8,128)(2,1)S(1)}, u32[]{:S(2)}, u32[]{:S(2)}) async-start(bf16[8,64,384]{2,1,0:T(8,128)(2,1)} %bitcast.11), calls=%async_computation.4 | async-start | bytes 786432 | tf_op jit(solution)/shard_map/all_to_all | solution.py:271
  132.6 7.7 %all-to-all-done.4.got_ref = bf16[8,64,384]{2,1,0:T(8,128)(2,1)S(1)} async-done(((bf16[8,64,384]{2,1,0:T(8,128)(2,1)}), bf16[8,64,384]{2,1,0:T(8,128)(2,1)S(1)}, u32[]{:S(2)}, u32[]{:S(2)}) %all-to-all-start.4) | async-done | bytes 393248 | tf_op jit(solution)/shard_map/all_to_all | solution.py:271
  140.3 1.6 %shard_map.76 = bf16[4,4,64,384]{3,2,1,0:T(8,128)(2,1)} custom-call(s32[16]{0:T(128)S(1)} %select_reduce_fusion.source_ref, bf16[8,64,384]{2,1,0:T(8,128)(2,1)S(1)} %all-to-all-done.4.got_ref), custom_call_target="tpu_custom_call" | custom-call | bytes 393280 | tf_op jit(solution)/shard_map/pallas_call | solution.py:41
  141.9 4.0 %all-to-all-start.5 = ((bf16[4,4,64,384]{3,2,1,0:T(8,128)(2,1)}), bf16[4,4,64,384]{3,2,1,0:T(8,128)(2,1)S(1)}, u32[]{:S(2)}, u32[]{:S(2)}) async-start(bf16[4,4,64,384]{3,2,1,0:T(8,128)(2,1)} %shard_map.76), calls=%async_computation.5 | async-start | bytes 1572864 | tf_op jit(solution)/shard_map/all_to_all | solution.py:273
  145.9 2.5 %collective-permute-start.6 = (f32[64,384]{1,0:T(8,128)S(1)}, f32[64,384]{1,0:T(8,128)S(1)}, u32[]{:S(2)}, u32[]{:S(2)}) collective-permute-start(f32[64,384]{1,0:T(8,128)S(1)} %get-tuple-element.17), channel_id=1, source_target_pairs={{0,16},{16,0},{1,17},{17,1},{2,18},{18,2},{3,19},{19,3},{4,20},{20... | collective-permute-start | bytes 294920 | tf_op jit(solution)/shard_map/ppermute | solution.py:206
  148.7 0.7 collective-permute-done.6
  149.5 0.8 copy.13
  150.3 7.4 %all-to-all-done.5.got_ref = bf16[4,4,64,384]{3,2,1,0:T(8,128)(2,1)S(1)} async-done(((bf16[4,4,64,384]{3,2,1,0:T(8,128)(2,1)}), bf16[4,4,64,384]{3,2,1,0:T(8,128)(2,1)S(1)}, u32[]{:S(2)}, u32[]{:S(2)}) %all-to-all-start.5) | async-done | bytes 786464 | tf_op jit(solution)/shard_map/all_to_all | solution.py:273
  157.7 1.4 shard_map.77
  (29 shorter events, 2.9 us)
Async XLA Ops:
  0.6 1.6 %copy-start = (bf16[512,1,2048]{2,0,1:T(8,128)(2,1)S(1)}, bf16[512,1,2048]{2,0,1:T(8,128)(2,1)}, u32[]{:S(2)}) copy-start(bf16[512,1,2048]{2,0,1:T(8,128)(2,1)} %param.5) | copy-start | bytes 6291460
  2.2 1.0 copy-start.1
  3.2 0.7 copy-start.2
  5.8 11.8 %collective-permute-start = (bf16[4,4,128,384]{3,2,1,0:T(8,128)(2,1)S(1)}, bf16[4,4,128,384]{3,2,1,0:T(8,128)(2,1)S(1)}, u32[]{:S(2)}, u32[]{:S(2)}) collective-permute-start(bf16[4,4,128,384]{3,2,1,0:T(8,128)(2,1)S(1)} %shard_map.69), channel_id=1, source_target_pairs={{0,16},{16,0},{1,17},{17,1},{2,18},{18,2},{3,19},{19,3},{4,20},{20... | collective-permute-start | bytes 4718600 | tf_op jit(solution)/shard_map/ppermute | solution.py:206
  18.0 34.0 %copy-start.3 = (f32[64,2,384]{2,1,0:T(2,128)S(1)}, f32[64,2,384]{2,1,0:T(2,128)}, u32[]{:S(2)}) copy-start(f32[64,2,384]{2,1,0:T(2,128)} %param.8) | copy-start | bytes 589828
  18.0 24.3 %collective-permute-start.3 = (bf16[4,128,384]{2,1,0:T(8,128)(2,1)S(1)}, bf16[4,128,384]{2,1,0:T(8,128)(2,1)S(1)}, u32[]{:S(2)}, u32[]{:S(2)}) collective-permute-start(bf16[4,128,384]{2,1,0:T(8,128)(2,1)S(1)} %get-tuple-element.14), channel_id=1, source_target_pairs={{0,32},{32,64},{64,96},{96,128},{128,160},{160,192},{192,224},{224... | collective-permute-start | bytes 1179656 | tf_op jit(solution)/shard_map/ppermute | solution.py:203
  20.1 22.3 %collective-permute-start.4 = (bf16[4,128,384]{2,1,0:T(8,128)(2,1)S(1)}, bf16[4,128,384]{2,1,0:T(8,128)(2,1)S(1)}, u32[]{:S(2)}, u32[]{:S(2)}) collective-permute-start(bf16[4,128,384]{2,1,0:T(8,128)(2,1)S(1)} %get-tuple-element.15), channel_id=1, source_target_pairs={{0,480},{32,0},{64,32},{96,64},{128,96},{160,128},{192,160},{224,1... | collective-permute-start | bytes 1179656 | tf_op jit(solution)/shard_map/ppermute | solution.py:203
  25.8 13.9 %collective-permute-start.1 = (bf16[2,128,384]{2,1,0:T(8,128)(2,1)S(1)}, bf16[2,128,384]{2,1,0:T(8,128)(2,1)S(1)}, u32[]{:S(2)}, u32[]{:S(2)}) collective-permute-start(bf16[2,128,384]{2,1,0:T(8,128)(2,1)S(1)} %get-tuple-element.12), channel_id=1, source_target_pairs={{0,64},{32,96},{64,128},{96,160},{128,192},{160,224},{192,256},{22... | collective-permute-start | bytes 589832 | tf_op jit(solution)/shard_map/ppermute | solution.py:203
  27.7 14.6 %collective-permute-start.2 = (bf16[2,128,384]{2,1,0:T(8,128)(2,1)S(1)}, bf16[2,128,384]{2,1,0:T(8,128)(2,1)S(1)}, u32[]{:S(2)}, u32[]{:S(2)}) collective-permute-start(bf16[2,128,384]{2,1,0:T(8,128)(2,1)S(1)} %get-tuple-element.13), channel_id=1, source_target_pairs={{0,448},{32,480},{64,0},{96,32},{128,64},{160,96},{192,128},{224,1... | collective-permute-start | bytes 589832 | tf_op jit(solution)/shard_map/ppermute | solution.py:203
  43.3 29.2 %all-to-all-start = ((bf16[4,128,384]{2,1,0:T(8,128)(2,1)}), bf16[4,128,384]{2,1,0:T(8,128)(2,1)S(1)}, u32[]{:S(2)}, u32[]{:S(2)}) async-start(bf16[4,128,384]{2,1,0:T(8,128)(2,1)} %shard_map.71), calls=%async_computation | async-start | bytes 786432 | tf_op jit(solution)/shard_map/all_to_all | solution.py:233
  52.1 4.6 %collective-permute-start.5 = (f32[64,384]{1,0:T(8,128)S(1)}, f32[64,384]{1,0:T(8,128)S(1)}, u32[]{:S(2)}, u32[]{:S(2)}) collective-permute-start(f32[64,384]{1,0:T(8,128)S(1)} %bitcast.28), channel_id=1, source_target_pairs={{0,16},{16,0},{1,17},{17,1},{2,18},{18,2},{3,19},{19,3},{4,20},{20... | collective-permute-start | bytes 294920 | tf_op jit(solution)/shard_map/ppermute | solution.py:206
  72.5 36.1 %copy-start.4 = (s32[32,1]{0,1:T(1,128)S(1)}, s32[32,1]{0,1:T(1,128)}, u32[]{:S(2)}) copy-start(s32[32,1]{0,1:T(1,128)} %param.9) | copy-start | bytes 388
  104.1 12.2 %all-to-all-start.3 = ((f32[4,192,128]{2,1,0:T(8,128)}), f32[4,192,128]{2,1,0:T(8,128)S(1)}, u32[]{:S(2)}, u32[]{:S(2)}) async-start(f32[4,192,128]{2,1,0:T(8,128)} %shard_map.74), calls=%async_computation.3 | async-start | bytes 786432 | tf_op jit(solution)/shard_map/all_to_all | solution.py:242
  122.8 17.5 %all-to-all-start.4 = ((bf16[8,64,384]{2,1,0:T(8,128)(2,1)}), bf16[8,64,384]{2,1,0:T(8,128)(2,1)S(1)}, u32[]{:S(2)}, u32[]{:S(2)}) async-start(bf16[8,64,384]{2,1,0:T(8,128)(2,1)} %bitcast.11), calls=%async_computation.4 | async-start | bytes 786432 | tf_op jit(solution)/shard_map/all_to_all | solution.py:271
  141.9 15.8 %all-to-all-start.5 = ((bf16[4,4,64,384]{3,2,1,0:T(8,128)(2,1)}), bf16[4,4,64,384]{3,2,1,0:T(8,128)(2,1)S(1)}, u32[]{:S(2)}, u32[]{:S(2)}) async-start(bf16[4,4,64,384]{3,2,1,0:T(8,128)(2,1)} %shard_map.76), calls=%async_computation.5 | async-start | bytes 1572864 | tf_op jit(solution)/shard_map/all_to_all | solution.py:273
  145.9 3.5 %collective-permute-start.6 = (f32[64,384]{1,0:T(8,128)S(1)}, f32[64,384]{1,0:T(8,128)S(1)}, u32[]{:S(2)}, u32[]{:S(2)}) collective-permute-start(f32[64,384]{1,0:T(8,128)S(1)} %get-tuple-element.17), channel_id=1, source_target_pairs={{0,16},{16,0},{1,17},{17,1},{2,18},{18,2},{3,19},{19,3},{4,20},{20... | collective-permute-start | bytes 294920 | tf_op jit(solution)/shard_map/ppermute | solution.py:206

commit v5 on v4

--- a/solution.py
+++ b/solution.py
@@ -30,19 +30,20 @@
 BLOCKS = ((0, 0), (0, 1), (0, 2), (1, 1), (1, 2), (2, 2))
 MIB = 1024 * 1024
 VMEM = pl.BlockSpec(memory_space=pltpu.VMEM)
+ANY = pl.BlockSpec(memory_space=pl.ANY)
 SMEM = pl.BlockSpec(memory_space=pltpu.SMEM)
 BF16 = jnp.bfloat16
 F32 = jnp.float32
 
 
-def call(kernel, args, outs, scalars=0, scratch=(), flops=0):
+def call(kernel, args, outs, scalars=0, scratch=(), flops=0, spaces=None):
     many = isinstance(outs, list)
     nbytes = sum(a.size * a.dtype.itemsize for a in args)
     return pl.pallas_call(
         kernel,
         out_shape=outs,
         in_specs=[SMEM] * scalars + [VMEM] * (len(args) - scalars),
-        out_specs=[VMEM] * len(outs) if many else VMEM,
+        out_specs=spaces or ([VMEM] * len(outs) if many else VMEM),
         scratch_shapes=list(scratch),
         compiler_params=pltpu.CompilerParams(vmem_limit_bytes=16 * MIB),
         cost_estimate=pl.CostEstimate(flops=flops, bytes_accessed=nbytes, transcendentals=0),
@@ -141,7 +142,12 @@
     return dot(jnp.concatenate([xh, xl, xh], axis=1), jnp.concatenate([yh, yh, yl], axis=0))
 
 
-def newton_schulz_kernel(owner_ref, gram_ref, x_ref, out_ref):
+def newton_schulz_kernel(
+    owner_ref, gram_ref, x_ref, mine_ref, other_ref, out_ref, new_ref, update_ref, sems
+):
+    first = lax.axis_index("core") == 0
+    new_ref[:, 0, :] = jnp.where(first, mine_ref[...], other_ref[...])
+    new_ref[:, 1, :] = jnp.where(first, other_ref[...], mine_ref[...])
     blocks = {}
     for at, (i, j) in enumerate(BLOCKS):
         block = gram_ref[at * LANE : (at + 1) * LANE, :]
@@ -165,28 +171,24 @@
         current = dot3(split(current), poly_parts)
         if sweep < ITERS - 1:
             weights = dot3(split(dot3(parts, poly_parts)), poly_parts)
-    update = (current * math.sqrt(D)).astype(BF16)
-    out_ref[...] = jnp.zeros_like(out_ref)
-    for core in range(CORES):
-        out_ref[core, lax.rem(owner_ref[0], out_ref.shape[1])] = update[core * ROWS : (core + 1) * ROWS, :]
-
-
-def place_kernel(source_ref, got_ref, out_ref):
-    out_ref[...] = jnp.zeros_like(out_ref)
-    for owner in range(out_ref.shape[0]):
-        for slot in range(MOST):
-            source = source_ref[owner * MOST + slot]
-
-            @pl.when(source >= 0)
-            def _():
-                out_ref[owner, slot] = got_ref[source]
+    update_ref[...] = (current * math.sqrt(D)).astype(BF16)
+    copies = [
+        pltpu.make_async_copy(
+            update_ref.at[pl.ds(core * ROWS, ROWS), :], out_ref.at[core, owner_ref[0]], sems.at[core]
+        )
+        for core in range(CORES)
+    ]
+    for copy in copies:
+        copy.start()
+    for copy in copies:
+        copy.wait()
 
 
 def stack_kernel(source_ref, got_ref, out_ref, wide_ref):
     for slot in range(MOST):
         source = source_ref[slot]
-        filled = jnp.where(source >= 0, 1.0, 0.0).astype(F32)
-        wide_ref[:, slot, :] = got_ref[jnp.maximum(source, 0), slot].astype(F32) * filled
+        taken = got_ref[jnp.maximum(source, 0)].astype(F32)
+        wide_ref[:, slot, :] = jnp.where(source >= 0, taken, jnp.zeros_like(taken))
     out_ref[...] = wide_ref[...].astype(BF16)
 
 
@@ -242,35 +244,28 @@
     gram = lax.all_to_all(far_sum, "near", 0, 0).reshape(packed_rows, LANE)
 
     new_other = swap(new_give)
-    new_momentum = jnp.stack(
-        [jnp.where(core == 0, new_mine, new_other), jnp.where(core == 0, new_other, new_mine)], axis=1
-    )
-
     owner_ids = packing[:, 0]
     experts = owner_ids.shape[0]
     positions = jnp.arange(experts, dtype=jnp.int32)
     shared = (owner_ids[:, None] == owner_ids[None, :]) & (positions[None, :] < positions[:, None])
     target = owner_ids * MOST + jnp.sum(shared.astype(jnp.int32), axis=1)
-    of_core, of_y = positions % CORES, positions // CORES % n_y
-    of_x = positions // (CORES * n_y)
-    slots = jnp.arange(MOST, dtype=jnp.int32)
-    line = (jnp.arange(n_x, dtype=jnp.int32)[:, None] * n_y + y) * MOST + slots[None, :]
-    passes = (line.reshape(-1)[:, None] == target[None, :]) & (of_x == x)[None, :]
-    placed_from = jnp.max(jnp.where(passes, (of_core * n_y + of_y)[None, :], -1), axis=1)
-    fills = ((x * n_y + y) * MOST + slots)[:, None] == target[None, :]
-    stacked_from = jnp.max(jnp.where(fills, of_x[None, :], -1), axis=1)
+    n_owner = n_x * n_y
+    lies = positions % CORES * n_owner + positions // CORES
+    wanted = (x * n_y + y) * MOST + jnp.arange(MOST, dtype=jnp.int32)
+    fills = wanted[:, None] == target[None, :]
+    stacked_from = jnp.max(jnp.where(fills, lies[None, :], -1), axis=1)
     my_owner = lax.dynamic_slice_in_dim(owner_ids, (x * n_y + y) * CORES + core, 1, 0)
 
-    sent = call(
+    sent, new_momentum = call(
         newton_schulz_kernel,
-        (my_owner, gram, ns_input),
-        shape((CORES, n_y, ROWS, FF)),
+        (my_owner, gram, ns_input, new_mine, new_other),
+        [shape((CORES, n_owner, ROWS, FF)), shape((ROWS, CORES, FF), F32)],
         scalars=1,
+        scratch=[pltpu.VMEM((PAIR, FF), BF16), pltpu.SemaphoreType.DMA((CORES,))],
         flops=2 * 27 * FF * FF * FF,
-    )
-    got = lax.all_to_all(sent.reshape(CORES * n_y, ROWS, FF), ("core", "y"), 0, 0)
-    placed = call(place_kernel, (placed_from, got), shape((n_x, MOST, ROWS, FF)), scalars=1)
-    got = lax.all_to_all(placed, "x", 0, 0)
+        spaces=[ANY, VMEM],
+    )
+    got = lax.all_to_all(sent.reshape(CORES * n_owner, ROWS, FF), ("core", "x", "y"), 0, 0)
     stacked = call(
         stack_kernel,
         (stacked_from, got),

time: 160 us -> 160 us (level)
  starting transfers between devices: 56.8 us -> 58.7 us
    all_to_all x2 -> x1, waiting for transfers between devices: 15.1 us -> 21.8 us  [body(): lax.all_to_all(sent.reshape(CORES * n_owner, ROWS, FF), ('core', 'x', 'y'...]
    all_to_all x1, waiting for transfers between devices: 6.9 us -> 0.99 us  [body(): gram = lax.all_to_all(far_sum, 'near', 0, 0).reshape(packed_rows, LANE)]
    ppermute x3, starting transfers between devices: 15 us -> 18.3 us  [swap(): return lax.ppermute(value, 'core', ring(CORES, 1))]
    all_to_all x2 -> x1, starting transfers between devices: 13.5 us -> 12.2 us  [body(): lax.all_to_all(sent.reshape(CORES * n_owner, ROWS, FF), ('core', 'x', 'y'...]
    pallas_call x10 -> x9, Pallas kernels: 15.9 us -> 14.8 us  [call(): pl.pallas_call(kernel, out_shape=outs, in_specs=[SMEM] * scalars + [VMEM]...]
    unnamed x13 -> x12, local copies, waits for them, and re-layouts: 4.09 us -> 3.26 us
  transfers between devices with their start and end apart: 11 -> 10, of which waited for: 9 -> 8; matrix products, arithmetic and copies ran while one was open for 1% -> 1% of each run, Pallas kernels for 1% -> 1%
where the time goes in v5:
time: 160 us; the launch traced here: 159 us
  starting transfers between devices  58.7 us (37%)
  waiting for transfers between devices  49.9 us (31%)
  blocking collectives  30.5 us (19%)
  Pallas kernels  14.8 us (9%)
  local copies, waits for them, and re-layouts  4.02 us (3%)
    all_to_all x1, waiting for transfers between devices, body(): lax.all_to_all(sent.reshape(CORES * n_owner, ROWS, FF), ('core', 'x', 'y'...  21.8 us
    ppermute x3, starting transfers between devices, swap(): return lax.ppermute(value, 'core', ring(CORES, 1))  18.3 us
    all_to_all x1, blocking collectives, body(): far_parts = lax.all_to_all(near_sum, 'far', 0, 0)  17.4 us
    all_to_all x1, waiting for transfers between devices, body(): lax.all_to_all(near, 'far', 0, 0)  15.7 us
    ppermute x4, starting transfers between devices, go(): return lax.ppermute(value, ('far', 'near'), ring(FAR * NEAR, step))  15.2 us
    pallas_call x9, Pallas kernels, call(): pl.pallas_call(kernel, out_shape=outs, in_specs=[SMEM] * scalars + [VMEM]...  14.8 us
    all_to_all x1, blocking collectives, body(): near_parts = lax.all_to_all(packed, 'near', 0, 0)  13.1 us
    all_to_all x1, starting transfers between devices, body(): lax.all_to_all(sent.reshape(CORES * n_owner, ROWS, FF), ('core', 'x', 'y'...  12.2 us
  transfers between devices with their start and end apart: 10, of which 8 were waited for; matrix products, arithmetic and copies ran while one was open for 1% of the time, Pallas kernels for 1%

profile of v5, /device:TPU:1, one launch (start us, length us, event | category | flops | bytes accessed | tf_op | source)
XLA Modules:
  0.0 159.1 jit_solution(3573561361906039805)
XLA Ops:
  0.6 1.6 copy-done
  2.2 1.0 copy-done.1
  3.2 0.7 copy-done.2
  3.9 1.9 %shard_map.69 = bf16[4,4,128,384]{3,2,1,0:T(8,128)(2,1)S(1)} custom-call(s32[2]{0:T(128)S(1)} %bitcast.22, bf16[512,2048]{1,0:T(8,128)(2,1)S(1)} %bitcast.15, bf16[512,384]{1,0:T(8,128)(2,1)S(1)} %bitcast.17), custom_call_target="tpu_custom_call" | custom-call | flops 805306368 | bytes 2490376 | tf_op jit(solution)/shard_map/pallas_call | solution.py:42
  5.8 8.8 %collective-permute-start = (bf16[4,4,128,384]{3,2,1,0:T(8,128)(2,1)S(1)}, bf16[4,4,128,384]{3,2,1,0:T(8,128)(2,1)S(1)}, u32[]{:S(2)}, u32[]{:S(2)}) collective-permute-start(bf16[4,4,128,384]{3,2,1,0:T(8,128)(2,1)S(1)} %shard_map.69), channel_id=1, source_target_pairs={{0,16},{16,0},{1,17},{17,1},{2,18},{18,2},{3,19},{19,3},{4,20},{20... | collective-permute-start | bytes 4718600 | tf_op jit(solution)/shard_map/ppermute | solution.py:208
  14.6 1.9 %shard_map.68.mine_ref = bf16[4,4,128,384]{3,2,1,0:T(8,128)(2,1)S(1)} custom-call(s32[2]{0:T(128)S(1)} %bitcast.23, bf16[512,2048]{1,0:T(8,128)(2,1)S(1)} %bitcast.16, bf16[512,384]{1,0:T(8,128)(2,1)S(1)} %bitcast.18), custom_call_target="tpu_custom_call" | custom-call | flops 805306368 | bytes 2490376 | tf_op jit(solution)/shard_map/pallas_call | solution.py:42
  16.5 1.1 collective-permute-done.other_ref
  17.6 0.4 shard_map.70
  18.0 2.1 %collective-permute-start.3 = (bf16[4,128,384]{2,1,0:T(8,128)(2,1)S(1)}, bf16[4,128,384]{2,1,0:T(8,128)(2,1)S(1)}, u32[]{:S(2)}, u32[]{:S(2)}) collective-permute-start(bf16[4,128,384]{2,1,0:T(8,128)(2,1)S(1)} %get-tuple-element.16), channel_id=1, source_target_pairs={{0,32},{32,64},{64,96},{96,128},{128,160},{160,192},{192,224},{224... | collective-permute-start | bytes 1179656 | tf_op jit(solution)/shard_map/ppermute | solution.py:205
  20.1 5.7 %collective-permute-start.4 = (bf16[4,128,384]{2,1,0:T(8,128)(2,1)S(1)}, bf16[4,128,384]{2,1,0:T(8,128)(2,1)S(1)}, u32[]{:S(2)}, u32[]{:S(2)}) collective-permute-start(bf16[4,128,384]{2,1,0:T(8,128)(2,1)S(1)} %get-tuple-element.17), channel_id=1, source_target_pairs={{0,480},{32,0},{64,32},{96,64},{128,96},{160,128},{192,160},{224,1... | collective-permute-start | bytes 1179656 | tf_op jit(solution)/shard_map/ppermute | solution.py:205
  25.8 1.9 %collective-permute-start.1 = (bf16[2,128,384]{2,1,0:T(8,128)(2,1)S(1)}, bf16[2,128,384]{2,1,0:T(8,128)(2,1)S(1)}, u32[]{:S(2)}, u32[]{:S(2)}) collective-permute-start(bf16[2,128,384]{2,1,0:T(8,128)(2,1)S(1)} %get-tuple-element.14), channel_id=1, source_target_pairs={{0,64},{32,96},{64,128},{96,160},{128,192},{160,224},{192,256},{22... | collective-permute-start | bytes 589832 | tf_op jit(solution)/shard_map/ppermute | solution.py:205
  27.7 5.5 %collective-permute-start.2 = (bf16[2,128,384]{2,1,0:T(8,128)(2,1)S(1)}, bf16[2,128,384]{2,1,0:T(8,128)(2,1)S(1)}, u32[]{:S(2)}, u32[]{:S(2)}) collective-permute-start(bf16[2,128,384]{2,1,0:T(8,128)(2,1)S(1)} %get-tuple-element.15), channel_id=1, source_target_pairs={{0,448},{32,480},{64,0},{96,32},{128,64},{160,96},{192,128},{224,1... | collective-permute-start | bytes 589832 | tf_op jit(solution)/shard_map/ppermute | solution.py:205
  33.2 6.5 %collective-permute-done.1.c_ref = bf16[2,128,384]{2,1,0:T(8,128)(2,1)S(1)} collective-permute-done((bf16[2,128,384]{2,1,0:T(8,128)(2,1)S(1)}, bf16[2,128,384]{2,1,0:T(8,128)(2,1)S(1)}, u32[]{:S(2)}, u32[]{:S(2)}) %collective-permute-start.1) | collective-permute-done | bytes 196640 | tf_op jit(solution)/shard_map/ppermute | solution.py:205
  39.7 2.6 %collective-permute-done.2.d_ref = bf16[2,128,384]{2,1,0:T(8,128)(2,1)S(1)} collective-permute-done((bf16[2,128,384]{2,1,0:T(8,128)(2,1)S(1)}, bf16[2,128,384]{2,1,0:T(8,128)(2,1)S(1)}, u32[]{:S(2)}, u32[]{:S(2)}) %collective-permute-start.2) | collective-permute-done | bytes 196640 | tf_op jit(solution)/shard_map/ppermute | solution.py:205
  42.3 1.0 shard_map.71
  43.3 8.7 %all-to-all-start = ((bf16[4,128,384]{2,1,0:T(8,128)(2,1)}), bf16[4,128,384]{2,1,0:T(8,128)(2,1)S(1)}, u32[]{:S(2)}, u32[]{:S(2)}) async-start(bf16[4,128,384]{2,1,0:T(8,128)(2,1)} %shard_map.71), calls=%async_computation | async-start | bytes 786432 | tf_op jit(solution)/shard_map/all_to_all | solution.py:235
  52.1 3.7 %collective-permute-start.5 = (f32[64,384]{1,0:T(8,128)S(1)}, f32[64,384]{1,0:T(8,128)S(1)}, u32[]{:S(2)}, u32[]{:S(2)}) collective-permute-start(f32[64,384]{1,0:T(8,128)S(1)} %bitcast.24), channel_id=1, source_target_pairs={{0,16},{16,0},{1,17},{17,1},{2,18},{18,2},{3,19},{19,3},{4,20},{20... | collective-permute-start | bytes 294920 | tf_op jit(solution)/shard_map/ppermute | solution.py:208
  55.9 0.9 collective-permute-done.5.lent_ref
  56.8 15.7 %all-to-all-done.parts_ref = bf16[4,128,384]{2,1,0:T(8,128)(2,1)S(1)} async-done(((bf16[4,128,384]{2,1,0:T(8,128)(2,1)}), bf16[4,128,384]{2,1,0:T(8,128)(2,1)S(1)}, u32[]{:S(2)}, u32[]{:S(2)}) %all-to-all-start) | async-done | bytes 393248 | tf_op jit(solution)/shard_map/all_to_all | solution.py:235
  72.4 0.3 shard_map.72
  72.8 13.1 %all_to_all.25.parts_ref = bf16[4,192,128]{2,1,0:T(8,128)(2,1)S(1)} all-to-all(bf16[4,192,128]{2,1,0:T(8,128)(2,1)S(1)} %bitcast.21), channel_id=1, replica_groups=mesh['far'=4,'near'=4,'core'=2,'x'=4,'y'=4] {'near'}, dimensions={0} | all-to-all | bytes 393216 | tf_op jit(solution)/shard_map/all_to_all | solution.py:240
  86.0 17.4 %all_to_all.26.parts_ref = bf16[4,192,128]{2,1,0:T(8,128)(2,1)S(1)} all-to-all(bf16[4,192,128]{2,1,0:T(8,128)(2,1)S(1)} %shard_map.73), channel_id=1, replica_groups=mesh['far'=4,'near'=4,'core'=2,'x'=4,'y'=4] {'far'}, dimensions={0} | all-to-all | bytes 393216 | tf_op jit(solution)/shard_map/all_to_all | solution.py:242
  103.3 0.8 shard_map.74
  104.1 4.4 %all-to-all-start.3 = ((f32[4,192,128]{2,1,0:T(8,128)}), f32[4,192,128]{2,1,0:T(8,128)S(1)}, u32[]{:S(2)}, u32[]{:S(2)}) async-start(f32[4,192,128]{2,1,0:T(8,128)} %shard_map.74), calls=%async_computation.3 | async-start | bytes 786432 | tf_op jit(solution)/shard_map/all_to_all | solution.py:244
  108.5 5.8 %collective-permute-start.6 = (f32[64,384]{1,0:T(8,128)S(1)}, f32[64,384]{1,0:T(8,128)S(1)}, u32[]{:S(2)}, u32[]{:S(2)}) collective-permute-start(f32[64,384]{1,0:T(8,128)S(1)} %get-tuple-element.21), channel_id=1, source_target_pairs={{0,16},{16,0},{1,17},{17,1},{2,18},{18,2},{3,19},{19,3},{4,20},{20... | collective-permute-start | bytes 294920 | tf_op jit(solution)/shard_map/ppermute | solution.py:208
  114.4 0.6 constant_dynamic-slice_fusion.2
  115.0 0.3 collective-permute-done.6.other_ref
  115.3 1.0 all-to-all-done.3
  116.3 7.0 %shard_map.75 = (bf16[2,16,64,384]{3,2,1,0:T(8,128)(2,1)}, f32[64,2,384]{2,1,0:T(2,128)}) custom-call(s32[1]{0:T(128)} %bitcast.owner_ref, f32[768,128]{1,0:T(8,128)S(1)} %bitcast.19, bf16[128,384]{1,0:T(8,128)(2,1)S(1)} %get-tuple-element.19.x_ref, f32[64,384]{1,0:T(8,128)S(1)} %get-tuple-element.20.mine_ref, f32[64,384]{1,0:T(8,128)S(1)} %collective-permute-done.6.other_ref), custom_call_target="tpu_custom_call" | custom-call | flops 3057647616 | bytes 688132 | tf_op jit(solution)/shard_map/pallas_call | solution.py:42
  123.3 12.2 %all-to-all-start.4 = ((bf16[32,64,384]{2,1,0:T(8,128)(2,1)}), bf16[32,64,384]{2,1,0:T(8,128)(2,1)S(1)}, u32[]{:S(2)}, u32[]{:S(2)}) async-start(bf16[32,64,384]{2,1,0:T(8,128)(2,1)} %bitcast.9), calls=%async_computation.4 | async-start | bytes 3145728 | tf_op jit(solution)/shard_map/all_to_all | solution.py:268
  135.9 21.8 %all-to-all-done.4.got_ref = bf16[32,64,384]{2,1,0:T(8,128)(2,1)S(1)} async-done(((bf16[32,64,384]{2,1,0:T(8,128)(2,1)}), bf16[32,64,384]{2,1,0:T(8,128)(2,1)S(1)}, u32[]{:S(2)}, u32[]{:S(2)}) %all-to-all-start.4) | async-done | bytes 1572896 | tf_op jit(solution)/shard_map/all_to_all | solution.py:268
  157.7 1.4 shard_map.76
  (17 shorter events, 0.6 us)
Async XLA Ops:
  0.6 1.6 %copy-start = (bf16[512,1,2048]{2,0,1:T(8,128)(2,1)S(1)}, bf16[512,1,2048]{2,0,1:T(8,128)(2,1)}, u32[]{:S(2)}) copy-start(bf16[512,1,2048]{2,0,1:T(8,128)(2,1)} %param.5) | copy-start | bytes 6291460
  2.2 1.0 copy-start.1
  3.2 0.7 copy-start.2
  5.8 11.8 %collective-permute-start = (bf16[4,4,128,384]{3,2,1,0:T(8,128)(2,1)S(1)}, bf16[4,4,128,384]{3,2,1,0:T(8,128)(2,1)S(1)}, u32[]{:S(2)}, u32[]{:S(2)}) collective-permute-start(bf16[4,4,128,384]{3,2,1,0:T(8,128)(2,1)S(1)} %shard_map.69), channel_id=1, source_target_pairs={{0,16},{16,0},{1,17},{17,1},{2,18},{18,2},{3,19},{19,3},{4,20},{20... | collective-permute-start | bytes 4718600 | tf_op jit(solution)/shard_map/ppermute | solution.py:208
  18.0 34.0 %copy-start.3 = (f32[64,2,384]{2,1,0:T(2,128)S(1)}, f32[64,2,384]{2,1,0:T(2,128)}, u32[]{:S(2)}) copy-start(f32[64,2,384]{2,1,0:T(2,128)} %param.8) | copy-start | bytes 589828
  18.0 24.3 %collective-permute-start.3 = (bf16[4,128,384]{2,1,0:T(8,128)(2,1)S(1)}, bf16[4,128,384]{2,1,0:T(8,128)(2,1)S(1)}, u32[]{:S(2)}, u32[]{:S(2)}) collective-permute-start(bf16[4,128,384]{2,1,0:T(8,128)(2,1)S(1)} %get-tuple-element.16), channel_id=1, source_target_pairs={{0,32},{32,64},{64,96},{96,128},{128,160},{160,192},{192,224},{224... | collective-permute-start | bytes 1179656 | tf_op jit(solution)/shard_map/ppermute | solution.py:205
  20.1 22.3 %collective-permute-start.4 = (bf16[4,128,384]{2,1,0:T(8,128)(2,1)S(1)}, bf16[4,128,384]{2,1,0:T(8,128)(2,1)S(1)}, u32[]{:S(2)}, u32[]{:S(2)}) collective-permute-start(bf16[4,128,384]{2,1,0:T(8,128)(2,1)S(1)} %get-tuple-element.17), channel_id=1, source_target_pairs={{0,480},{32,0},{64,32},{96,64},{128,96},{160,128},{192,160},{224,1... | collective-permute-start | bytes 1179656 | tf_op jit(solution)/shard_map/ppermute | solution.py:205
  25.8 13.9 %collective-permute-start.1 = (bf16[2,128,384]{2,1,0:T(8,128)(2,1)S(1)}, bf16[2,128,384]{2,1,0:T(8,128)(2,1)S(1)}, u32[]{:S(2)}, u32[]{:S(2)}) collective-permute-start(bf16[2,128,384]{2,1,0:T(8,128)(2,1)S(1)} %get-tuple-element.14), channel_id=1, source_target_pairs={{0,64},{32,96},{64,128},{96,160},{128,192},{160,224},{192,256},{22... | collective-permute-start | bytes 589832 | tf_op jit(solution)/shard_map/ppermute | solution.py:205
  27.7 14.6 %collective-permute-start.2 = (bf16[2,128,384]{2,1,0:T(8,128)(2,1)S(1)}, bf16[2,128,384]{2,1,0:T(8,128)(2,1)S(1)}, u32[]{:S(2)}, u32[]{:S(2)}) collective-permute-start(bf16[2,128,384]{2,1,0:T(8,128)(2,1)S(1)} %get-tuple-element.15), channel_id=1, source_target_pairs={{0,448},{32,480},{64,0},{96,32},{128,64},{160,96},{192,128},{224,1... | collective-permute-start | bytes 589832 | tf_op jit(solution)/shard_map/ppermute | solution.py:205
  43.3 29.2 %all-to-all-start = ((bf16[4,128,384]{2,1,0:T(8,128)(2,1)}), bf16[4,128,384]{2,1,0:T(8,128)(2,1)S(1)}, u32[]{:S(2)}, u32[]{:S(2)}) async-start(bf16[4,128,384]{2,1,0:T(8,128)(2,1)} %shard_map.71), calls=%async_computation | async-start | bytes 786432 | tf_op jit(solution)/shard_map/all_to_all | solution.py:235
  52.1 4.6 %collective-permute-start.5 = (f32[64,384]{1,0:T(8,128)S(1)}, f32[64,384]{1,0:T(8,128)S(1)}, u32[]{:S(2)}, u32[]{:S(2)}) collective-permute-start(f32[64,384]{1,0:T(8,128)S(1)} %bitcast.24), channel_id=1, source_target_pairs={{0,16},{16,0},{1,17},{17,1},{2,18},{18,2},{3,19},{19,3},{4,20},{20... | collective-permute-start | bytes 294920 | tf_op jit(solution)/shard_map/ppermute | solution.py:208
  72.4 41.9 %copy-start.4 = (s32[32,1]{0,1:T(1,128)S(1)}, s32[32,1]{0,1:T(1,128)}, u32[]{:S(2)}) copy-start(s32[32,1]{0,1:T(1,128)} %param.9) | copy-start | bytes 388
  104.1 12.2 %all-to-all-start.3 = ((f32[4,192,128]{2,1,0:T(8,128)}), f32[4,192,128]{2,1,0:T(8,128)S(1)}, u32[]{:S(2)}, u32[]{:S(2)}) async-start(f32[4,192,128]{2,1,0:T(8,128)} %shard_map.74), calls=%async_computation.3 | async-start | bytes 786432 | tf_op jit(solution)/shard_map/all_to_all | solution.py:244
  108.5 6.7 %collective-permute-start.6 = (f32[64,384]{1,0:T(8,128)S(1)}, f32[64,384]{1,0:T(8,128)S(1)}, u32[]{:S(2)}, u32[]{:S(2)}) collective-permute-start(f32[64,384]{1,0:T(8,128)S(1)} %get-tuple-element.21), channel_id=1, source_target_pairs={{0,16},{16,0},{1,17},{17,1},{2,18},{18,2},{3,19},{19,3},{4,20},{20... | collective-permute-start | bytes 294920 | tf_op jit(solution)/shard_map/ppermute | solution.py:208
  123.3 34.3 %all-to-all-start.4 = ((bf16[32,64,384]{2,1,0:T(8,128)(2,1)}), bf16[32,64,384]{2,1,0:T(8,128)(2,1)S(1)}, u32[]{:S(2)}, u32[]{:S(2)}) async-start(bf16[32,64,384]{2,1,0:T(8,128)(2,1)} %bitcast.9), calls=%async_computation.4 | async-start | bytes 3145728 | tf_op jit(solution)/shard_map/all_to_all | solution.py:268

commit v6 on v4

--- a/solution.py
+++ b/solution.py
@@ -27,7 +27,10 @@
 COEF_C = 2.0315
 BETA = 0.95
 EPSILON = 1e-07
-BLOCKS = ((0, 0), (0, 1), (0, 2), (1, 1), (1, 2), (2, 2))
+BLOCKS = ((0, 1), (0, 2), (1, 2))
+SIDE = FF // LANE
+HALF = LANE // 2
+PACKED = len(BLOCKS) * LANE + (SIDE + 2) * HALF
 MIB = 1024 * 1024
 VMEM = pl.BlockSpec(memory_space=pltpu.VMEM)
 SMEM = pl.BlockSpec(memory_space=pltpu.SMEM)
@@ -112,11 +115,19 @@
         new_ref[...] = new
         ns_ref[rows, :] = (grad + BETA * new).astype(BF16)
     x = ns_ref[...]
-    gram = transposed_dot(x, x).astype(BF16)
-    for at, (i, j) in enumerate(BLOCKS):
-        gram_ref[at * LANE : (at + 1) * LANE, :] = gram[
-            i * LANE : (i + 1) * LANE, j * LANE : (j + 1) * LANE
-        ]
+    gram = transposed_dot(x, x)
+    top, bottom = [], []
+    for i in range(SIDE):
+        columns = slice(i * LANE, (i + 1) * LANE)
+        top.append(gram[i * LANE : i * LANE + HALF, columns])
+        bottom.append(gram[i * LANE + HALF : (i + 1) * LANE, columns])
+    left = lax.broadcasted_iota(jnp.int32, (HALF, LANE), 1) < HALF
+    pair = jnp.where(left, pltpu.roll(bottom[0], HALF, 1), bottom[1])
+    whole = [gram[i * LANE : (i + 1) * LANE, j * LANE : (j + 1) * LANE] for i, j in BLOCKS]
+    at = 0
+    for part in whole + top + [pair, bottom[2]]:
+        gram_ref[at : at + part.shape[0], :] = part.astype(BF16)
+        at += part.shape[0]
 
 
 def spread_sum_kernel(parts_ref, out_ref):
@@ -145,9 +156,15 @@
     blocks = {}
     for at, (i, j) in enumerate(BLOCKS):
         block = gram_ref[at * LANE : (at + 1) * LANE, :]
-        blocks[i, j] = block
-        if i != j:
-            blocks[j, i] = block.T
+        blocks[i, j], blocks[j, i] = block, block.T
+    start = len(BLOCKS) * LANE
+    halves = [gram_ref[start + i * HALF : start + (i + 1) * HALF, :] for i in range(SIDE + 2)]
+    left = lax.broadcasted_iota(jnp.int32, (HALF, LANE), 1) < HALF
+    corners = (pltpu.roll(halves[SIDE], HALF, 1), halves[SIDE], halves[SIDE + 1])
+    for i in range(SIDE):
+        turned = jnp.concatenate([halves[i], halves[i]], axis=0).T
+        below = jnp.where(left, turned[HALF:, :], corners[i])
+        blocks[i, i] = jnp.concatenate([halves[i], below], axis=0)
     gram = jnp.concatenate(
         [jnp.concatenate([blocks[i, j] for j in range(3)], axis=1) for i in range(3)], axis=0
     )
@@ -227,7 +244,7 @@
     kept = lax.dynamic_index_in_dim(momentum, core, 1, keepdims=False)
     lent = swap(lax.dynamic_index_in_dim(momentum, 1 - core, 1, keepdims=False))
     rows = shape((ROWS, FF), F32)
-    packed_rows = len(BLOCKS) * LANE
+    packed_rows = PACKED
     ns_input, new_mine, new_give, packed = call(
         momentum_kernel,
         (lax.all_to_all(near, "far", 0, 0), kept, lent),

time: 160 us -> 158 us (0.988)
  transfers between devices with their start and end apart: 11 -> 11, of which waited for: 9 -> 9; matrix products, arithmetic and copies ran while one was open for 1% -> 2% of each run, Pallas kernels for 1% -> 1%
where the time goes in v6:
time: 158 us; the launch traced here: 157 us
  starting transfers between devices  56.3 us (36%)
  waiting for transfers between devices  48.1 us (30%)
  blocking collectives  30.3 us (19%)
  Pallas kernels  16 us (10%)
  local copies, waits for them, and re-layouts  4.93 us (3%)
    all_to_all x1, blocking collectives, body(): far_parts = lax.all_to_all(near_sum, 'far', 0, 0)  17.3 us
    pallas_call x10, Pallas kernels, call(): pl.pallas_call(kernel, out_shape=outs, in_specs=[SMEM] * scalars + [VMEM]...  16 us
    all_to_all x1, waiting for transfers between devices, body(): lax.all_to_all(near, 'far', 0, 0)  15.7 us
    ppermute x4, starting transfers between devices, go(): return lax.ppermute(value, ('far', 'near'), ring(FAR * NEAR, step))  15.2 us
    ppermute x3, starting transfers between devices, swap(): return lax.ppermute(value, 'core', ring(CORES, 1))  15 us
    all_to_all x1, blocking collectives, body(): near_parts = lax.all_to_all(packed, 'near', 0, 0)  13.1 us
    all_to_all x1, starting transfers between devices, body(): lax.all_to_all(sent.reshape(CORES * n_y, ROWS, FF), ('core', 'y'), 0, 0)  9.98 us
    ppermute x4, waiting for transfers between devices, go(): return lax.ppermute(value, ('far', 'near'), ring(FAR * NEAR, step))  9.13 us
  transfers between devices with their start and end apart: 11, of which 9 were waited for; matrix products, arithmetic and copies ran while one was open for 2% of the time, Pallas kernels for 1%

profile of v6, /device:TPU:1, one launch (start us, length us, event | category | flops | bytes accessed | tf_op | source)
XLA Modules:
  0.0 157.2 jit_solution(2193052546074767528)
XLA Ops:
  0.6 1.6 %copy-done = bf16[512,1,2048]{2,0,1:T(8,128)(2,1)S(1)} copy-done((bf16[512,1,2048]{2,0,1:T(8,128)(2,1)S(1)}, bf16[512,1,2048]{2,0,1:T(8,128)(2,1)}, u32[]{:S(2)}) %copy-start) | copy-done | bytes 2097176
  2.2 1.0 copy-done.1
  3.9 1.9 %shard_map.69 = bf16[4,4,128,384]{3,2,1,0:T(8,128)(2,1)S(1)} custom-call(s32[2]{0:T(128)S(1)} %bitcast.26, bf16[512,2048]{1,0:T(8,128)(2,1)S(1)} %bitcast.19, bf16[512,384]{1,0:T(8,128)(2,1)S(1)} %bitcast.21), custom_call_target="tpu_custom_call" | custom-call | flops 805306368 | bytes 2490376 | tf_op jit(solution)/shard_map/pallas_call | solution.py:44
  5.8 8.8 %collective-permute-start = (bf16[4,4,128,384]{3,2,1,0:T(8,128)(2,1)S(1)}, bf16[4,4,128,384]{3,2,1,0:T(8,128)(2,1)S(1)}, u32[]{:S(2)}, u32[]{:S(2)}) collective-permute-start(bf16[4,4,128,384]{3,2,1,0:T(8,128)(2,1)S(1)} %shard_map.69), channel_id=1, source_target_pairs={{0,16},{16,0},{1,17},{17,1},{2,18},{18,2},{3,19},{19,3},{4,20},{20... | collective-permute-start | bytes 4718600 | tf_op jit(solution)/shard_map/ppermute | solution.py:223
  14.6 1.9 %shard_map.68.mine_ref = bf16[4,4,128,384]{3,2,1,0:T(8,128)(2,1)S(1)} custom-call(s32[2]{0:T(128)S(1)} %bitcast.27, bf16[512,2048]{1,0:T(8,128)(2,1)S(1)} %bitcast.20, bf16[512,384]{1,0:T(8,128)(2,1)S(1)} %bitcast.22), custom_call_target="tpu_custom_call" | custom-call | flops 805306368 | bytes 2490376 | tf_op jit(solution)/shard_map/pallas_call | solution.py:44
  16.5 1.1 collective-permute-done.other_ref
  18.0 2.1 %collective-permute-start.3 = (bf16[4,128,384]{2,1,0:T(8,128)(2,1)S(1)}, bf16[4,128,384]{2,1,0:T(8,128)(2,1)S(1)}, u32[]{:S(2)}, u32[]{:S(2)}) collective-permute-start(bf16[4,128,384]{2,1,0:T(8,128)(2,1)S(1)} %get-tuple-element.14), channel_id=1, source_target_pairs={{0,32},{32,64},{64,96},{96,128},{128,160},{160,192},{192,224},{224... | collective-permute-start | bytes 1179656 | tf_op jit(solution)/shard_map/ppermute | solution.py:220
  20.1 5.7 %collective-permute-start.4 = (bf16[4,128,384]{2,1,0:T(8,128)(2,1)S(1)}, bf16[4,128,384]{2,1,0:T(8,128)(2,1)S(1)}, u32[]{:S(2)}, u32[]{:S(2)}) collective-permute-start(bf16[4,128,384]{2,1,0:T(8,128)(2,1)S(1)} %get-tuple-element.15), channel_id=1, source_target_pairs={{0,480},{32,0},{64,32},{96,64},{128,96},{160,128},{192,160},{224,1... | collective-permute-start | bytes 1179656 | tf_op jit(solution)/shard_map/ppermute | solution.py:220
  25.8 1.9 %collective-permute-start.1 = (bf16[2,128,384]{2,1,0:T(8,128)(2,1)S(1)}, bf16[2,128,384]{2,1,0:T(8,128)(2,1)S(1)}, u32[]{:S(2)}, u32[]{:S(2)}) collective-permute-start(bf16[2,128,384]{2,1,0:T(8,128)(2,1)S(1)} %get-tuple-element.12), channel_id=1, source_target_pairs={{0,64},{32,96},{64,128},{96,160},{128,192},{160,224},{192,256},{22... | collective-permute-start | bytes 589832 | tf_op jit(solution)/shard_map/ppermute | solution.py:220
  27.7 5.5 %collective-permute-start.2 = (bf16[2,128,384]{2,1,0:T(8,128)(2,1)S(1)}, bf16[2,128,384]{2,1,0:T(8,128)(2,1)S(1)}, u32[]{:S(2)}, u32[]{:S(2)}) collective-permute-start(bf16[2,128,384]{2,1,0:T(8,128)(2,1)S(1)} %get-tuple-element.13), channel_id=1, source_target_pairs={{0,448},{32,480},{64,0},{96,32},{128,64},{160,96},{192,128},{224,1... | collective-permute-start | bytes 589832 | tf_op jit(solution)/shard_map/ppermute | solution.py:220
  33.2 6.5 %collective-permute-done.1.c_ref = bf16[2,128,384]{2,1,0:T(8,128)(2,1)S(1)} collective-permute-done((bf16[2,128,384]{2,1,0:T(8,128)(2,1)S(1)}, bf16[2,128,384]{2,1,0:T(8,128)(2,1)S(1)}, u32[]{:S(2)}, u32[]{:S(2)}) %collective-permute-start.1) | collective-permute-done | bytes 196640 | tf_op jit(solution)/shard_map/ppermute | solution.py:220
  39.7 2.6 %collective-permute-done.2.d_ref = bf16[2,128,384]{2,1,0:T(8,128)(2,1)S(1)} collective-permute-done((bf16[2,128,384]{2,1,0:T(8,128)(2,1)S(1)}, bf16[2,128,384]{2,1,0:T(8,128)(2,1)S(1)}, u32[]{:S(2)}, u32[]{:S(2)}) %collective-permute-start.2) | collective-permute-done | bytes 196640 | tf_op jit(solution)/shard_map/ppermute | solution.py:220
  42.3 1.0 shard_map.71
  43.3 8.7 %all-to-all-start = ((bf16[4,128,384]{2,1,0:T(8,128)(2,1)}), bf16[4,128,384]{2,1,0:T(8,128)(2,1)S(1)}, u32[]{:S(2)}, u32[]{:S(2)}) async-start(bf16[4,128,384]{2,1,0:T(8,128)(2,1)} %shard_map.71), calls=%async_computation | async-start | bytes 786432 | tf_op jit(solution)/shard_map/all_to_all | solution.py:250
  52.1 3.7 %collective-permute-start.5 = (f32[64,384]{1,0:T(8,128)S(1)}, f32[64,384]{1,0:T(8,128)S(1)}, u32[]{:S(2)}, u32[]{:S(2)}) collective-permute-start(f32[64,384]{1,0:T(8,128)S(1)} %bitcast.28), channel_id=1, source_target_pairs={{0,16},{16,0},{1,17},{17,1},{2,18},{18,2},{3,19},{19,3},{4,20},{20... | collective-permute-start | bytes 294920 | tf_op jit(solution)/shard_map/ppermute | solution.py:223
  55.9 0.9 collective-permute-done.5.lent_ref
  56.8 15.7 %all-to-all-done.parts_ref = bf16[4,128,384]{2,1,0:T(8,128)(2,1)S(1)} async-done(((bf16[4,128,384]{2,1,0:T(8,128)(2,1)}), bf16[4,128,384]{2,1,0:T(8,128)(2,1)S(1)}, u32[]{:S(2)}, u32[]{:S(2)}) %all-to-all-start) | async-done | bytes 393248 | tf_op jit(solution)/shard_map/all_to_all | solution.py:250
  72.8 13.1 %all_to_all.30.parts_ref = bf16[4,176,128]{2,1,0:T(8,128)(2,1)S(1)} all-to-all(bf16[4,176,128]{2,1,0:T(8,128)(2,1)S(1)} %bitcast.25), channel_id=1, replica_groups=mesh['far'=4,'near'=4,'core'=2,'x'=4,'y'=4] {'near'}, dimensions={0} | all-to-all | bytes 360448 | tf_op jit(solution)/shard_map/all_to_all | solution.py:255
  85.9 17.3 %all_to_all.31.parts_ref = bf16[4,176,128]{2,1,0:T(8,128)(2,1)S(1)} all-to-all(bf16[4,176,128]{2,1,0:T(8,128)(2,1)S(1)} %shard_map.73), channel_id=1, replica_groups=mesh['far'=4,'near'=4,'core'=2,'x'=4,'y'=4] {'far'}, dimensions={0} | all-to-all | bytes 360448 | tf_op jit(solution)/shard_map/all_to_all | solution.py:257
  103.2 0.8 shard_map.74
  104.0 3.5 %all-to-all-start.3 = ((f32[4,176,128]{2,1,0:T(8,128)}), f32[4,176,128]{2,1,0:T(8,128)S(1)}, u32[]{:S(2)}, u32[]{:S(2)}) async-start(f32[4,176,128]{2,1,0:T(8,128)} %shard_map.74), calls=%async_computation.3 | async-start | bytes 720896 | tf_op jit(solution)/shard_map/all_to_all | solution.py:259
  108.3 5.5 %all-to-all-done.3 = f32[4,176,128]{2,1,0:T(8,128)S(1)} async-done(((f32[4,176,128]{2,1,0:T(8,128)}), f32[4,176,128]{2,1,0:T(8,128)S(1)}, u32[]{:S(2)}, u32[]{:S(2)}) %all-to-all-start.3) | async-done | bytes 360480 | tf_op jit(solution)/shard_map/all_to_all | solution.py:259
  113.8 6.6 %shard_map.75 = bf16[2,4,64,384]{3,2,1,0:T(8,128)(2,1)} custom-call(s32[1]{0:T(128)} %bitcast.8.owner_ref, f32[704,128]{1,0:T(8,128)S(1)} %bitcast.24, bf16[128,384]{1,0:T(8,128)(2,1)S(1)} %get-tuple-element.19.x_ref), custom_call_target="tpu_custom_call" | custom-call | flops 3057647616 | bytes 458756 | tf_op jit(solution)/shard_map/pallas_call | solution.py:44
  120.5 10.0 %all-to-all-start.4 = ((bf16[8,64,384]{2,1,0:T(8,128)(2,1)}), bf16[8,64,384]{2,1,0:T(8,128)(2,1)S(1)}, u32[]{:S(2)}, u32[]{:S(2)}) async-start(bf16[8,64,384]{2,1,0:T(8,128)(2,1)} %bitcast.11), calls=%async_computation.4 | async-start | bytes 786432 | tf_op jit(solution)/shard_map/all_to_all | solution.py:288
  130.7 7.7 %all-to-all-done.4.got_ref = bf16[8,64,384]{2,1,0:T(8,128)(2,1)S(1)} async-done(((bf16[8,64,384]{2,1,0:T(8,128)(2,1)}), bf16[8,64,384]{2,1,0:T(8,128)(2,1)S(1)}, u32[]{:S(2)}, u32[]{:S(2)}) %all-to-all-start.4) | async-done | bytes 393248 | tf_op jit(solution)/shard_map/all_to_all | solution.py:288
  138.4 1.6 %shard_map.76 = bf16[4,4,64,384]{3,2,1,0:T(8,128)(2,1)} custom-call(s32[16]{0:T(128)S(1)} %select_reduce_fusion.source_ref, bf16[8,64,384]{2,1,0:T(8,128)(2,1)S(1)} %all-to-all-done.4.got_ref), custom_call_target="tpu_custom_call" | custom-call | bytes 393280 | tf_op jit(solution)/shard_map/pallas_call | solution.py:44
  140.1 4.0 %all-to-all-start.5 = ((bf16[4,4,64,384]{3,2,1,0:T(8,128)(2,1)}), bf16[4,4,64,384]{3,2,1,0:T(8,128)(2,1)S(1)}, u32[]{:S(2)}, u32[]{:S(2)}) async-start(bf16[4,4,64,384]{3,2,1,0:T(8,128)(2,1)} %shard_map.76), calls=%async_computation.5 | async-start | bytes 1572864 | tf_op jit(solution)/shard_map/all_to_all | solution.py:290
  144.1 2.5 %collective-permute-start.6 = (f32[64,384]{1,0:T(8,128)S(1)}, f32[64,384]{1,0:T(8,128)S(1)}, u32[]{:S(2)}, u32[]{:S(2)}) collective-permute-start(f32[64,384]{1,0:T(8,128)S(1)} %get-tuple-element.17), channel_id=1, source_target_pairs={{0,16},{16,0},{1,17},{17,1},{2,18},{18,2},{3,19},{19,3},{4,20},{20... | collective-permute-start | bytes 294920 | tf_op jit(solution)/shard_map/ppermute | solution.py:223
  146.8 0.7 collective-permute-done.6
  147.6 0.8 copy.13
  148.4 7.4 %all-to-all-done.5.got_ref = bf16[4,4,64,384]{3,2,1,0:T(8,128)(2,1)S(1)} async-done(((bf16[4,4,64,384]{3,2,1,0:T(8,128)(2,1)}), bf16[4,4,64,384]{3,2,1,0:T(8,128)(2,1)S(1)}, u32[]{:S(2)}, u32[]{:S(2)}) %all-to-all-start.5) | async-done | bytes 786464 | tf_op jit(solution)/shard_map/all_to_all | solution.py:290
  155.8 1.4 shard_map.77
  (29 shorter events, 3.0 us)
Async XLA Ops:
  0.6 1.6 %copy-start = (bf16[512,1,2048]{2,0,1:T(8,128)(2,1)S(1)}, bf16[512,1,2048]{2,0,1:T(8,128)(2,1)}, u32[]{:S(2)}) copy-start(bf16[512,1,2048]{2,0,1:T(8,128)(2,1)} %param.5) | copy-start | bytes 6291460
  2.2 1.0 copy-start.1
  3.2 0.7 copy-start.2
  5.8 11.8 %collective-permute-start = (bf16[4,4,128,384]{3,2,1,0:T(8,128)(2,1)S(1)}, bf16[4,4,128,384]{3,2,1,0:T(8,128)(2,1)S(1)}, u32[]{:S(2)}, u32[]{:S(2)}) collective-permute-start(bf16[4,4,128,384]{3,2,1,0:T(8,128)(2,1)S(1)} %shard_map.69), channel_id=1, source_target_pairs={{0,16},{16,0},{1,17},{17,1},{2,18},{18,2},{3,19},{19,3},{4,20},{20... | collective-permute-start | bytes 4718600 | tf_op jit(solution)/shard_map/ppermute | solution.py:223
  18.0 34.0 %copy-start.3 = (f32[64,2,384]{2,1,0:T(2,128)S(1)}, f32[64,2,384]{2,1,0:T(2,128)}, u32[]{:S(2)}) copy-start(f32[64,2,384]{2,1,0:T(2,128)} %param.8) | copy-start | bytes 589828
  18.0 24.3 %collective-permute-start.3 = (bf16[4,128,384]{2,1,0:T(8,128)(2,1)S(1)}, bf16[4,128,384]{2,1,0:T(8,128)(2,1)S(1)}, u32[]{:S(2)}, u32[]{:S(2)}) collective-permute-start(bf16[4,128,384]{2,1,0:T(8,128)(2,1)S(1)} %get-tuple-element.14), channel_id=1, source_target_pairs={{0,32},{32,64},{64,96},{96,128},{128,160},{160,192},{192,224},{224... | collective-permute-start | bytes 1179656 | tf_op jit(solution)/shard_map/ppermute | solution.py:220
  20.1 22.3 %collective-permute-start.4 = (bf16[4,128,384]{2,1,0:T(8,128)(2,1)S(1)}, bf16[4,128,384]{2,1,0:T(8,128)(2,1)S(1)}, u32[]{:S(2)}, u32[]{:S(2)}) collective-permute-start(bf16[4,128,384]{2,1,0:T(8,128)(2,1)S(1)} %get-tuple-element.15), channel_id=1, source_target_pairs={{0,480},{32,0},{64,32},{96,64},{128,96},{160,128},{192,160},{224,1... | collective-permute-start | bytes 1179656 | tf_op jit(solution)/shard_map/ppermute | solution.py:220
  25.8 13.9 %collective-permute-start.1 = (bf16[2,128,384]{2,1,0:T(8,128)(2,1)S(1)}, bf16[2,128,384]{2,1,0:T(8,128)(2,1)S(1)}, u32[]{:S(2)}, u32[]{:S(2)}) collective-permute-start(bf16[2,128,384]{2,1,0:T(8,128)(2,1)S(1)} %get-tuple-element.12), channel_id=1, source_target_pairs={{0,64},{32,96},{64,128},{96,160},{128,192},{160,224},{192,256},{22... | collective-permute-start | bytes 589832 | tf_op jit(solution)/shard_map/ppermute | solution.py:220
  27.7 14.6 %collective-permute-start.2 = (bf16[2,128,384]{2,1,0:T(8,128)(2,1)S(1)}, bf16[2,128,384]{2,1,0:T(8,128)(2,1)S(1)}, u32[]{:S(2)}, u32[]{:S(2)}) collective-permute-start(bf16[2,128,384]{2,1,0:T(8,128)(2,1)S(1)} %get-tuple-element.13), channel_id=1, source_target_pairs={{0,448},{32,480},{64,0},{96,32},{128,64},{160,96},{192,128},{224,1... | collective-permute-start | bytes 589832 | tf_op jit(solution)/shard_map/ppermute | solution.py:220
  43.3 29.2 %all-to-all-start = ((bf16[4,128,384]{2,1,0:T(8,128)(2,1)}), bf16[4,128,384]{2,1,0:T(8,128)(2,1)S(1)}, u32[]{:S(2)}, u32[]{:S(2)}) async-start(bf16[4,128,384]{2,1,0:T(8,128)(2,1)} %shard_map.71), calls=%async_computation | async-start | bytes 786432 | tf_op jit(solution)/shard_map/all_to_all | solution.py:250
  52.1 4.6 %collective-permute-start.5 = (f32[64,384]{1,0:T(8,128)S(1)}, f32[64,384]{1,0:T(8,128)S(1)}, u32[]{:S(2)}, u32[]{:S(2)}) collective-permute-start(f32[64,384]{1,0:T(8,128)S(1)} %bitcast.28), channel_id=1, source_target_pairs={{0,16},{16,0},{1,17},{17,1},{2,18},{18,2},{3,19},{19,3},{4,20},{20... | collective-permute-start | bytes 294920 | tf_op jit(solution)/shard_map/ppermute | solution.py:223
  55.9 51.6 %copy-start.4 = (s32[32,1]{0,1:T(1,128)S(1)}, s32[32,1]{0,1:T(1,128)}, u32[]{:S(2)}) copy-start(s32[32,1]{0,1:T(1,128)} %param.9) | copy-start | bytes 388
  104.0 9.9 %all-to-all-start.3 = ((f32[4,176,128]{2,1,0:T(8,128)}), f32[4,176,128]{2,1,0:T(8,128)S(1)}, u32[]{:S(2)}, u32[]{:S(2)}) async-start(f32[4,176,128]{2,1,0:T(8,128)} %shard_map.74), calls=%async_computation.3 | async-start | bytes 720896 | tf_op jit(solution)/shard_map/all_to_all | solution.py:259
  120.5 17.9 %all-to-all-start.4 = ((bf16[8,64,384]{2,1,0:T(8,128)(2,1)}), bf16[8,64,384]{2,1,0:T(8,128)(2,1)S(1)}, u32[]{:S(2)}, u32[]{:S(2)}) async-start(bf16[8,64,384]{2,1,0:T(8,128)(2,1)} %bitcast.11), calls=%async_computation.4 | async-start | bytes 786432 | tf_op jit(solution)/shard_map/all_to_all | solution.py:288
  140.1 15.7 %all-to-all-start.5 = ((bf16[4,4,64,384]{3,2,1,0:T(8,128)(2,1)}), bf16[4,4,64,384]{3,2,1,0:T(8,128)(2,1)S(1)}, u32[]{:S(2)}, u32[]{:S(2)}) async-start(bf16[4,4,64,384]{3,2,1,0:T(8,128)(2,1)} %shard_map.76), calls=%async_computation.5 | async-start | bytes 1572864 | tf_op jit(solution)/shard_map/all_to_all | solution.py:290
  144.1 3.5 %collective-permute-start.6 = (f32[64,384]{1,0:T(8,128)S(1)}, f32[64,384]{1,0:T(8,128)S(1)}, u32[]{:S(2)}, u32[]{:S(2)}) collective-permute-start(f32[64,384]{1,0:T(8,128)S(1)} %get-tuple-element.17), channel_id=1, source_target_pairs={{0,16},{16,0},{1,17},{17,1},{2,18},{18,2},{3,19},{19,3},{4,20},{20... | collective-permute-start | bytes 294920 | tf_op jit(solution)/shard_map/ppermute | solution.py:223

commit v7 on v6

--- a/solution.py
+++ b/solution.py
@@ -152,6 +152,12 @@
     return dot(jnp.concatenate([xh, xl, xh], axis=1), jnp.concatenate([yh, yh, yl], axis=0))
 
 
+def square3(x):
+    high, low = x
+    mixed = dot(high, low)
+    return dot(high, high) + (mixed + mixed.T)
+
+
 def newton_schulz_kernel(owner_ref, gram_ref, x_ref, out_ref):
     blocks = {}
     for at, (i, j) in enumerate(BLOCKS):
@@ -177,7 +183,7 @@
     current = x_ref[...].astype(F32) * inv_norm
     for sweep in range(ITERS):
         parts = split(weights)
-        poly = COEF_A * eye + COEF_B * weights + COEF_C * dot3(parts, parts)
+        poly = COEF_A * eye + COEF_B * weights + COEF_C * square3(parts)
         poly_parts = split(poly)
         current = dot3(split(current), poly_parts)
         if sweep < ITERS - 1:

time: 158 us -> 158 us (level)
  no operation moved by 1% of the time
where the time goes in v7:
time: 158 us; the launch traced here: 157 us
  starting transfers between devices  56.3 us (36%)
  waiting for transfers between devices  48.1 us (30%)
  blocking collectives  30.3 us (19%)
  Pallas kernels  15.7 us (10%)
  local copies, waits for them, and re-layouts  4.93 us (3%)
    all_to_all x1, blocking collectives, body(): far_parts = lax.all_to_all(near_sum, 'far', 0, 0)  17.3 us
    pallas_call x10, Pallas kernels, call(): pl.pallas_call(kernel, out_shape=outs, in_specs=[SMEM] * scalars + [VMEM]...  15.7 us
    all_to_all x1, waiting for transfers between devices, body(): lax.all_to_all(near, 'far', 0, 0)  15.7 us
    ppermute x4, starting transfers between devices, go(): return lax.ppermute(value, ('far', 'near'), ring(FAR * NEAR, step))  15.2 us
    ppermute x3, starting transfers between devices, swap(): return lax.ppermute(value, 'core', ring(CORES, 1))  15 us
    all_to_all x1, blocking collectives, body(): near_parts = lax.all_to_all(packed, 'near', 0, 0)  13.1 us
    all_to_all x1, starting transfers between devices, body(): lax.all_to_all(sent.reshape(CORES * n_y, ROWS, FF), ('core', 'y'), 0, 0)  9.98 us
    ppermute x4, waiting for transfers between devices, go(): return lax.ppermute(value, ('far', 'near'), ring(FAR * NEAR, step))  9.13 us
  transfers between devices with their start and end apart: 11, of which 9 were waited for; matrix products, arithmetic and copies ran while one was open for 2% of the time, Pallas kernels for 1%

profile of v7, /device:TPU:1, one launch (start us, length us, event | category | flops | bytes accessed | tf_op | source)
XLA Modules:
  0.0 156.9 jit_solution(15333754879769343178)
XLA Ops:
  0.6 1.6 %copy-done = bf16[512,1,2048]{2,0,1:T(8,128)(2,1)S(1)} copy-done((bf16[512,1,2048]{2,0,1:T(8,128)(2,1)S(1)}, bf16[512,1,2048]{2,0,1:T(8,128)(2,1)}, u32[]{:S(2)}) %copy-start) | copy-done | bytes 2097176
  2.2 1.0 copy-done.1
  3.9 1.9 %shard_map.69 = bf16[4,4,128,384]{3,2,1,0:T(8,128)(2,1)S(1)} custom-call(s32[2]{0:T(128)S(1)} %bitcast.26, bf16[512,2048]{1,0:T(8,128)(2,1)S(1)} %bitcast.19, bf16[512,384]{1,0:T(8,128)(2,1)S(1)} %bitcast.21), custom_call_target="tpu_custom_call" | custom-call | flops 805306368 | bytes 2490376 | tf_op jit(solution)/shard_map/pallas_call | solution.py:44
  5.8 8.8 %collective-permute-start = (bf16[4,4,128,384]{3,2,1,0:T(8,128)(2,1)S(1)}, bf16[4,4,128,384]{3,2,1,0:T(8,128)(2,1)S(1)}, u32[]{:S(2)}, u32[]{:S(2)}) collective-permute-start(bf16[4,4,128,384]{3,2,1,0:T(8,128)(2,1)S(1)} %shard_map.69), channel_id=1, source_target_pairs={{0,16},{16,0},{1,17},{17,1},{2,18},{18,2},{3,19},{19,3},{4,20},{20... | collective-permute-start | bytes 4718600 | tf_op jit(solution)/shard_map/ppermute | solution.py:229
  14.6 1.9 %shard_map.68.mine_ref = bf16[4,4,128,384]{3,2,1,0:T(8,128)(2,1)S(1)} custom-call(s32[2]{0:T(128)S(1)} %bitcast.27, bf16[512,2048]{1,0:T(8,128)(2,1)S(1)} %bitcast.20, bf16[512,384]{1,0:T(8,128)(2,1)S(1)} %bitcast.22), custom_call_target="tpu_custom_call" | custom-call | flops 805306368 | bytes 2490376 | tf_op jit(solution)/shard_map/pallas_call | solution.py:44
  16.5 1.1 collective-permute-done.other_ref
  18.0 2.1 %collective-permute-start.3 = (bf16[4,128,384]{2,1,0:T(8,128)(2,1)S(1)}, bf16[4,128,384]{2,1,0:T(8,128)(2,1)S(1)}, u32[]{:S(2)}, u32[]{:S(2)}) collective-permute-start(bf16[4,128,384]{2,1,0:T(8,128)(2,1)S(1)} %get-tuple-element.14), channel_id=1, source_target_pairs={{0,32},{32,64},{64,96},{96,128},{128,160},{160,192},{192,224},{224... | collective-permute-start | bytes 1179656 | tf_op jit(solution)/shard_map/ppermute | solution.py:226
  20.1 5.7 %collective-permute-start.4 = (bf16[4,128,384]{2,1,0:T(8,128)(2,1)S(1)}, bf16[4,128,384]{2,1,0:T(8,128)(2,1)S(1)}, u32[]{:S(2)}, u32[]{:S(2)}) collective-permute-start(bf16[4,128,384]{2,1,0:T(8,128)(2,1)S(1)} %get-tuple-element.15), channel_id=1, source_target_pairs={{0,480},{32,0},{64,32},{96,64},{128,96},{160,128},{192,160},{224,1... | collective-permute-start | bytes 1179656 | tf_op jit(solution)/shard_map/ppermute | solution.py:226
  25.8 1.9 %collective-permute-start.1 = (bf16[2,128,384]{2,1,0:T(8,128)(2,1)S(1)}, bf16[2,128,384]{2,1,0:T(8,128)(2,1)S(1)}, u32[]{:S(2)}, u32[]{:S(2)}) collective-permute-start(bf16[2,128,384]{2,1,0:T(8,128)(2,1)S(1)} %get-tuple-element.12), channel_id=1, source_target_pairs={{0,64},{32,96},{64,128},{96,160},{128,192},{160,224},{192,256},{22... | collective-permute-start | bytes 589832 | tf_op jit(solution)/shard_map/ppermute | solution.py:226
  27.7 5.5 %collective-permute-start.2 = (bf16[2,128,384]{2,1,0:T(8,128)(2,1)S(1)}, bf16[2,128,384]{2,1,0:T(8,128)(2,1)S(1)}, u32[]{:S(2)}, u32[]{:S(2)}) collective-permute-start(bf16[2,128,384]{2,1,0:T(8,128)(2,1)S(1)} %get-tuple-element.13), channel_id=1, source_target_pairs={{0,448},{32,480},{64,0},{96,32},{128,64},{160,96},{192,128},{224,1... | collective-permute-start | bytes 589832 | tf_op jit(solution)/shard_map/ppermute | solution.py:226
  33.2 6.5 %collective-permute-done.1.c_ref = bf16[2,128,384]{2,1,0:T(8,128)(2,1)S(1)} collective-permute-done((bf16[2,128,384]{2,1,0:T(8,128)(2,1)S(1)}, bf16[2,128,384]{2,1,0:T(8,128)(2,1)S(1)}, u32[]{:S(2)}, u32[]{:S(2)}) %collective-permute-start.1) | collective-permute-done | bytes 196640 | tf_op jit(solution)/shard_map/ppermute | solution.py:226
  39.7 2.6 %collective-permute-done.2.d_ref = bf16[2,128,384]{2,1,0:T(8,128)(2,1)S(1)} collective-permute-done((bf16[2,128,384]{2,1,0:T(8,128)(2,1)S(1)}, bf16[2,128,384]{2,1,0:T(8,128)(2,1)S(1)}, u32[]{:S(2)}, u32[]{:S(2)}) %collective-permute-start.2) | collective-permute-done | bytes 196640 | tf_op jit(solution)/shard_map/ppermute | solution.py:226
  42.3 1.0 shard_map.71
  43.3 8.7 %all-to-all-start = ((bf16[4,128,384]{2,1,0:T(8,128)(2,1)}), bf16[4,128,384]{2,1,0:T(8,128)(2,1)S(1)}, u32[]{:S(2)}, u32[]{:S(2)}) async-start(bf16[4,128,384]{2,1,0:T(8,128)(2,1)} %shard_map.71), calls=%async_computation | async-start | bytes 786432 | tf_op jit(solution)/shard_map/all_to_all | solution.py:256
  52.1 3.7 %collective-permute-start.5 = (f32[64,384]{1,0:T(8,128)S(1)}, f32[64,384]{1,0:T(8,128)S(1)}, u32[]{:S(2)}, u32[]{:S(2)}) collective-permute-start(f32[64,384]{1,0:T(8,128)S(1)} %bitcast.28), channel_id=1, source_target_pairs={{0,16},{16,0},{1,17},{17,1},{2,18},{18,2},{3,19},{19,3},{4,20},{20... | collective-permute-start | bytes 294920 | tf_op jit(solution)/shard_map/ppermute | solution.py:229
  55.9 0.9 collective-permute-done.5.lent_ref
  56.8 15.7 %all-to-all-done.parts_ref = bf16[4,128,384]{2,1,0:T(8,128)(2,1)S(1)} async-done(((bf16[4,128,384]{2,1,0:T(8,128)(2,1)}), bf16[4,128,384]{2,1,0:T(8,128)(2,1)S(1)}, u32[]{:S(2)}, u32[]{:S(2)}) %all-to-all-start) | async-done | bytes 393248 | tf_op jit(solution)/shard_map/all_to_all | solution.py:256
  72.8 13.1 %all_to_all.30.parts_ref = bf16[4,176,128]{2,1,0:T(8,128)(2,1)S(1)} all-to-all(bf16[4,176,128]{2,1,0:T(8,128)(2,1)S(1)} %bitcast.25), channel_id=1, replica_groups=mesh['far'=4,'near'=4,'core'=2,'x'=4,'y'=4] {'near'}, dimensions={0} | all-to-all | bytes 360448 | tf_op jit(solution)/shard_map/all_to_all | solution.py:261
  85.9 17.3 %all_to_all.31.parts_ref = bf16[4,176,128]{2,1,0:T(8,128)(2,1)S(1)} all-to-all(bf16[4,176,128]{2,1,0:T(8,128)(2,1)S(1)} %shard_map.73), channel_id=1, replica_groups=mesh['far'=4,'near'=4,'core'=2,'x'=4,'y'=4] {'far'}, dimensions={0} | all-to-all | bytes 360448 | tf_op jit(solution)/shard_map/all_to_all | solution.py:263
  103.2 0.8 shard_map.74
  104.0 3.5 %all-to-all-start.3 = ((f32[4,176,128]{2,1,0:T(8,128)}), f32[4,176,128]{2,1,0:T(8,128)S(1)}, u32[]{:S(2)}, u32[]{:S(2)}) async-start(f32[4,176,128]{2,1,0:T(8,128)} %shard_map.74), calls=%async_computation.3 | async-start | bytes 720896 | tf_op jit(solution)/shard_map/all_to_all | solution.py:265
  108.3 5.5 %all-to-all-done.3 = f32[4,176,128]{2,1,0:T(8,128)S(1)} async-done(((f32[4,176,128]{2,1,0:T(8,128)}), f32[4,176,128]{2,1,0:T(8,128)S(1)}, u32[]{:S(2)}, u32[]{:S(2)}) %all-to-all-start.3) | async-done | bytes 360480 | tf_op jit(solution)/shard_map/all_to_all | solution.py:265
  113.8 6.4 %shard_map.75 = bf16[2,4,64,384]{3,2,1,0:T(8,128)(2,1)} custom-call(s32[1]{0:T(128)} %bitcast.8.owner_ref, f32[704,128]{1,0:T(8,128)S(1)} %bitcast.24, bf16[128,384]{1,0:T(8,128)(2,1)S(1)} %get-tuple-element.19.x_ref), custom_call_target="tpu_custom_call" | custom-call | flops 3057647616 | bytes 458756 | tf_op jit(solution)/shard_map/pallas_call | solution.py:44
  120.2 10.0 %all-to-all-start.4 = ((bf16[8,64,384]{2,1,0:T(8,128)(2,1)}), bf16[8,64,384]{2,1,0:T(8,128)(2,1)S(1)}, u32[]{:S(2)}, u32[]{:S(2)}) async-start(bf16[8,64,384]{2,1,0:T(8,128)(2,1)} %bitcast.11), calls=%async_computation.4 | async-start | bytes 786432 | tf_op jit(solution)/shard_map/all_to_all | solution.py:294
  130.4 7.7 %all-to-all-done.4.got_ref = bf16[8,64,384]{2,1,0:T(8,128)(2,1)S(1)} async-done(((bf16[8,64,384]{2,1,0:T(8,128)(2,1)}), bf16[8,64,384]{2,1,0:T(8,128)(2,1)S(1)}, u32[]{:S(2)}, u32[]{:S(2)}) %all-to-all-start.4) | async-done | bytes 393248 | tf_op jit(solution)/shard_map/all_to_all | solution.py:294
  138.1 1.6 %shard_map.76 = bf16[4,4,64,384]{3,2,1,0:T(8,128)(2,1)} custom-call(s32[16]{0:T(128)S(1)} %select_reduce_fusion.source_ref, bf16[8,64,384]{2,1,0:T(8,128)(2,1)S(1)} %all-to-all-done.4.got_ref), custom_call_target="tpu_custom_call" | custom-call | bytes 393280 | tf_op jit(solution)/shard_map/pallas_call | solution.py:44
  139.8 4.0 %all-to-all-start.5 = ((bf16[4,4,64,384]{3,2,1,0:T(8,128)(2,1)}), bf16[4,4,64,384]{3,2,1,0:T(8,128)(2,1)S(1)}, u32[]{:S(2)}, u32[]{:S(2)}) async-start(bf16[4,4,64,384]{3,2,1,0:T(8,128)(2,1)} %shard_map.76), calls=%async_computation.5 | async-start | bytes 1572864 | tf_op jit(solution)/shard_map/all_to_all | solution.py:296
  143.8 2.5 %collective-permute-start.6 = (f32[64,384]{1,0:T(8,128)S(1)}, f32[64,384]{1,0:T(8,128)S(1)}, u32[]{:S(2)}, u32[]{:S(2)}) collective-permute-start(f32[64,384]{1,0:T(8,128)S(1)} %get-tuple-element.17), channel_id=1, source_target_pairs={{0,16},{16,0},{1,17},{17,1},{2,18},{18,2},{3,19},{19,3},{4,20},{20... | collective-permute-start | bytes 294920 | tf_op jit(solution)/shard_map/ppermute | solution.py:229
  146.5 0.7 collective-permute-done.6
  147.3 0.8 copy.13
  148.1 7.4 %all-to-all-done.5.got_ref = bf16[4,4,64,384]{3,2,1,0:T(8,128)(2,1)S(1)} async-done(((bf16[4,4,64,384]{3,2,1,0:T(8,128)(2,1)}), bf16[4,4,64,384]{3,2,1,0:T(8,128)(2,1)S(1)}, u32[]{:S(2)}, u32[]{:S(2)}) %all-to-all-start.5) | async-done | bytes 786464 | tf_op jit(solution)/shard_map/all_to_all | solution.py:296
  155.5 1.4 shard_map.77
  (29 shorter events, 3.0 us)
Async XLA Ops:
  0.6 1.6 %copy-start = (bf16[512,1,2048]{2,0,1:T(8,128)(2,1)S(1)}, bf16[512,1,2048]{2,0,1:T(8,128)(2,1)}, u32[]{:S(2)}) copy-start(bf16[512,1,2048]{2,0,1:T(8,128)(2,1)} %param.5) | copy-start | bytes 6291460
  2.2 1.0 copy-start.1
  3.2 0.7 copy-start.2
  5.8 11.8 %collective-permute-start = (bf16[4,4,128,384]{3,2,1,0:T(8,128)(2,1)S(1)}, bf16[4,4,128,384]{3,2,1,0:T(8,128)(2,1)S(1)}, u32[]{:S(2)}, u32[]{:S(2)}) collective-permute-start(bf16[4,4,128,384]{3,2,1,0:T(8,128)(2,1)S(1)} %shard_map.69), channel_id=1, source_target_pairs={{0,16},{16,0},{1,17},{17,1},{2,18},{18,2},{3,19},{19,3},{4,20},{20... | collective-permute-start | bytes 4718600 | tf_op jit(solution)/shard_map/ppermute | solution.py:229
  18.0 34.0 %copy-start.3 = (f32[64,2,384]{2,1,0:T(2,128)S(1)}, f32[64,2,384]{2,1,0:T(2,128)}, u32[]{:S(2)}) copy-start(f32[64,2,384]{2,1,0:T(2,128)} %param.8) | copy-start | bytes 589828
  18.0 24.3 %collective-permute-start.3 = (bf16[4,128,384]{2,1,0:T(8,128)(2,1)S(1)}, bf16[4,128,384]{2,1,0:T(8,128)(2,1)S(1)}, u32[]{:S(2)}, u32[]{:S(2)}) collective-permute-start(bf16[4,128,384]{2,1,0:T(8,128)(2,1)S(1)} %get-tuple-element.14), channel_id=1, source_target_pairs={{0,32},{32,64},{64,96},{96,128},{128,160},{160,192},{192,224},{224... | collective-permute-start | bytes 1179656 | tf_op jit(solution)/shard_map/ppermute | solution.py:226
  20.1 22.3 %collective-permute-start.4 = (bf16[4,128,384]{2,1,0:T(8,128)(2,1)S(1)}, bf16[4,128,384]{2,1,0:T(8,128)(2,1)S(1)}, u32[]{:S(2)}, u32[]{:S(2)}) collective-permute-start(bf16[4,128,384]{2,1,0:T(8,128)(2,1)S(1)} %get-tuple-element.15), channel_id=1, source_target_pairs={{0,480},{32,0},{64,32},{96,64},{128,96},{160,128},{192,160},{224,1... | collective-permute-start | bytes 1179656 | tf_op jit(solution)/shard_map/ppermute | solution.py:226
  25.8 13.9 %collective-permute-start.1 = (bf16[2,128,384]{2,1,0:T(8,128)(2,1)S(1)}, bf16[2,128,384]{2,1,0:T(8,128)(2,1)S(1)}, u32[]{:S(2)}, u32[]{:S(2)}) collective-permute-start(bf16[2,128,384]{2,1,0:T(8,128)(2,1)S(1)} %get-tuple-element.12), channel_id=1, source_target_pairs={{0,64},{32,96},{64,128},{96,160},{128,192},{160,224},{192,256},{22... | collective-permute-start | bytes 589832 | tf_op jit(solution)/shard_map/ppermute | solution.py:226
  27.7 14.6 %collective-permute-start.2 = (bf16[2,128,384]{2,1,0:T(8,128)(2,1)S(1)}, bf16[2,128,384]{2,1,0:T(8,128)(2,1)S(1)}, u32[]{:S(2)}, u32[]{:S(2)}) collective-permute-start(bf16[2,128,384]{2,1,0:T(8,128)(2,1)S(1)} %get-tuple-element.13), channel_id=1, source_target_pairs={{0,448},{32,480},{64,0},{96,32},{128,64},{160,96},{192,128},{224,1... | collective-permute-start | bytes 589832 | tf_op jit(solution)/shard_map/ppermute | solution.py:226
  43.3 29.2 %all-to-all-start = ((bf16[4,128,384]{2,1,0:T(8,128)(2,1)}), bf16[4,128,384]{2,1,0:T(8,128)(2,1)S(1)}, u32[]{:S(2)}, u32[]{:S(2)}) async-start(bf16[4,128,384]{2,1,0:T(8,128)(2,1)} %shard_map.71), calls=%async_computation | async-start | bytes 786432 | tf_op jit(solution)/shard_map/all_to_all | solution.py:256
  52.1 4.6 %collective-permute-start.5 = (f32[64,384]{1,0:T(8,128)S(1)}, f32[64,384]{1,0:T(8,128)S(1)}, u32[]{:S(2)}, u32[]{:S(2)}) collective-permute-start(f32[64,384]{1,0:T(8,128)S(1)} %bitcast.28), channel_id=1, source_target_pairs={{0,16},{16,0},{1,17},{17,1},{2,18},{18,2},{3,19},{19,3},{4,20},{20... | collective-permute-start | bytes 294920 | tf_op jit(solution)/shard_map/ppermute | solution.py:229
  55.9 51.6 %copy-start.4 = (s32[32,1]{0,1:T(1,128)S(1)}, s32[32,1]{0,1:T(1,128)}, u32[]{:S(2)}) copy-start(s32[32,1]{0,1:T(1,128)} %param.9) | copy-start | bytes 388
  104.0 9.9 %all-to-all-start.3 = ((f32[4,176,128]{2,1,0:T(8,128)}), f32[4,176,128]{2,1,0:T(8,128)S(1)}, u32[]{:S(2)}, u32[]{:S(2)}) async-start(f32[4,176,128]{2,1,0:T(8,128)} %shard_map.74), calls=%async_computation.3 | async-start | bytes 720896 | tf_op jit(solution)/shard_map/all_to_all | solution.py:265
  120.2 17.9 %all-to-all-start.4 = ((bf16[8,64,384]{2,1,0:T(8,128)(2,1)}), bf16[8,64,384]{2,1,0:T(8,128)(2,1)S(1)}, u32[]{:S(2)}, u32[]{:S(2)}) async-start(bf16[8,64,384]{2,1,0:T(8,128)(2,1)} %bitcast.11), calls=%async_computation.4 | async-start | bytes 786432 | tf_op jit(solution)/shard_map/all_to_all | solution.py:294
  139.8 15.7 %all-to-all-start.5 = ((bf16[4,4,64,384]{3,2,1,0:T(8,128)(2,1)}), bf16[4,4,64,384]{3,2,1,0:T(8,128)(2,1)S(1)}, u32[]{:S(2)}, u32[]{:S(2)}) async-start(bf16[4,4,64,384]{3,2,1,0:T(8,128)(2,1)} %shard_map.76), calls=%async_computation.5 | async-start | bytes 1572864 | tf_op jit(solution)/shard_map/all_to_all | solution.py:296
  143.8 3.5 %collective-permute-start.6 = (f32[64,384]{1,0:T(8,128)S(1)}, f32[64,384]{1,0:T(8,128)S(1)}, u32[]{:S(2)}, u32[]{:S(2)}) collective-permute-start(f32[64,384]{1,0:T(8,128)S(1)} %get-tuple-element.17), channel_id=1, source_target_pairs={{0,16},{16,0},{1,17},{17,1},{2,18},{18,2},{3,19},{19,3},{4,20},{20... | collective-permute-start | bytes 294920 | tf_op jit(solution)/shard_map/ppermute | solution.py:229
